TPU v7x, 128 devices: a whole 4x4x4 slice. The times are simulated.
128 devices in a mesh: dp: 8 (over z_lo, x), tensor: 16 (over z_hi, y, core).
Axes of the slice: x: 4, y: 4, z: 4 (z_hi: 2, z_lo: 2; z = z_hi * 2 + z_lo), core: 2. Of those that a mesh axis runs over, the one named last changes fastest.
Arguments:
- tokens: bfloat16 [4096, 14784], P('dp', 'tensor'), may hold values from -6 to 6
- base_weight: bfloat16 [14784, 4096], P('tensor'), may hold values from -0.046875 to 0.046875
- first_factor: bfloat16 [32, 462, 128], P('tensor'), may hold values from -0.25 to 0.25
- second_factor: bfloat16 [32, 128, 128], P('tensor'), may hold values from -0.5 to 0.5
- channel_order: int32 [4096], replicated, may hold values from 0 to 4095, each once
- cotangent: bfloat16 [4096, 4096], P(('dp', 'tensor')), may hold values from -6 to 6
Outputs:
- output: float32 [4096, 4096], P(('dp', 'tensor'))
- d_tokens: float32 [4096, 14784], P('dp', 'tensor')
- d_first: float32 [32, 462, 128], P('tensor')
- d_second: float32 [32, 128, 128], P('tensor')
Inputs may be any that keep to these rules, and one draw needn't show every extreme that they name: channel_order holds each of 0 to 4095 once.
All inputs are finite; a program needn't handle non-finite values.
Results may differ from a plain program's by a relative error of at most 0.0029.
Values may be sent and summed in bfloat16 or wider, within the bound.
No kernel may reach another device: no remote copies, remote signals or barrier semaphores. Data moves between devices by JAX's collectives and lax.ppermute only.
A program may use at most 128 MiB of HBM per device.

v0:
```python
import jax
import jax.numpy as jnp
from jax import lax
from jax.sharding import PartitionSpec as P


def per_device(tokens, base_weight, first_factor, second_factor, channel_order, cotangent):
    tok_rows = tokens.shape[0]
    local_blocks = first_factor.shape[0]
    block_in = first_factor.shape[1]
    block_out = first_factor.shape[2]
    tensor_count = lax.axis_size("tensor")
    tensor_place = lax.axis_index("tensor")
    share_rows = tok_rows // tensor_count
    local_channels = local_blocks * block_out
    model_width = base_weight.shape[1]
    all_blocks = model_width // block_out
    pieces = tokens.reshape(tok_rows, local_blocks, block_in)
    inner_act = jnp.einsum("tnb,nbo->tno", pieces, first_factor, preferred_element_type=jnp.float32)
    inner_act = inner_act.reshape(tok_rows, local_channels).astype(jnp.bfloat16)
    full_second = lax.all_gather(second_factor, "tensor", axis=0, tiled=True)
    whole_rows = lax.all_gather(inner_act, "tensor", axis=1, tiled=True)
    arrived = lax.dynamic_slice_in_dim(whole_rows, tensor_place * share_rows, share_rows, 0)
    mixed_blocks = jnp.take(arrived, channel_order, axis=1).reshape(
        share_rows, all_blocks, block_out
    )
    base_out = lax.psum_scatter(
        jnp.dot(tokens, base_weight, preferred_element_type=jnp.float32),
        "tensor",
        scatter_dimension=0,
        tiled=True,
    )
    delta_out = jnp.einsum(
        "tnb,nbo->tno", mixed_blocks, full_second, preferred_element_type=jnp.float32
    )
    output = base_out + delta_out.reshape(share_rows, model_width)
    grad_blocks = cotangent.reshape(share_rows, all_blocks, block_out)
    d_mixed = jnp.einsum(
        "tno,nbo->tnb", grad_blocks, full_second, preferred_element_type=jnp.float32
    )
    d_mixed = d_mixed.reshape(share_rows, model_width).astype(jnp.bfloat16)
    part_second = jnp.einsum(
        "tnb,tno->nbo", mixed_blocks, grad_blocks, preferred_element_type=jnp.float32
    )
    inverse = jnp.argsort(channel_order)
    wanted = lax.dynamic_slice_in_dim(inverse, tensor_place * local_channels, local_channels, 0)
    all_grads = lax.all_gather(d_mixed, "tensor", axis=0, tiled=True)
    d_inner = jnp.take(all_grads, wanted, axis=1)
    d_inner_blocks = d_inner.reshape(tok_rows, local_blocks, block_out)
    d_first_part = jnp.einsum(
        "tnb,tno->nbo", pieces, d_inner_blocks, preferred_element_type=jnp.float32
    )
    d_delta = jnp.einsum(
        "tno,nbo->tnb", d_inner_blocks, first_factor, preferred_element_type=jnp.float32
    )
    d_delta = d_delta.reshape(tok_rows, local_blocks * block_in)
    d_base = jnp.einsum(
        "td,fd->tf",
        lax.all_gather(cotangent, "tensor", axis=0, tiled=True),
        base_weight,
        preferred_element_type=jnp.float32,
    )
    d_tokens = d_base + d_delta
    summed_second = lax.psum(part_second, "dp")
    d_second = lax.psum_scatter(summed_second, "tensor", scatter_dimension=0, tiled=True)
    d_first = lax.psum(d_first_part, "dp")
    return (output, d_tokens, d_first, d_second)


def solution(mesh):
    return jax.shard_map(
        per_device,
        mesh=mesh,
        in_specs=(
            P("dp", "tensor"),
            P("tensor", None),
            P("tensor", None, None),
            P("tensor", None, None),
            P(),
            P(("dp", "tensor"), None),
        ),
        out_specs=(
            P(("dp", "tensor"), None),
            P("dp", "tensor"),
            P("tensor", None, None),
            P("tensor", None, None),
        ),
        check_vma=False,
    )
```

profile of v0, /device:TPU:2, one launch (start us, length us, event | category | flops | bytes accessed | tf_op | source)
XLA Modules:
  0.0 498.1 jit_solution(8697121184378325510)
XLA Ops:
  7.2 0.7 all-gather.7.cloned.1.call-update
  8.0 1.4 reshape.48
  9.3 2.0 convolution_convert_fusion.1
  11.4 46.6 %all-gather.7.cloned.1.call-done = bf16[32,128,128]{2,1,0:T(8,128)(2,1)} async-done(((bf16[2,128,128]{2,1,0:T(8,128)(2,1)}), bf16[32,128,128]{2,1,0:T(8,128)(2,1)}) %all-gather.7.cloned.1.call-update) | async-done | bytes 1048592 | tf_op jit(solution)/shard_map/all_gather | solution.py:21
  58.0 1.9 fusion
  59.9 0.8 copy.55
  60.8 54.9 %all-gather.5.cloned.1.call-done = bf16[512,4096]{0,1:T(8,128)(2,1)} async-done(((bf16[512,256]{0,1:T(8,128)(2,1)}), bf16[512,4096]{0,1:T(8,128)(2,1)}) %all-gather.5.cloned.1.call-update) | async-done | bytes 4194320 | tf_op jit(solution)/shard_map/all_gather | solution.py:22
  115.7 1.6 constant_dynamic-slice_fusion
  117.3 15.0 %gather_fusion = bf16[4096,32]{1,0:T(8,128)(2,1)} fusion(bf16[32,4096]{0,1:T(8,128)(2,1)S(1)} %constant_dynamic-slice_fusion, s32[4096]{0:T(1024)S(1)} %fusion.12), kind=kCustom, calls=%fused_computation | custom fusion | bytes 540672 | tf_op jit(solution)/shard_map/jit(_take)/gather | solution.py:24
  132.4 1.6 copy.29
  133.9 1.8 fusion.1
  135.8 0.5 all-gather.9.cloned.1.call-update
  136.4 5.8 %sort.17 = (s32[4096]{0:T(1024)}, s32[4096]{0:T(1024)S(1)}) sort(s32[4096]{0:T(1024)S(1)} %copy-done.4, s32[4096]{0:T(1024)S(1)} %iota.4), dimensions={0}, to_apply=%region_1.2 | sort | flops 49152 | bytes 65536 | tf_op jit(solution)/shard_map/jit(argsort)/sort | solution.py:45
  142.3 31.2 %all-gather.11.cloned.1.call-done = bf16[512,4096]{1,0:T(8,128)(2,1)} async-done(((bf16[32,4096]{1,0:T(8,128)(2,1)}), bf16[512,4096]{1,0:T(8,128)(2,1)}) %all-gather.11.cloned.1.call-update) | async-done | bytes 4194320 | tf_op jit(solution)/shard_map/all_gather | solution.py:47
  173.5 6.5 %copy.33 = bf16[512,4096]{0,1:T(8,128)(2,1)} copy(bf16[512,4096]{1,0:T(8,128)(2,1)} %all-gather.11.cloned.1.call-done) | data formatting | bytes 8388608 | tf_op jit(solution)/shard_map/all_gather | solution.py:47
  180.0 4.0 gather_fusion.1
  184.1 0.2 copy.34
  184.2 1.2 convolution_bitcast_fusion.2
  185.4 61.4 %reduce-scatter.5.cloned.1.call-done = f32[2,128,128]{2,1,0:T(8,128)} async-done(((f32[32,128,128]{2,1,0:T(8,128)}), f32[2,128,128]{2,1,0:T(8,128)}) %reduce-scatter.5.cloned.1.call-update) | async-done | bytes 131088 | tf_op jit(solution)/shard_map/reduce_scatter | solution.py:65
  246.9 0.2 reduce-scatter.3.cloned.1.call-start
  247.1 9.9 %fusion.17 = f32[512,4096]{1,0:T(8,128)} fusion(bf16[512,924]{0,1:T(8,128)(2,1)S(1)} %copy-done, bf16[924,4096]{1,0:T(8,128)(2,1)} %param.7), kind=kOutput, calls=%fused_computation.35 | convolution fusion | flops 3875536896 | bytes 16904192 | tf_op jit(solution)/shard_map/dot_general | solution.py:28
  257.1 1.2 copy-done.1
  258.3 0.4 convolution_bitcast_fusion.1
  258.7 0.4 convolution_bitcast_fusion
  259.1 1.4 reshape.51
  260.5 43.8 %all-gather.9.cloned.1.call-done = bf16[512,4096]{1,0:T(8,128)(2,1)} async-done(((bf16[32,4096]{1,0:T(8,128)(2,1)}), bf16[512,4096]{1,0:T(8,128)(2,1)}) %all-gather.9.cloned.1.call-update) | async-done | bytes 4194320 | tf_op jit(solution)/shard_map/all_gather | solution.py:59
  304.3 10.2 %convolution_add_fusion = f32[512,924]{0,1:T(8,128)} fusion(f32[512,924]{0,1:T(8,128)} %reshape.51, bf16[512,4096]{1,0:T(8,128)(2,1)} %all-gather.9.cloned.1.call-done, bf16[924,4096]{1,0:T(8,128)(2,1)} %param.7), kind=kOutput, calls=%fused_computation.3 | convolution fusion | flops 3876009984 | bytes 15548416 | tf_op jit(solution)/shard_map/td,fd->tf/dot_general | solution.py:57
  314.5 65.1 %all-reduce.3.cloned.1.call-done = (f32[2,462,128]{2,1,0:T(8,128)}, f32[2,128,128]{2,1,0:T(8,128)}) async-done(((f32[2,462,128]{2,1,0:T(8,128)}, f32[2,128,128]{2,1,0:T(8,128)}), (f32[2,462,128]{2,1,0:T(8,128)}, f32[2,128,128]{2,1,0:T(8,128)})) %all-reduce.3.cloned.1.call-update) | async-done | bytes 604176 | tf_op jit(solution)/shard_map/psum | solution.py:66
  379.6 2.0 copy.37
  381.7 106.1 %reduce-scatter.3.cloned.1.call-done = f32[32,4096]{1,0:T(8,128)} async-done(((f32[512,4096]{1,0:T(8,128)}), f32[32,4096]{1,0:T(8,128)}) %reduce-scatter.3.cloned.1.call-update) | async-done | bytes 524304 | tf_op jit(solution)/shard_map/reduce_scatter | solution.py:27
  487.8 1.9 bitcast_add_fusion
  489.7 1.6 copy.58
  (25 shorter events, 0.4 us)
Async XLA Ops:
  7.2 53.6 %copy-start.4 = (s32[4096]{0:T(1024)S(1)}, s32[4096]{0:T(1024)}, u32[]{:S(2)}) copy-start(s32[4096]{0:T(1024)} %param.10) | copy-start | bytes 49156
  7.2 50.8 %all-gather.7.cloned.1.call-start = ((), (), s32[]{:S(2)}) async-start(), calls=%async_computation.4 | async-start | bytes 1114112 | tf_op jit(solution)/shard_map/all_gather | solution.py:21
  7.9 107.8 %all-gather.5.cloned.1.call-start = ((), (), s32[]{:S(2)}) async-start(), calls=%async_computation.3 | async-start | bytes 4456448 | tf_op jit(solution)/shard_map/all_gather | solution.py:22
  11.3 122.6 %copy-start.2 = (bf16[32,4096]{1,0:T(8,128)(2,1)S(1)}, bf16[32,4096]{1,0:T(8,128)(2,1)}, u32[]{:S(2)}) copy-start(bf16[32,4096]{1,0:T(8,128)(2,1)} %param.11) | copy-start | bytes 786436
  11.4 162.2 %all-gather.11.cloned.1.call-start = ((), (), s32[]{:S(2)}) async-start(), calls=%async_computation.6 | async-start | bytes 4456448 | tf_op jit(solution)/shard_map/all_gather | solution.py:47
  60.7 186.1 %reduce-scatter.5.cloned.1.call-start = ((), (), s32[]{:S(2)}) async-start(), calls=%async_computation.7 | async-start | bytes 2228224 | tf_op jit(solution)/shard_map/reduce_scatter | solution.py:65
  135.8 168.5 %all-gather.9.cloned.1.call-start = ((), (), s32[]{:S(2)}) async-start(), calls=%async_computation.5 | async-start | bytes 4456448 | tf_op jit(solution)/shard_map/all_gather | solution.py:59
  136.4 243.2 %all-reduce.3.cloned.1.call-start = ((), (), s32[]{:S(2)}) async-start(), calls=%async_computation.8 | async-start | bytes 1212416 | tf_op jit(solution)/shard_map/psum | solution.py:66
  180.0 67.1 %copy-start = (bf16[512,924]{0,1:T(8,128)(2,1)S(1)}, bf16[512,924]{0,1:T(8,128)(2,1)}, u32[]{:S(2)}) copy-start(bf16[512,924]{0,1:T(8,128)(2,1)} %param.6) | copy-start | bytes 2838532
  246.9 240.9 %reduce-scatter.3.cloned.1.call-start = ((), (), s32[]{:S(2)}) async-start(), calls=%async_computation.2 | async-start | bytes 8912896 | tf_op jit(solution)/shard_map/reduce_scatter | solution.py:27
  257.0 1.3 copy-start.1
  257.0 1.6 copy-start.3
Sparse Core Ops, SparseCore 0:
  10.5 47.5 all-gather.6
  61.0 54.6 all-gather.4
  118.8 54.7 all-gather.10
  177.3 69.4 reduce-scatter.4
  249.1 55.1 all-gather.8
  307.3 72.2 all-reduce.2
  383.9 103.7 reduce-scatter.2
where the time goes:
time: 499 us; the launch traced here: 498 us
  waiting for transfers between devices  410 us (82%)
  local copies, waits for them, and re-layouts  37.3 us (7%)
  matrix products  27.9 us (6%)
  between operations  14.2 us (3%)
  other arithmetic  7.76 us (2%)
    reduce_scatter x1, waiting for transfers between devices, per_device(): lax.psum_scatter(jnp.dot(tokens, base_weight, preferred_element_type=jnp....  106 us
    psum x1, waiting for transfers between devices, per_device(): d_first = lax.psum(d_first_part, 'dp')  65.1 us
    reduce_scatter x1, waiting for transfers between devices, per_device(): lax.psum_scatter(summed_second, 'tensor', scatter_dimension=0, tiled=True)  61.4 us
    all_gather x1, waiting for transfers between devices, per_device(): whole_rows = lax.all_gather(inner_act, 'tensor', axis=1, tiled=True)  54.9 us
    all_gather x1, waiting for transfers between devices, per_device(): full_second = lax.all_gather(second_factor, 'tensor', axis=0, tiled=True)  46.6 us
    all_gather x1, waiting for transfers between devices, per_device(): lax.all_gather(cotangent, 'tensor', axis=0, tiled=True)  43.8 us
    all_gather x1, waiting for transfers between devices, per_device(): all_grads = lax.all_gather(d_mixed, 'tensor', axis=0, tiled=True)  31.2 us
    gather x2, local copies, waits for them, and re-layouts, per_device(): jnp.take(arrived, channel_order, axis=1)  16.6 us
  transfers between devices with their start and end apart: 7, of which 7 were waited for; matrix products, arithmetic and copies ran while one was open for 14% of the time, Pallas kernels for 0%

commit v1 on v0

v1 whole, which is shorter than its diff:
```python
import jax
import jax.numpy as jnp
from jax import lax
from jax.sharding import Mesh, PartitionSpec as P

F32 = jnp.float32
BF16 = jnp.bfloat16
DP = ("zl", "x")
CHIPS = ("zh", "y")
TENSOR = ("zh", "y", "c")
OTHER_CORE = [(0, 1), (1, 0)]


def spread(value, axes, count):
    whole = jnp.broadcast_to(value[None], (count,) + value.shape)
    return lax.all_to_all(whole, axes, 0, 0)


def pair_up(mine, other, core):
    first = jnp.where(core == 0, mine, other)
    second = jnp.where(core == 0, other, mine)
    return jnp.stack([first, second], axis=1)


def per_device(tokens, base_weight, first_factor, second_factor, channel_order, cotangent):
    rows, hidden = tokens.shape
    blocks, block_in, block_out = first_factor.shape
    width = base_weight.shape[1]
    channels = blocks * block_out
    core = lax.axis_index("c")
    place = lax.axis_index(TENSOR)
    group = lax.axis_index(DP)
    chips = lax.axis_size(CHIPS)
    groups = lax.axis_size(DP)
    share = rows // (2 * chips)

    second_mine = spread(second_factor.reshape(channels, block_out), CHIPS, chips)
    cot_mine = spread(cotangent, CHIPS, chips)
    second_other = lax.ppermute(second_mine, "c", OTHER_CORE)
    second_all = pair_up(second_mine, second_other, core).reshape(-1, block_out, block_out)
    own = place * channels + jnp.arange(channels, dtype=jnp.int32)
    hits = (own[:, None] == channel_order[None, :]).astype(BF16).reshape(channels, -1, block_out)
    routed = jnp.einsum("knb,nbo->kno", hits, second_all, preferred_element_type=F32)
    routed = routed.reshape(channels, width).astype(BF16)

    wide = jnp.zeros((hidden, channels), BF16)
    for n in range(blocks):
        wide = wide.at[n * block_in : (n + 1) * block_in, n * block_out : (n + 1) * block_out].set(
            first_factor[n]
        )
    inner = jnp.dot(tokens, wide, preferred_element_type=F32).astype(BF16)

    def part(which):
        tok = lax.dynamic_index_in_dim(tokens.reshape(chips, 2, share, hidden), which, 1, False)
        inn = lax.dynamic_index_in_dim(inner.reshape(chips, 2, share, channels), which, 1, False)
        out = jnp.dot(tok.reshape(-1, hidden), base_weight, preferred_element_type=F32)
        return out + jnp.dot(inn.reshape(-1, channels), routed, preferred_element_type=F32)

    got = lax.ppermute(part(1 - core).astype(BF16), "c", OTHER_CORE)
    pair_sum = part(core) + got.astype(F32)
    terms = lax.all_to_all(pair_sum.astype(BF16).reshape(chips, share, width), CHIPS, 0, 0)
    output = jnp.sum(terms.astype(F32), axis=0)

    cot_other = lax.ppermute(cot_mine, "c", OTHER_CORE)
    cot_all = pair_up(cot_mine, cot_other, core).reshape(rows, width)
    d_inner = lax.dot_general(cot_all, routed, (((1,), (1,)), ((), ())), preferred_element_type=F32)
    d_inner = d_inner.astype(BF16)
    d_base = lax.dot_general(base_weight, cot_all, (((1,), (1,)), ((), ())), preferred_element_type=F32)
    d_delta = lax.dot_general(wide, d_inner, (((1,), (1,)), ((), ())), preferred_element_type=F32)
    d_tokens = (d_base + d_delta).T
    full = lax.dot_general(tokens, d_inner, (((0,), (0,)), ((), ())), preferred_element_type=F32)
    row = jnp.arange(hidden, dtype=jnp.int32)[:, None] // block_in
    d_first = full[:, :block_out]
    for n in range(1, blocks):
        d_first = jnp.where(row == n, full[:, n * block_out : (n + 1) * block_out], d_first)
    grads = lax.dot_general(inner, cot_all, (((0,), (0,)), ((), ())), preferred_element_type=F32)
    in_block = jnp.max(hits, axis=2).astype(F32)
    d_rows = jnp.sum(grads.reshape(channels, -1, block_out) * in_block[:, :, None], axis=1)

    first_share = -(-hidden // groups)
    row_share = channels // groups
    d_first = jnp.pad(d_first, ((0, first_share * groups - hidden), (0, 0)))
    sent = jnp.concatenate(
        [
            d_first.reshape(groups, first_share, block_out),
            d_rows.reshape(groups, row_share, block_out),
        ],
        axis=1,
    )
    sums = jnp.sum(lax.all_to_all(sent.astype(BF16), DP, 0, 0).astype(F32), axis=0)
    sums = sums.astype(BF16)
    rows_all = spread(sums[first_share:], TENSOR, 2 * chips).reshape(-1, block_out)
    wanted = lax.dynamic_slice_in_dim(channel_order, place * channels, channels, 0)
    held = (
        jnp.arange(2 * chips, dtype=jnp.int32)[:, None] * channels
        + group * row_share
        + jnp.arange(row_share, dtype=jnp.int32)[None, :]
    ).reshape(-1)
    pick = (wanted[:, None] == held[None, :]).astype(BF16)
    picked = jnp.dot(pick, rows_all, preferred_element_type=F32).astype(BF16)
    final = spread(jnp.concatenate([sums[:first_share], picked]), DP, groups)
    d_first = final[:, :first_share].reshape(-1, block_out)[:hidden].astype(F32)
    d_second = jnp.sum(final[:, first_share:].astype(F32), axis=0)
    return (
        output,
        d_tokens,
        d_first.reshape(blocks, block_in, block_out),
        d_second.reshape(blocks, block_out, block_out),
    )


def solution(mesh):
    fine = Mesh(mesh.devices.reshape(2, 4, 2, 4, 2), ("zl", "x", "zh", "y", "c"))
    return jax.shard_map(
        per_device,
        mesh=fine,
        in_specs=(
            P(DP, TENSOR),
            P(TENSOR, None),
            P(TENSOR, None, None),
            P(TENSOR, None, None),
            P(),
            P(DP + TENSOR, None),
        ),
        out_specs=(
            P(DP + TENSOR, None),
            P(DP, TENSOR),
            P(TENSOR, None, None),
            P(TENSOR, None, None),
        ),
        check_vma=False,
    )
```

time: 499 us -> 167 us (0.33)
  waiting for transfers between devices: 410 us -> 62.1 us
  starting transfers between devices: 0.46 us -> 33.1 us
  local copies, waits for them, and re-layouts: 37.3 us -> 19.3 us
  between operations: 14.2 us -> 0.99 us
  matrix products: 27.9 us -> 40.8 us
    all_gather x4 -> x0, waiting for transfers between devices: 177 us -> none  [the longest x1 54.9 us: per_device(): whole_rows = lax.all_gather(inner_act, 'tensor', axis=1, tiled=True)]
    reduce_scatter x2 -> x0, waiting for transfers between devices: 168 us -> none  [the longest x1 106 us: per_device(): lax.psum_scatter(jnp.dot(tokens, base_weight, preferred_element_type=jnp....]
    psum x1 -> x0, waiting for transfers between devices: 65.1 us -> none  [per_device(): d_first = lax.psum(d_first_part, 'dp')]
    all_to_all x0 -> x6, waiting for transfers between devices: none -> 62.1 us  [the longest x4 35.6 us: spread(): return lax.all_to_all(whole, axes, 0, 0)]
    all_to_all x0 -> x6, starting transfers between devices: none -> 32.5 us  [the longest x4 23 us: spread(): return lax.all_to_all(whole, axes, 0, 0)]
    gather x4 -> x0, local copies, waits for them, and re-layouts: 20.8 us -> none  [the longest x2 16.6 us: per_device(): jnp.take(arrived, channel_order, axis=1)]
    dot_general x8 -> x12, matrix products: 27.9 us -> 40.8 us  [the longest x2 13 us: part(): jnp.dot(tok.reshape(-1, hidden), base_weight, preferred_element_type=F32)]
    dot_general x0 -> x1, local copies, waits for them, and re-layouts: none -> 6.52 us  [per_device(): lax.dot_general(inner, cot_all, (((0,), (0,)), ((), ())), preferred_eleme...]
  transfers between devices with their start and end apart: 7 -> 9, of which waited for: 7 -> 5; matrix products, arithmetic and copies ran while one was open for 14% -> 37% of each run, Pallas kernels for 0% -> 0%
where the time goes in v1:
time: 167 us; the launch traced here: 164 us
  waiting for transfers between devices  62.1 us (37%)
  matrix products  40.8 us (24%)
  starting transfers between devices  33.1 us (20%)
  local copies, waits for them, and re-layouts  19.3 us (12%)
  other arithmetic  8.16 us (5%)
    all_to_all x4, waiting for transfers between devices, spread(): return lax.all_to_all(whole, axes, 0, 0)  35.6 us
    all_to_all x1, waiting for transfers between devices, per_device(): lax.all_to_all(pair_sum.astype(BF16).reshape(chips, share, width), CHIPS,...  26.5 us
    all_to_all x4, starting transfers between devices, spread(): return lax.all_to_all(whole, axes, 0, 0)  23 us
    dot_general x2, matrix products, part(): jnp.dot(tok.reshape(-1, hidden), base_weight, preferred_element_type=F32)  13 us
    dot_general x1, matrix products, per_device(): lax.dot_general(base_weight, cot_all, (((1,), (1,)), ((), ())), preferred...  10.2 us
    dot_general x2, matrix products, part(): jnp.dot(inn.reshape(-1, channels), routed, preferred_element_type=F32)  7.01 us
    dot_general x1, local copies, waits for them, and re-layouts, per_device(): lax.dot_general(inner, cot_all, (((0,), (0,)), ((), ())), preferred_eleme...  6.52 us
    all_to_all x1, starting transfers between devices, per_device(): lax.all_to_all(sent.astype(BF16), DP, 0, 0).astype(F32)  5.28 us
  transfers between devices with their start and end apart: 9, of which 5 were waited for; matrix products, arithmetic and copies ran while one was open for 37% of the time, Pallas kernels for 0%

profile of v1, /device:TPU:2, one launch (start us, length us, event | category | flops | bytes accessed | tf_op | source)
XLA Modules:
  0.0 164.5 jit_solution(11894210131648219141)
XLA Ops:
  0.7 2.6 %broadcast_in_dim.20 = bf16[8,32,4096]{2,1,0:T(8,128)(2,1)} broadcast(bf16[32,4096]{1,0:T(8,128)(2,1)} %param.15), dimensions={1,2} | broadcast | bytes 2359296 | tf_op jit(solution)/shard_map/broadcast_in_dim | solution.py:15
  3.3 7.9 %all-to-all-start.2 = ((bf16[8,32,4096]{2,1,0:T(8,128)(2,1)}), bf16[8,32,4096]{2,1,0:T(8,128)(2,1)}, u32[]{:S(2)}, u32[]{:S(2)}) async-start(bf16[8,32,4096]{2,1,0:T(8,128)(2,1)} %broadcast_in_dim.20), calls=%async_computation.2 | async-start | bytes 4194304 | tf_op jit(solution)/shard_map/all_to_all | solution.py:16
  11.6 1.0 scatter.9
  13.1 26.6 %all-to-all-done.2 = bf16[8,32,4096]{2,1,0:T(8,128)(2,1)} async-done(((bf16[8,32,4096]{2,1,0:T(8,128)(2,1)}), bf16[8,32,4096]{2,1,0:T(8,128)(2,1)}, u32[]{:S(2)}, u32[]{:S(2)}) %all-to-all-start.2) | async-done | bytes 2097184 | tf_op jit(solution)/shard_map/all_to_all | solution.py:16
  39.7 0.9 broadcast_in_dim.19
  40.6 5.9 %all-to-all-start = ((bf16[8,256,128]{2,1,0:T(8,128)(2,1)}), bf16[8,256,128]{2,1,0:T(8,128)(2,1)S(1)}, u32[]{:S(2)}, u32[]{:S(2)}) async-start(bf16[8,256,128]{2,1,0:T(8,128)(2,1)} %broadcast_in_dim.19), calls=%async_computation | async-start | bytes 1048576 | tf_op jit(solution)/shard_map/all_to_all | solution.py:16
  46.4 0.8 fusion.3
  50.0 0.9 constant_dynamic-slice_fusion.1
  50.9 5.9 %all-to-all-done = bf16[8,256,128]{2,1,0:T(8,128)(2,1)S(1)} async-done(((bf16[8,256,128]{2,1,0:T(8,128)(2,1)}), bf16[8,256,128]{2,1,0:T(8,128)(2,1)S(1)}, u32[]{:S(2)}, u32[]{:S(2)}) %all-to-all-start) | async-done | bytes 524320 | tf_op jit(solution)/shard_map/all_to_all | solution.py:16
  56.8 5.5 %fusion.20 = f32[256,4096]{1,0:T(8,128)S(1)} fusion(bf16[256,924]{1,0:T(8,128)(2,1)S(1)} %bitcast.74, bf16[924,4096]{1,0:T(8,128)(2,1)} %param.11), kind=kOutput, calls=%fused_computation.53 | convolution fusion | flops 1937768448 | bytes 12236800 | tf_op jit(solution)/shard_map/dot_general | solution.py:56
  62.9 1.1 fusion.6
  64.0 2.1 %fusion.2 = bf16[256,4096]{1,0:T(8,128)(2,1)} fusion(f32[256,4096]{1,0:T(8,128)S(1)} %fusion.20, bf16[256,256]{1,0:T(8,128)(2,1)S(1)} %bitcast.72, bf16[256,4096]{0,1:T(8,128)(2,1)S(1)} %bitcast.61), kind=kOutput, calls=%fused_computation.5 | convolution fusion | flops 538968064 | bytes 8519680 | tf_op jit(solution)/shard_map/dot_general | solution.py:57
  66.6 2.5 %select_bitcast_fusion.1 = (bf16[8,1,32,4096]{3,2,0,1:T(8,128)(2,1)S(1)}, bf16[8,1,32,4096]{3,2,0,1:T(8,128)(2,1)S(1)}) fusion(bf16[8,32,4096]{2,1,0:T(8,128)(2,1)} %all-to-all-done.2, bf16[8,32,4096]{2,1,0:T(8,128)(2,1)} %collective-permute-done.2, pred[]{:T(512)S(6)} %eq.45), kind=kLoop, calls=%fused_computation.12 | loop fusion | flops 2097152 | bytes 8388609 | tf_op jit(solution)/shard_map/stack | solution.py:22
  69.5 2.2 %copy.18 = bf16[8,2,32,4096]{3,2,1,0:T(8,128)(2,1)} copy(bf16[8,2,32,4096]{3,2,0,1:T(8,128)(2,1)S(1)} %pad_maximum_fusion) | data formatting | bytes 8388608 | tf_op jit(solution)/shard_map/stack | solution.py:22
  71.7 6.5 %copy.19 = bf16[4096,512]{1,0:T(8,128)(2,1)} copy(bf16[4096,512]{0,1:T(8,128)(2,1)} %bitcast.64) | data formatting | bytes 8388608 | tf_op jit(solution)/shard_map/dot_general | solution.py:76
  78.2 3.4 %convolution_convert_fusion = bf16[512,256]{1,0:T(8,128)(2,1)S(1)} fusion(bf16[512,4096]{1,0:T(8,128)(2,1)} %bitcast.65, bf16[256,4096]{0,1:T(8,128)(2,1)S(1)} %bitcast.62), kind=kOutput, calls=%fused_computation.18 | convolution fusion | flops 1073872896 | bytes 6553600 | tf_op jit(solution)/shard_map/dot_general | solution.py:66
  82.5 3.2 %multiply_reduce_fusion = bf16[256,128]{1,0:T(8,128)(2,1)S(1)} fusion(bf16[32,128,512]{2,1,0:T(8,128)(2,1)} %bitcast.68, f32[256,32]{0,1:T(8,128)} %convert_element_type.67, bf16[256,512]{1,0:T(8,128)(2,1)} %copy-done.6), kind=kOutput, calls=%fused_computation.7 | convolution fusion | flops 1075806208 | bytes 4554752 | tf_op jit(solution)/shard_map/dot_general | solution.py:76
  85.7 0.8 pad_maximum_fusion.2
  86.4 5.3 %all-to-all-start.3 = ((bf16[8,148,128]{2,1,0:T(8,128)(2,1)}), bf16[8,148,128]{2,1,0:T(8,128)(2,1)S(1)}, u32[]{:S(2)}, u32[]{:S(2)}) async-start(bf16[8,148,128]{2,1,0:T(8,128)(2,1)} %pad_maximum_fusion.2), calls=%async_computation.3 | async-start | bytes 622592 | tf_op jit(solution)/shard_map/all_to_all | solution.py:90
  91.7 7.5 %fusion.19 = f32[256,4096]{1,0:T(8,128)} fusion(bf16[256,924]{1,0:T(8,128)(2,1)S(1)} %bitcast.73, bf16[924,4096]{1,0:T(8,128)(2,1)} %param.11), kind=kOutput, calls=%fused_computation.52 | convolution fusion | flops 1937768448 | bytes 12236800 | tf_op jit(solution)/shard_map/dot_general | solution.py:56
  100.0 3.5 %all-to-all-start.4 = ((bf16[16,32,128]{2,1,0:T(8,128)(2,1)}), bf16[16,32,128]{2,1,0:T(8,128)(2,1)S(1)}, u32[]{:S(2)}, u32[]{:S(2)}) async-start(bf16[16,32,128]{2,1,0:T(8,128)(2,1)} %broadcast_in_dim.22), calls=%async_computation.4 | async-start | bytes 262144 | tf_op jit(solution)/shard_map/all_to_all | solution.py:16
  103.5 4.9 %add_convert_fusion = bf16[256,4096]{1,0:T(8,128)(2,1)} fusion(bf16[256,4096]{1,0:T(8,128)(2,1)} %collective-permute-done.1, f32[256,4096]{1,0:T(8,128)} %fusion.19, bf16[256,256]{1,0:T(8,128)(2,1)} %bitcast.75, bf16[256,4096]{0,1:T(8,128)(2,1)S(1)} %bitcast.63), kind=kOutput, calls=%fused_computation.9 | convolution fusion | flops 541065216 | bytes 10616832 | tf_op jit(solution)/shard_map/dot_general | solution.py:57
  108.4 3.0 %all-to-all-done.4 = bf16[16,32,128]{2,1,0:T(8,128)(2,1)S(1)} async-done(((bf16[16,32,128]{2,1,0:T(8,128)(2,1)}), bf16[16,32,128]{2,1,0:T(8,128)(2,1)S(1)}, u32[]{:S(2)}, u32[]{:S(2)}) %all-to-all-start.4) | async-done | bytes 131104 | tf_op jit(solution)/shard_map/all_to_all | solution.py:16
  111.4 4.2 %all-to-all-start.1 = ((bf16[8,32,4096]{2,1,0:T(8,128)(2,1)}), bf16[8,32,4096]{2,1,0:T(8,128)(2,1)S(1)}, u32[]{:S(2)}, u32[]{:S(2)}) async-start(bf16[8,32,4096]{2,1,0:T(8,128)(2,1)} %bitcast.67), calls=%async_computation.1 | async-start | bytes 4194304 | tf_op jit(solution)/shard_map/all_to_all | solution.py:61
  115.9 1.7 %fusion.21 = f32[512,924]{0,1:T(8,128)} fusion(bf16[512,256]{1,0:T(8,128)(2,1)S(1)} %copy-done.2, bf16[924,256]{1,0:T(8,128)(2,1)S(1)} %scatter.9), kind=kOutput, calls=%fused_computation.54 | convolution fusion | flops 242221056 | bytes 2627584 | tf_op jit(solution)/shard_map/dot_general | solution.py:69
  117.9 26.5 %all-to-all-done.1 = bf16[8,32,4096]{2,1,0:T(8,128)(2,1)S(1)} async-done(((bf16[8,32,4096]{2,1,0:T(8,128)(2,1)}), bf16[8,32,4096]{2,1,0:T(8,128)(2,1)S(1)}, u32[]{:S(2)}, u32[]{:S(2)}) %all-to-all-start.1) | async-done | bytes 2097184 | tf_op jit(solution)/shard_map/all_to_all | solution.py:61
  144.4 1.0 broadcast_in_dim.23
  145.4 5.7 %all-to-all-start.5 = ((bf16[8,372,128]{2,1,0:T(8,128)(2,1)}), bf16[8,372,128]{2,1,0:T(8,128)(2,1)S(1)}, u32[]{:S(2)}, u32[]{:S(2)}) async-start(bf16[8,372,128]{2,1,0:T(8,128)(2,1)} %broadcast_in_dim.23), calls=%async_computation.5 | async-start | bytes 1540096 | tf_op jit(solution)/shard_map/all_to_all | solution.py:16
  151.1 10.2 %convolution_add_fusion.2 = f32[512,924]{0,1:T(8,128)} fusion(f32[512,924]{0,1:T(8,128)} %fusion.21, bf16[512,4096]{1,0:T(8,128)(2,1)} %bitcast.66, bf16[924,4096]{1,0:T(8,128)(2,1)} %param.11), kind=kOutput, calls=%fused_computation.16 | convolution fusion | flops 3876009984 | bytes 15548416 | tf_op jit(solution)/shard_map/dot_general | solution.py:68
  161.3 1.1 convert_reduce_fusion
  162.6 1.0 copy.20
  163.7 0.8 convert_reduce_fusion.1
  (63 shorter events, 7.3 us)
Async XLA Ops:
  0.6 10.5 %copy-start.3 = (bf16[2,462,128]{2,0,1:T(2,128)(2,1)S(1)}, bf16[2,462,128]{2,0,1:T(2,128)(2,1)}, u32[]{:S(2)}) copy-start(bf16[2,462,128]{2,0,1:T(2,128)(2,1)} %param.12) | copy-start | bytes 709636
  0.6 12.0 %copy-start = (bf16[512,924]{0,1:T(8,128)(2,1)S(1)}, bf16[512,924]{0,1:T(8,128)(2,1)}, u32[]{:S(2)}) copy-start(bf16[512,924]{0,1:T(8,128)(2,1)} %param.10) | copy-start | bytes 2838532
  3.3 36.5 %copy-start.8 = (bf16[2,128,128]{2,1,0:T(8,128)(2,1)S(1)}, bf16[2,128,128]{2,1,0:T(8,128)(2,1)}, u32[]{:S(2)}) copy-start(bf16[2,128,128]{2,1,0:T(8,128)(2,1)} %param.13) | copy-start | bytes 196612
  3.3 43.2 %copy-start.7 = (s32[4096]{0:T(1024)S(1)}, s32[4096]{0:T(1024)}, u32[]{:S(2)}) copy-start(s32[4096]{0:T(1024)} %param.14) | copy-start | bytes 49156
  3.3 36.5 %all-to-all-start.2 = ((bf16[8,32,4096]{2,1,0:T(8,128)(2,1)}), bf16[8,32,4096]{2,1,0:T(8,128)(2,1)}, u32[]{:S(2)}, u32[]{:S(2)}) async-start(bf16[8,32,4096]{2,1,0:T(8,128)(2,1)} %broadcast_in_dim.20), calls=%async_computation.2 | async-start | bytes 4194304 | tf_op jit(solution)/shard_map/all_to_all | solution.py:16
  12.6 35.9 %copy-start.9 = (s32[256]{0:T(256)}, s32[256]{0:T(256)S(1)}, u32[]{:S(2)}) copy-start(s32[256]{0:T(256)S(1)} %iota_add_fusion.1) | copy-start | bytes 3076
  13.1 36.9 %copy-start.6 = (bf16[256,512]{1,0:T(8,128)(2,1)}, bf16[256,512]{1,0:T(8,128)(2,1)S(1)}, u32[]{:S(2)}) copy-start(bf16[256,512]{1,0:T(8,128)(2,1)S(1)} %convolution_convert_fusion.1) | copy-start | bytes 786436
  40.6 16.2 %all-to-all-start = ((bf16[8,256,128]{2,1,0:T(8,128)(2,1)}), bf16[8,256,128]{2,1,0:T(8,128)(2,1)S(1)}, u32[]{:S(2)}, u32[]{:S(2)}) async-start(bf16[8,256,128]{2,1,0:T(8,128)(2,1)} %broadcast_in_dim.19), calls=%async_computation | async-start | bytes 1048576 | tf_op jit(solution)/shard_map/all_to_all | solution.py:16
  47.3 19.3 %collective-permute-start.2 = (bf16[8,32,4096]{2,1,0:T(8,128)(2,1)}, bf16[8,32,4096]{2,1,0:T(8,128)(2,1)}, u32[]{:S(2)}, u32[]{:S(2)}) collective-permute-start(bf16[8,32,4096]{2,1,0:T(8,128)(2,1)} %all-to-all-done.2), channel_id=1, source_target_pairs={{0,1},{1,0},{2,3},{3,2},{4,5},{5,4},{6,7},{7,6},{8,9},{9,8},{10,11... | collective-permute-start | bytes 6291464 | tf_op jit(solution)/shard_map/ppermute | solution.py:64
  56.8 5.5 %collective-permute-start = (bf16[8,256,128]{2,1,0:T(8,128)(2,1)S(1)}, bf16[8,256,128]{2,1,0:T(8,128)(2,1)S(1)}, u32[]{:S(2)}, u32[]{:S(2)}) collective-permute-start(bf16[8,256,128]{2,1,0:T(8,128)(2,1)S(1)} %all-to-all-done), channel_id=1, source_target_pairs={{0,1},{1,0},{2,3},{3,2},{4,5},{5,4},{6,7},{7,6},{8,9},{9,8},{10,11... | collective-permute-start | bytes 1572872 | tf_op jit(solution)/shard_map/ppermute | solution.py:39
  62.3 0.6 copy-start.10
  62.3 1.7 %copy-start.4 = (bf16[8,1,32,256]{3,2,1,0:T(8,128)(2,1)S(1)}, bf16[8,1,32,256]{3,2,1,0:T(8,128)(2,1)}, u32[]{:S(2)}) copy-start(bf16[8,1,32,256]{3,2,1,0:T(8,128)(2,1)} %get-tuple-element.38) | copy-start | bytes 393220
  66.1 37.4 %collective-permute-start.1 = (bf16[256,4096]{1,0:T(8,128)(2,1)}, bf16[256,4096]{1,0:T(8,128)(2,1)}, u32[]{:S(2)}, u32[]{:S(2)}) collective-permute-start(bf16[256,4096]{1,0:T(8,128)(2,1)} %fusion.2), channel_id=1, source_target_pairs={{0,1},{1,0},{2,3},{3,2},{4,5},{5,4},{6,7},{7,6},{8,9},{9,8},{10,11... | collective-permute-start | bytes 6291464 | tf_op jit(solution)/shard_map/ppermute | solution.py:59
  78.2 3.9 %copy-start.11 = (pred[924]{0:T(1024)(128)(4,1)S(1)}, pred[924]{0:T(1024)(128)(4,1)}, u32[]{:S(2)}) copy-start(pred[924]{0:T(1024)(128)(4,1)} %fusion.14) | copy-start | bytes 2776
  81.7 0.7 copy-start.1
  82.5 9.3 %copy-start.5 = (bf16[8,1,32,924]{3,2,1,0:T(8,128)(2,1)S(1)}, bf16[8,1,32,924]{3,2,1,0:T(8,128)(2,1)}, u32[]{:S(2)}) copy-start(bf16[8,1,32,924]{3,2,1,0:T(8,128)(2,1)} %get-tuple-element.35) | copy-start | bytes 1419268
  86.4 12.8 %all-to-all-start.3 = ((bf16[8,148,128]{2,1,0:T(8,128)(2,1)}), bf16[8,148,128]{2,1,0:T(8,128)(2,1)S(1)}, u32[]{:S(2)}, u32[]{:S(2)}) async-start(bf16[8,148,128]{2,1,0:T(8,128)(2,1)} %pad_maximum_fusion.2), calls=%async_computation.3 | async-start | bytes 622592 | tf_op jit(solution)/shard_map/all_to_all | solution.py:90
  100.0 11.4 %all-to-all-start.4 = ((bf16[16,32,128]{2,1,0:T(8,128)(2,1)}), bf16[16,32,128]{2,1,0:T(8,128)(2,1)S(1)}, u32[]{:S(2)}, u32[]{:S(2)}) async-start(bf16[16,32,128]{2,1,0:T(8,128)(2,1)} %broadcast_in_dim.22), calls=%async_computation.4 | async-start | bytes 262144 | tf_op jit(solution)/shard_map/all_to_all | solution.py:16
  108.4 7.4 %copy-start.2 = (bf16[512,256]{1,0:T(8,128)(2,1)S(1)}, bf16[512,256]{1,0:T(8,128)(2,1)}, u32[]{:S(2)}) copy-start(bf16[512,256]{1,0:T(8,128)(2,1)} %copy-done.1) | copy-start | bytes 786436
  111.4 33.0 %all-to-all-start.1 = ((bf16[8,32,4096]{2,1,0:T(8,128)(2,1)}), bf16[8,32,4096]{2,1,0:T(8,128)(2,1)S(1)}, u32[]{:S(2)}, u32[]{:S(2)}) async-start(bf16[8,32,4096]{2,1,0:T(8,128)(2,1)} %bitcast.67), calls=%async_computation.1 | async-start | bytes 4194304 | tf_op jit(solution)/shard_map/all_to_all | solution.py:61
  145.4 17.1 %all-to-all-start.5 = ((bf16[8,372,128]{2,1,0:T(8,128)(2,1)}), bf16[8,372,128]{2,1,0:T(8,128)(2,1)S(1)}, u32[]{:S(2)}, u32[]{:S(2)}) async-start(bf16[8,372,128]{2,1,0:T(8,128)(2,1)} %broadcast_in_dim.23), calls=%async_computation.5 | async-start | bytes 1540096 | tf_op jit(solution)/shard_map/all_to_all | solution.py:16

commit v2 on v1

v2 whole, which is shorter than its diff:
```python
import jax
import jax.numpy as jnp
from jax import lax
from jax.experimental import pallas as pl
from jax.experimental.pallas import tpu as pltpu
from jax.sharding import Mesh, PartitionSpec as P

F32 = jnp.float32
BF16 = jnp.bfloat16
DP = ("zl", "x")
TENSOR = ("zh", "y", "c")
SWAP = [(0, 1), (1, 0)]
TURNS = (1, 3, 2)
VMEM = pl.BlockSpec(memory_space=pltpu.VMEM)
SMEM = pl.BlockSpec(memory_space=pltpu.SMEM)
ANY = pl.BlockSpec(memory_space=pl.ANY)
MIB = 1 << 20
CHUNKS = 10
HELD = ((0, 0, 0), (0, 1, 0), (1, 0, 1), (1, 1, 1), (2, 0, 3), (2, 1, 3), (3, 0, 2), (4, 0, 2))
SCALE = 100


def params(mib):
    return pltpu.CompilerParams(vmem_limit_bytes=mib * MIB)


def cost(flops, moved):
    return pl.CostEstimate(flops=flops // SCALE, bytes_accessed=moved // SCALE, transcendentals=0)


def turn(value, by):
    return lax.ppermute(value, "y", [(i, (i + by) % 4) for i in range(4)])


def spread(value, axes, count):
    whole = jnp.broadcast_to(value[None], (count,) + value.shape)
    return lax.all_to_all(whole, axes, 0, 0)


def dot(a, b):
    return jnp.dot(a, b, preferred_element_type=F32)


def dot_nt(a, b):
    return lax.dot_general(a, b, (((1,), (1,)), ((), ())), preferred_element_type=F32)


def base_rows(where, tokens, weight, other, own, held):
    step = pl.program_id(0)
    share = tokens.shape[0] // 16
    half = tokens.shape[0] // 2

    @pl.when(step == 0)
    def _():
        core, zh, y = where[0], where[1], where[2]
        for p in range(2):
            for z in range(2):
                for k in range(4):
                    c = 1 - core if p == 0 else core
                    zz = 1 - zh if z == 0 else zh
                    g = zz * 8 + lax.rem(y + (k + 1) % 4, 4) * 2 + c
                    at = p * half + (z * 4 + k) * share
                    held[at : at + share, :] = tokens[pl.ds(pl.multiple_of(g * share, share), share), :]

    total = dot(held[...], weight[...])
    other[...] = total[:half].astype(BF16)
    own[...] = total[half:]


def call_base_rows(where, tokens, weight, tile=1024):
    rows, hidden = tokens.shape
    width = weight.shape[1]
    half = rows // 2
    return pl.pallas_call(
        base_rows,
        grid=(width // tile,),
        in_specs=[
            SMEM,
            pl.BlockSpec((rows, hidden), lambda j: (0, 0)),
            pl.BlockSpec((hidden, tile), lambda j: (0, j)),
        ],
        out_specs=[pl.BlockSpec((half, tile), lambda j: (0, j))] * 2,
        out_shape=[
            jax.ShapeDtypeStruct((half, width), BF16),
            jax.ShapeDtypeStruct((half, width), F32),
        ],
        scratch_shapes=[pltpu.VMEM((rows, hidden), BF16)],
        compiler_params=params(60),
        name="base_rows",
        cost_estimate=cost(2 * rows * hidden * width, hidden * width * 2),
    )(where, tokens, weight)


def pair_sum(own, got, left, right, kept):
    total = own[...] + got[...].astype(F32)
    quarter = kept.shape[0]
    kept[...] = total[quarter:]
    step = pl.program_id(0)
    steps = pl.num_programs(0)

    @pl.when(step < steps // 2)
    def _():
        left[...] = total[:quarter].astype(BF16)

    @pl.when(step >= steps // 2)
    def _():
        right[...] = total[:quarter].astype(BF16)


def call_pair_sum(own, got, tile=1024):
    half, width = own.shape
    steps = width // tile
    mid = steps // 2
    out = (half // 2, tile)
    *sent, kept = pl.pallas_call(
        pair_sum,
        grid=(steps,),
        in_specs=[pl.BlockSpec((half, tile), lambda j: (0, j))] * 2,
        out_specs=[
            pl.BlockSpec(out, lambda j: (0, jnp.minimum(j, mid - 1))),
            pl.BlockSpec(out, lambda j: (0, jnp.maximum(j - mid, 0))),
            pl.BlockSpec(out, lambda j: (0, j)),
        ],
        out_shape=[jax.ShapeDtypeStruct((half // 2, width // 2), BF16)] * 2
        + [jax.ShapeDtypeStruct((half // 2, width), F32)],
        compiler_params=params(60),
        name="pair_sum",
        cost_estimate=cost(half * width, half * width * 9),
    )(own, got)
    return sent, kept


def quad_sum(kept, left, right, one, two, three, own):
    share = own.shape[0]
    first = pl.program_id(0) < pl.num_programs(0) // 2
    got = jnp.where(first, left[...], right[...]).astype(F32)
    for k, out in enumerate((one, two, three, own)):
        rows = slice(k * share, (k + 1) * share)
        out[...] = (kept[rows, :] + got[rows, :]).astype(out.dtype)


def call_quad_sum(kept, got, tile=1024):
    quarter, width = kept.shape
    share = quarter // 4
    steps = width // tile
    mid = steps // 2
    return pl.pallas_call(
        quad_sum,
        grid=(steps,),
        in_specs=[
            pl.BlockSpec((quarter, tile), lambda j: (0, j)),
            pl.BlockSpec((quarter, tile), lambda j: (0, jnp.minimum(j, mid - 1))),
            pl.BlockSpec((quarter, tile), lambda j: (0, jnp.maximum(j - mid, 0))),
        ],
        out_specs=[pl.BlockSpec((share, tile), lambda j: (0, j))] * 4,
        out_shape=[jax.ShapeDtypeStruct((share, width), BF16)] * 3
        + [jax.ShapeDtypeStruct((share, width), F32)],
        compiler_params=params(60),
        name="quad_sum",
        cost_estimate=cost(quarter * width, quarter * width * 8),
    )(kept, *got)


def reorder(order, inner, out, flat):
    count, share, channels = inner.shape
    block = order.shape[1]
    per = channels // block
    tiles = count * per
    for t in range(tiles):
        flat[t] = inner[t // per, :, (t % per) * block : (t % per + 1) * block].astype(F32)

    def one(j, _):
        wanted = jnp.broadcast_to(order[pl.ds(j, 1), :], (share, block))
        lane = wanted % block
        tile = wanted // block
        total = jnp.zeros((share, block), F32)
        for t in range(tiles):
            found = jnp.take_along_axis(flat[t], lane, axis=1, mode="promise_in_bounds")
            total = jnp.where(tile == t, found, total)
        out[j] = total.astype(BF16)
        return 0

    lax.fori_loop(0, tiles, one, 0)


def call_reorder(order, inner):
    count, share, channels = inner.shape
    tiles, block = order.shape
    return pl.pallas_call(
        reorder,
        in_specs=[VMEM] * 2,
        out_specs=VMEM,
        out_shape=jax.ShapeDtypeStruct((tiles, share, block), BF16),
        scratch_shapes=[pltpu.VMEM((tiles, share, block), F32)],
        compiler_params=params(60),
        name="reorder",
        cost_estimate=cost(tiles * tiles * share * block * 4, count * share * channels * 4),
    )(order, inner)


def sources(where):
    core, zh, y = where[0], where[1], where[2]
    found = []
    for c in range(2):
        for slot, (chunk, row, back) in enumerate(HELD):
            cc = core if c == 0 else 1 - core
            zz = zh if slot % 2 == 0 else 1 - zh
            place = zz * 8 + lax.rem(y + 4 - back, 4) * 2 + cc
            found.append((c * 5 + chunk, row, place))
    return found


def block_of(ref, z, i, share, block, base=0):
    each = block // share
    parts = [
        ref[z * share : (z + 1) * share, base + (i * each + q) * block : base + (i * each + q + 1) * block]
        for q in range(each)
    ]
    return jnp.concatenate(parts, axis=0)


def last_sum(where, own, one, two, three, mixed, *refs):
    chunks, out = refs[:CHUNKS], refs[CHUNKS]
    share = own.shape[0]
    block = mixed.shape[2]
    for chunk, z, g in sources(where):
        for i in range(2):
            n = g * 2 + i
            cols = pl.ds(pl.multiple_of(n * block, block), block)
            delta = dot(mixed[n], block_of(chunks[chunk], z, i, share, block))
            out[:, cols] = (
                delta
                + own[:, cols]
                + one[:, cols].astype(F32)
                + two[:, cols].astype(F32)
                + three[:, cols].astype(F32)
            )


def call_last_sum(where, own, parts, mixed, chunks):
    share, width = own.shape
    tiles, _, block = mixed.shape
    per = chunks[0].shape[1] - width
    second = [pl.BlockSpec((v.shape[0], per), lambda j: (0, width // per)) for v in chunks]
    whole = pl.BlockSpec((share, width), lambda j: (0, 0))
    return pl.pallas_call(
        last_sum,
        grid=(1,),
        in_specs=[SMEM] + [whole] * 4 + [pl.BlockSpec(mixed.shape, lambda j: (0, 0, 0))] + second,
        out_specs=whole,
        out_shape=jax.ShapeDtypeStruct((share, width), F32),
        compiler_params=params(60),
        name="last_sum",
        cost_estimate=cost(2 * share * width * block, share * width * 16),
    )(where, own, *parts, mixed, *chunks)


def factor_grads(where, order, mixed, tokens_t, *refs):
    chunks, (d_inner, sums, cot, routed) = refs[:CHUNKS], refs[CHUNKS:]
    core, zh, y = where[0], where[1], where[2]
    block = order.shape[1]
    rows, channels = d_inner.shape
    share = rows // 16
    width = cot.shape[1]
    hidden = tokens_t.shape[0]
    found = sources(where)
    place = zh * 8 + y * 2 + core
    row = lax.broadcasted_iota(jnp.int32, (channels, block), 0) + place * channels
    for chunk, z, g in found:
        cot[pl.ds(pl.multiple_of(g * share, share), share), :] = chunks[chunk][
            z * share : (z + 1) * share, :width
        ]
        for i in range(2):
            n = g * 2 + i
            hits = jnp.where(row == order[pl.ds(n, 1), :], 1.0, 0.0).astype(BF16)
            factor = block_of(chunks[chunk], z, i, share, block, width)
            cols = pl.ds(pl.multiple_of(n * block, block), block)
            routed[:, cols] = dot(hits, factor).astype(BF16)
    grad = dot_nt(cot[...], routed[...]).astype(BF16)
    d_inner[...] = grad
    whole = dot(tokens_t[...], grad)
    unit = lax.broadcasted_iota(jnp.int32, (hidden, block), 0)
    d_first = jnp.where(unit < hidden // 2, whole[:, :block], whole[:, block:]).astype(BF16)
    each = sums.shape[0] // 8
    few = channels // 8
    room = each - few
    for k in range(8):
        have = min(room, hidden - k * room)
        if have < room:
            sums[k * each : k * each + room, :] = jnp.zeros((room, block), BF16)
        sums[k * each : k * each + have, :] = d_first[k * room : k * room + have]
    mixed_t = mixed[...].reshape(rows, channels).T
    for i in range(channels // block):
        n = place * 2 + i
        cols = pl.ds(pl.multiple_of(n * block, block), block)
        d_second = dot(mixed_t[i * block : (i + 1) * block, :], cot[:, cols]).astype(BF16)
        for q in range(block // few):
            k = i * (block // few) + q
            sums[k * each + room : (k + 1) * each, :] = d_second[q * few : (q + 1) * few]


def call_factor_grads(where, order, mixed, tokens_t, chunks, room):
    groups, share, channels = mixed.shape
    rows = groups * share
    tiles, block = order.shape
    width = tiles * block
    each = room + channels // 8
    return pl.pallas_call(
        factor_grads,
        in_specs=[SMEM] + [VMEM] * (3 + CHUNKS),
        out_specs=[VMEM] * 2,
        out_shape=[
            jax.ShapeDtypeStruct((rows, channels), BF16),
            jax.ShapeDtypeStruct((8 * each, block), BF16),
        ],
        scratch_shapes=[pltpu.VMEM((rows, width), BF16), pltpu.VMEM((channels, width), BF16)],
        compiler_params=params(60),
        name="factor_grads",
        cost_estimate=cost(4 * rows * channels * width, rows * width * 2),
    )(where, order, mixed, tokens_t, *chunks)


def token_grads(where, weight, wide, d_inner, *refs):
    chunks, (out, cot) = refs[:CHUNKS], refs[CHUNKS:]
    share = cot.shape[0] // 16
    for chunk, z, g in sources(where):
        cot[pl.ds(pl.multiple_of(g * share, share), share), :] = chunks[chunk][
            z * share : (z + 1) * share, :
        ]
    term = dot_nt(weight[...], cot[...])

    @pl.when(pl.program_id(0) == 0)
    def _():
        out[...] = term + dot_nt(wide[...], d_inner[...])

    @pl.when(pl.program_id(0) > 0)
    def _():
        out[...] += term


def call_token_grads(where, weight, wide, d_inner, chunks, tile=1024):
    hidden, width = weight.shape
    rows, channels = d_inner.shape
    return pl.pallas_call(
        token_grads,
        grid=(width // tile,),
        in_specs=[
            SMEM,
            pl.BlockSpec((hidden, tile), lambda k: (0, k)),
            pl.BlockSpec((hidden, channels), lambda k: (0, 0)),
            pl.BlockSpec((rows, channels), lambda k: (0, 0)),
        ]
        + [pl.BlockSpec((v.shape[0], tile), lambda k: (0, k)) for v in chunks],
        out_specs=pl.BlockSpec((hidden, rows), lambda k: (0, 0)),
        out_shape=jax.ShapeDtypeStruct((hidden, rows), F32),
        scratch_shapes=[pltpu.VMEM((rows, tile), BF16)],
        compiler_params=params(60),
        name="token_grads",
        cost_estimate=cost(2 * rows * hidden * width, hidden * width * 2),
    )(where, weight, wide, d_inner, *chunks)


def per_device(tokens, base_weight, first_factor, second_factor, channel_order, cotangent):
    rows, hidden = tokens.shape
    blocks, block_in, block_out = first_factor.shape
    width = base_weight.shape[1]
    channels = blocks * block_out
    share = rows // 16
    room = -(-hidden // 128) * 16
    hold = lax.optimization_barrier
    where = jnp.stack([lax.axis_index("c"), lax.axis_index("zh"), lax.axis_index("y")])
    where = where.astype(jnp.int32)
    order = channel_order.reshape(-1, block_out)

    packed = second_factor.reshape(-1, share, block_out).transpose(1, 0, 2).reshape(share, -1)
    bundle = jnp.concatenate([cotangent, packed], axis=1)
    partner = lax.ppermute(bundle, "zh", SWAP)
    wide = jnp.concatenate(
        [
            jnp.pad(first_factor[n], ((0, 0), (n * block_out, channels - (n + 1) * block_out)))
            for n in range(blocks)
        ]
    )
    inner = dot(tokens, wide).astype(BF16).reshape(16, share, channels)
    bundle, partner, wide, inner, tokens = hold((bundle, partner, wide, inner, tokens))

    pair = jnp.concatenate([bundle, partner], axis=0)
    next_y, last_y = turn(pair, 1), turn(pair, 3)
    inner = lax.all_to_all(inner, TENSOR, 0, 0)
    other, own = call_base_rows(where, tokens, base_weight)
    pair, next_y, last_y, inner, other, own = hold((pair, next_y, last_y, inner, other, own))

    got = lax.ppermute(other, "c", SWAP)
    far = turn(pair[:share], 2)
    mine = [pair, next_y, last_y]
    theirs = [lax.ppermute(v, "c", SWAP) for v in mine]
    mixed = call_reorder(order, inner)
    sent, kept = call_pair_sum(own, got)
    far, theirs, mixed, sent, kept, pair = hold((far, theirs, mixed, sent, kept, pair))

    left = lax.ppermute(sent[0], "zh", SWAP)
    far_z = turn(pair[share:], 2)
    mixed_mine = mixed.reshape(16, blocks, share, block_out).transpose(0, 2, 1, 3)
    mixed_mine = lax.all_to_all(mixed_mine.reshape(16, share, channels), TENSOR, 0, 0)
    left, far, far_z, mixed_mine, right = hold((left, far, far_z, mixed_mine, sent[1]))

    right = lax.ppermute(right, "zh", SWAP)
    theirs = theirs + [lax.ppermute(v, "c", SWAP) for v in (far, far_z)]
    chunks = mine + [far, far_z] + theirs
    d_inner, sums = call_factor_grads(where, order, mixed_mine, tokens.T, chunks, room)
    sums = lax.all_to_all(sums.reshape(8, -1, block_out), DP, 0, 0)
    right, sums, d_inner = hold((right, sums, d_inner))

    terms = call_quad_sum(kept, [left, right])
    parts = [turn(terms[d - 1], d) for d in (1, 2, 3)]
    sums = jnp.sum(sums.astype(F32), axis=0).astype(BF16)
    final = spread(sums, DP, 8)
    d_tokens = call_token_grads(where, base_weight, wide, d_inner, chunks).T
    parts, final, d_tokens = hold((parts, final, d_tokens))

    output = call_last_sum(where, terms[3], parts, mixed, chunks)
    d_first = final[:, :room].reshape(-1, block_out)[:hidden].astype(F32)
    d_second = final[:, room:].astype(F32)
    return (
        output,
        d_tokens,
        d_first.reshape(blocks, block_in, block_out),
        d_second.reshape(blocks, block_out, block_out),
    )


def solution(mesh):
    fine = Mesh(mesh.devices.reshape(2, 4, 2, 4, 2), ("zl", "x", "zh", "y", "c"))
    return jax.shard_map(
        per_device,
        mesh=fine,
        in_specs=(
            P(DP, TENSOR),
            P(TENSOR, None),
            P(TENSOR, None, None),
            P(TENSOR, None, None),
            P(),
            P(DP + TENSOR, None),
        ),
        out_specs=(
            P(DP + TENSOR, None),
            P(DP, TENSOR),
            P(TENSOR, None, None),
            P(TENSOR, None, None),
        ),
        check_vma=False,
    )
```

time: 167 us -> 123 us (0.74)
  waiting for transfers between devices: 62.1 us -> 13.5 us
  Pallas kernels: 0 us -> 44.3 us
  matrix products: 40.8 us -> 0.46 us
  blocking collectives: 0 us -> 15.1 us
  local copies, waits for them, and re-layouts: 19.3 us -> 9.5 us
  other arithmetic: 8.16 us -> 2.16 us
  starting transfers between devices: 33.1 us -> 35.8 us
    pallas_call x0 -> x7, Pallas kernels: none -> 44.3 us  [the longest x1 10.1 us: call_token_grads(): pl.pallas_call(token_grads, grid=(width // tile,), in_specs=[SMEM, pl.Blo...]
    dot_general x12 -> x1, matrix products: 40.8 us -> 0.46 us  [dot(): return jnp.dot(a, b, preferred_element_type=F32)]
    all_to_all x4 -> x1, waiting for transfers between devices: 35.6 us -> 0.01 us  [spread(): return lax.all_to_all(whole, axes, 0, 0)]
    ppermute x3 -> x16, starting transfers between devices: 0.59 us -> 19.9 us  [the longest x7 9.92 us: turn(): return lax.ppermute(value, 'y', [(i, (i + by) % 4) for i in range(4)])]
    all_to_all x4 -> x1, starting transfers between devices: 23 us -> 4.51 us  [spread(): return lax.all_to_all(whole, axes, 0, 0)]
    all_to_all x2, waiting for transfers between devices: 26.5 us -> 8.29 us  [the longest x1 6.12 us: per_device(): sums = lax.all_to_all(sums.reshape(8, -1, block_out), DP, 0, 0)]
    all_to_all x0 -> x1, blocking collectives: none -> 15.1 us  [per_device(): lax.all_to_all(mixed_mine.reshape(16, share, channels), TENSOR, 0, 0)]
    dot_general x1 -> x0, local copies, waits for them, and re-layouts: 6.52 us -> none  [per_device(): lax.dot_general(inner, cot_all, (((0,), (0,)), ((), ())), preferred_eleme...]
  transfers between devices with their start and end apart: 9 -> 19, of which waited for: 5 -> 5; matrix products, arithmetic and copies ran while one was open for 37% -> 6% of each run, Pallas kernels for 0% -> 34%
where the time goes in v2:
time: 123 us; the launch traced here: 122 us
  Pallas kernels  44.3 us (36%)
  starting transfers between devices  35.8 us (29%)
  blocking collectives  15.1 us (12%)
  waiting for transfers between devices  13.5 us (11%)
  local copies, waits for them, and re-layouts  9.5 us (8%)
  other arithmetic  2.16 us (2%)
    all_to_all x1, blocking collectives, per_device(): lax.all_to_all(mixed_mine.reshape(16, share, channels), TENSOR, 0, 0)  15.1 us
    pallas_call x1, Pallas kernels, call_token_grads(): pl.pallas_call(token_grads, grid=(width // tile,), in_specs=[SMEM, pl.Blo...  10.1 us
    ppermute x7, starting transfers between devices, turn(): return lax.ppermute(value, 'y', [(i, (i + by) % 4) for i in range(4)])  9.92 us
    pallas_call x1, Pallas kernels, call_base_rows(): pl.pallas_call(base_rows, grid=(width // tile,), in_specs=[SMEM, pl.Block...  8.96 us
    pallas_call x1, Pallas kernels, call_factor_grads(): pl.pallas_call(factor_grads, in_specs=[SMEM] + [VMEM] * (3 + CHUNKS), out...  6.99 us
    pallas_call x1, Pallas kernels, call_reorder(): pl.pallas_call(reorder, in_specs=[VMEM] * 2, out_specs=VMEM, out_shape=ja...  6.41 us
    all_to_all x1, waiting for transfers between devices, per_device(): sums = lax.all_to_all(sums.reshape(8, -1, block_out), DP, 0, 0)  6.12 us
    all_to_all x1, starting transfers between devices, per_device(): inner = lax.all_to_all(inner, TENSOR, 0, 0)  6.04 us
  transfers between devices with their start and end apart: 19, of which 5 were waited for; matrix products, arithmetic and copies ran while one was open for 6% of the time, Pallas kernels for 34%

profile of v2, /device:TPU:2, one launch (start us, length us, event | category | flops | bytes accessed | tf_op | source)
XLA Modules:
  0.0 121.7 jit_solution(13237402577429066720)
XLA Ops:
  0.6 1.1 constant_dynamic-update-slice_fusion
  1.7 0.9 copy.16
  2.6 4.0 %collective-permute-start = (bf16[32,5120]{1,0:T(8,128)(2,1)S(1)}, bf16[32,5120]{1,0:T(8,128)(2,1)S(1)}, u32[]{:S(2)}, u32[]{:S(2)}) collective-permute-start(bf16[32,5120]{1,0:T(8,128)(2,1)S(1)} %bitcast_dynamic-update-slice_fusion), channel_id=1, source_target_pairs={{0,8},{8,0},{1,9},{9,1},{2,10},{10,2},{3,11},{11,3},{4,12},{12,4},... | collective-permute-start | bytes 983048 | tf_op jit(solution)/shard_map/ppermute | solution.py:377
  6.5 1.5 %fusion.5 = (bf16[1,462,128]{2,0,1:T(2,128)(2,1)S(1)}, bf16[1,462,128]{2,0,1:T(2,128)(2,1)S(1)}) fusion(bf16[2,462,128]{2,0,1:T(2,128)(2,1)} %param.8), kind=kLoop, calls=%fused_computation.17 | loop fusion | bytes 473088 | tf_op jit(solution)/shard_map/slice | solution.py:380
  8.5 0.8 copy.19
  9.4 0.8 fusion.3.wide
  10.2 4.0 %collective-permute-done = bf16[32,5120]{1,0:T(8,128)(2,1)S(1)} collective-permute-done((bf16[32,5120]{1,0:T(8,128)(2,1)S(1)}, bf16[32,5120]{1,0:T(8,128)(2,1)S(1)}, u32[]{:S(2)}, u32[]{:S(2)}) %collective-permute-start) | collective-permute-done | bytes 327712 | tf_op jit(solution)/shard_map/ppermute | solution.py:377
  14.3 1.6 %collective-permute-start.1 = (bf16[64,5120]{1,0:T(8,128)(2,1)S(1)}, bf16[64,5120]{1,0:T(8,128)(2,1)S(1)}, u32[]{:S(2)}, u32[]{:S(2)}) collective-permute-start(bf16[64,5120]{1,0:T(8,128)(2,1)S(1)} %constant_dynamic-update-slice_fusion.1.refs_0_), channel_id=1, source_target_pairs={{0,2},{2,4},{4,6},{6,0},{1,3},{3,5},{5,7},{7,1},{8,10},{10,12},{12... | collective-permute-start | bytes 1966088 | tf_op jit(solution)/shard_map/ppermute | solution.py:32
  16.0 1.7 %collective-permute-start.2 = (bf16[64,5120]{1,0:T(8,128)(2,1)S(1)}, bf16[64,5120]{1,0:T(8,128)(2,1)S(1)}, u32[]{:S(2)}, u32[]{:S(2)}) collective-permute-start(bf16[64,5120]{1,0:T(8,128)(2,1)S(1)} %constant_dynamic-update-slice_fusion.1.refs_0_), channel_id=1, source_target_pairs={{0,6},{2,0},{4,2},{6,4},{1,7},{3,1},{5,3},{7,5},{8,14},{10,8},{12,... | collective-permute-start | bytes 1966088 | tf_op jit(solution)/shard_map/ppermute | solution.py:32
  17.6 6.0 %all-to-all-start = ((bf16[16,32,256]{2,1,0:T(8,128)(2,1)}), bf16[16,32,256]{2,1,0:T(8,128)(2,1)S(1)}, u32[]{:S(2)}, u32[]{:S(2)}) async-start(bf16[16,32,256]{2,1,0:T(8,128)(2,1)} %bitcast.8), calls=%async_computation | async-start | bytes 524288 | tf_op jit(solution)/shard_map/all_to_all | solution.py:389
  24.3 1.3 %copy.20.tokens = bf16[512,924]{1,0:T(8,128)(2,1)} copy(bf16[512,924]{0,1:T(8,128)(2,1)S(1)} %copy-done.5) | data formatting | bytes 1892352 | tf_op jit(solution)/shard_map/optimization_barrier | solution.py:385
  25.6 9.0 %base_rows.1 = (bf16[256,4096]{1,0:T(8,128)(2,1)}, f32[256,4096]{1,0:T(8,128)}) custom-call(s32[3]{0:T(128)} %pad_add_fusion.where, bf16[512,924]{1,0:T(8,128)(2,1)} %copy.20.tokens, bf16[924,4096]{1,0:T(8,128)(2,1)} %weight.3), custom_call_target="tpu_custom_call" | custom-call | flops 38755368 | bytes 75694 | tf_op jit(solution)/shard_map/base_rows/pallas_call | solution.py:74
  34.5 2.2 %all-to-all-done.inner = bf16[16,32,256]{2,1,0:T(8,128)(2,1)S(1)} async-done(((bf16[16,32,256]{2,1,0:T(8,128)(2,1)}), bf16[16,32,256]{2,1,0:T(8,128)(2,1)S(1)}, u32[]{:S(2)}, u32[]{:S(2)}) %all-to-all-start) | async-done | bytes 262176 | tf_op jit(solution)/shard_map/all_to_all | solution.py:389
  37.9 0.7 slice.23
  38.7 1.9 %collective-permute-start.3 = (bf16[32,5120]{1,0:T(8,128)(2,1)}, bf16[32,5120]{1,0:T(8,128)(2,1)S(1)}, u32[]{:S(2)}, u32[]{:S(2)}) collective-permute-start(bf16[32,5120]{1,0:T(8,128)(2,1)} %slice.23), channel_id=1, source_target_pairs={{0,4},{2,6},{4,0},{6,2},{1,5},{3,7},{5,1},{7,3},{8,12},{10,14},{12... | collective-permute-start | bytes 983048 | tf_op jit(solution)/shard_map/ppermute | solution.py:32
  40.6 6.4 %reorder.1.mixed = bf16[32,32,128]{2,1,0:T(8,128)(2,1)} custom-call(s32[32,128]{1,0:T(8,128)} %bitcast.37, bf16[16,32,256]{2,1,0:T(8,128)(2,1)} %copy-done.11), custom_call_target="tpu_custom_call" | custom-call | flops 167772 | bytes 5242 | tf_op jit(solution)/shard_map/reorder/pallas_call | solution.py:189
  47.0 5.0 %pair_sum.1 = (bf16[128,2048]{1,0:T(8,128)(2,1)}, bf16[128,2048]{1,0:T(8,128)(2,1)}, f32[128,4096]{1,0:T(8,128)}) custom-call(f32[256,4096]{1,0:T(8,128)} %get-tuple-element.58.own, bf16[256,4096]{1,0:T(8,128)(2,1)} %collective-permute-done.7.got), custom_call_target="tpu_custom_call" | custom-call | flops 10485 | bytes 94371 | tf_op jit(solution)/shard_map/pair_sum/pallas_call | solution.py:115
  52.1 2.3 %collective-permute-start.8 = (bf16[128,2048]{1,0:T(8,128)(2,1)}, bf16[128,2048]{1,0:T(8,128)(2,1)S(1)}, u32[]{:S(2)}, u32[]{:S(2)}) collective-permute-start(bf16[128,2048]{1,0:T(8,128)(2,1)} %get-tuple-element.64), channel_id=1, source_target_pairs={{0,8},{8,0},{1,9},{9,1},{2,10},{10,2},{3,11},{11,3},{4,12},{12,4},... | collective-permute-start | bytes 1572872 | tf_op jit(solution)/shard_map/ppermute | solution.py:401
  55.6 15.1 %all_to_all.20.mixed = bf16[16,32,256]{2,1,0:T(8,128)(2,1)} all-to-all(bf16[16,32,256]{2,1,0:T(8,128)(2,1)S(1)} %reshape.50), channel_id=1, replica_groups=mesh['zl'=2,'x'=4,'zh'=2,'y'=4,'c'=2] {'zh','y','c'}, dimensions={0} | all-to-all | bytes 524288 | tf_op jit(solution)/shard_map/all_to_all | solution.py:404
  71.3 1.9 %collective-permute-start.10 = (bf16[128,2048]{1,0:T(8,128)(2,1)}, bf16[128,2048]{1,0:T(8,128)(2,1)}, u32[]{:S(2)}, u32[]{:S(2)}) collective-permute-start(bf16[128,2048]{1,0:T(8,128)(2,1)} %get-tuple-element.70), channel_id=1, source_target_pairs={{0,8},{8,0},{1,9},{9,1},{2,10},{10,2},{3,11},{11,3},{4,12},{12,4},... | collective-permute-start | bytes 1572872 | tf_op jit(solution)/shard_map/ppermute | solution.py:407
  74.1 7.0 %factor_grads.1 = (bf16[512,256]{1,0:T(8,128)(2,1)}, bf16[1280,128]{1,0:T(8,128)(2,1)}) custom-call(s32[3]{0:T(128)} %pad_add_fusion.where, s32[32,128]{1,0:T(8,128)} %bitcast.38, bf16[16,32,256]{2,1,0:T(8,128)(2,1)} %all_to_all.20.mixed, bf16[924,512]{1,0:T(8,128)(2,1)} %bitcast.29, bf16[64,5120]{1,0:T(8,128)(2,1)} %copy-done, bf16[64,5120]{1,0:T(8,128)(2,1)} %copy-done.1, ...), custom_call_target="tpu_custom_call" | custom-call | flops 21474836 | bytes 41943 | tf_op jit(solution)/shard_map/factor_grads/pallas_call | solution.py:308
  81.1 5.3 %all-to-all-start.2 = ((bf16[8,160,128]{2,1,0:T(8,128)(2,1)}), bf16[8,160,128]{2,1,0:T(8,128)(2,1)S(1)}, u32[]{:S(2)}, u32[]{:S(2)}) async-start(bf16[8,160,128]{2,1,0:T(8,128)(2,1)} %bitcast.34), calls=%async_computation.2 | async-start | bytes 655360 | tf_op jit(solution)/shard_map/all_to_all | solution.py:411
  87.0 6.1 %all-to-all-done.2 = bf16[8,160,128]{2,1,0:T(8,128)(2,1)S(1)} async-done(((bf16[8,160,128]{2,1,0:T(8,128)(2,1)}), bf16[8,160,128]{2,1,0:T(8,128)(2,1)S(1)}, u32[]{:S(2)}, u32[]{:S(2)}) %all-to-all-start.2) | async-done | bytes 327712 | tf_op jit(solution)/shard_map/all_to_all | solution.py:411
  93.2 0.8 broadcast_in_dim.2
  94.0 4.5 %all-to-all-start.3 = ((bf16[8,160,128]{2,1,0:T(8,128)(2,1)}), bf16[8,160,128]{2,1,0:T(8,128)(2,1)S(1)}, u32[]{:S(2)}, u32[]{:S(2)}) async-start(bf16[8,160,128]{2,1,0:T(8,128)(2,1)} %broadcast_in_dim.2), calls=%async_computation.3 | async-start | bytes 655360 | tf_op jit(solution)/shard_map/all_to_all | solution.py:37
  98.5 3.9 %quad_sum.1 = (bf16[32,4096]{1,0:T(8,128)(2,1)}, bf16[32,4096]{1,0:T(8,128)(2,1)}, bf16[32,4096]{1,0:T(8,128)(2,1)}, f32[32,4096]{1,0:T(8,128)}) custom-call(f32[128,4096]{1,0:T(8,128)} %get-tuple-element.63.kept, bf16[128,2048]{1,0:T(8,128)(2,1)} %copy-done.12, bf16[128,2048]{1,0:T(8,128)(2,1)} %collective-permute-done.10.right), custom_call_target="tpu_custom_call" | custom-call | flops 5242 | bytes 41943 | tf_op jit(solution)/shard_map/quad_sum/pallas_call | solution.py:147
  102.4 1.1 collective-permute-start.13
  103.5 2.1 %collective-permute-start.14 = (bf16[32,4096]{1,0:T(8,128)(2,1)}, bf16[32,4096]{1,0:T(8,128)(2,1)S(1)}, u32[]{:S(2)}, u32[]{:S(2)}) collective-permute-start(bf16[32,4096]{1,0:T(8,128)(2,1)} %get-tuple-element.82), channel_id=1, source_target_pairs={{0,4},{2,6},{4,0},{6,2},{1,5},{3,7},{5,1},{7,3},{8,12},{10,14},{12... | collective-permute-start | bytes 786440 | tf_op jit(solution)/shard_map/ppermute | solution.py:32
  105.6 0.9 collective-permute-start.15
  106.5 10.1 %token_grads.1 = f32[924,512]{1,0:T(8,128)} custom-call(s32[3]{0:T(128)} %pad_add_fusion.where, bf16[924,4096]{1,0:T(8,128)(2,1)} %weight.3, bf16[924,256]{1,0:T(8,128)(2,1)} %fusion.3.wide, bf16[512,256]{1,0:T(8,128)(2,1)} %get-tuple-element.86.d_inner, bf16[64,5120]{1,0:T(8,128)(2,1)} %copy-done, bf16[64,5120]{1,0:T(8,128)(2,1)} %copy-done.1, ...), custom_call_target="tpu_custom_call" | custom-call | flops 38755368 | bytes 75694 | tf_op jit(solution)/shard_map/token_grads/pallas_call | solution.py:344
  117.2 1.0 copy.22
  118.9 2.9 %last_sum.1 = f32[32,4096]{1,0:T(8,128)} custom-call(s32[3]{0:T(128)} %pad_add_fusion.where, f32[32,4096]{1,0:T(8,128)} %get-tuple-element.80.own, bf16[32,4096]{1,0:T(8,128)(2,1)} %copy-done.13, bf16[32,4096]{1,0:T(8,128)(2,1)} %copy-done.14, bf16[32,4096]{1,0:T(8,128)(2,1)} %copy-done.15, bf16[32,32,128]{2,1,0:T(8,128)(2,1)} %reorder.1.mixed, ...), custom_call_target="tpu_custom_call" | custom-call | flops 335544 | bytes 20971 | tf_op jit(solution)/shard_map/last_sum/pallas_call | solution.py:246
  (70 shorter events, 6.9 us)
Async XLA Ops:
  0.6 7.4 %copy-start.5 = (bf16[512,924]{0,1:T(8,128)(2,1)S(1)}, bf16[512,924]{0,1:T(8,128)(2,1)}, u32[]{:S(2)}) copy-start(bf16[512,924]{0,1:T(8,128)(2,1)} %param.6) | copy-start | bytes 2838532
  2.6 11.7 %collective-permute-start = (bf16[32,5120]{1,0:T(8,128)(2,1)S(1)}, bf16[32,5120]{1,0:T(8,128)(2,1)S(1)}, u32[]{:S(2)}, u32[]{:S(2)}) collective-permute-start(bf16[32,5120]{1,0:T(8,128)(2,1)S(1)} %bitcast_dynamic-update-slice_fusion), channel_id=1, source_target_pairs={{0,8},{8,0},{1,9},{9,1},{2,10},{10,2},{3,11},{11,3},{4,12},{12,4},... | collective-permute-start | bytes 983048 | tf_op jit(solution)/shard_map/ppermute | solution.py:377
  14.3 40.1 %copy-start = (bf16[64,5120]{1,0:T(8,128)(2,1)}, bf16[64,5120]{1,0:T(8,128)(2,1)S(1)}, u32[]{:S(2)}) copy-start(bf16[64,5120]{1,0:T(8,128)(2,1)S(1)} %constant_dynamic-update-slice_fusion.1.refs_0_) | copy-start | bytes 1966084
  14.3 22.4 %collective-permute-start.1 = (bf16[64,5120]{1,0:T(8,128)(2,1)S(1)}, bf16[64,5120]{1,0:T(8,128)(2,1)S(1)}, u32[]{:S(2)}, u32[]{:S(2)}) collective-permute-start(bf16[64,5120]{1,0:T(8,128)(2,1)S(1)} %constant_dynamic-update-slice_fusion.1.refs_0_), channel_id=1, source_target_pairs={{0,2},{2,4},{4,6},{6,0},{1,3},{3,5},{5,7},{7,1},{8,10},{10,12},{12... | collective-permute-start | bytes 1966088 | tf_op jit(solution)/shard_map/ppermute | solution.py:32
  16.0 20.7 %collective-permute-start.2 = (bf16[64,5120]{1,0:T(8,128)(2,1)S(1)}, bf16[64,5120]{1,0:T(8,128)(2,1)S(1)}, u32[]{:S(2)}, u32[]{:S(2)}) collective-permute-start(bf16[64,5120]{1,0:T(8,128)(2,1)S(1)} %constant_dynamic-update-slice_fusion.1.refs_0_), channel_id=1, source_target_pairs={{0,6},{2,0},{4,2},{6,4},{1,7},{3,1},{5,3},{7,5},{8,14},{10,8},{12,... | collective-permute-start | bytes 1966088 | tf_op jit(solution)/shard_map/ppermute | solution.py:32
  17.6 19.1 %all-to-all-start = ((bf16[16,32,256]{2,1,0:T(8,128)(2,1)}), bf16[16,32,256]{2,1,0:T(8,128)(2,1)S(1)}, u32[]{:S(2)}, u32[]{:S(2)}) async-start(bf16[16,32,256]{2,1,0:T(8,128)(2,1)} %bitcast.8), calls=%async_computation | async-start | bytes 524288 | tf_op jit(solution)/shard_map/all_to_all | solution.py:389
  36.7 3.9 %copy-start.11 = (bf16[16,32,256]{2,1,0:T(8,128)(2,1)}, bf16[16,32,256]{2,1,0:T(8,128)(2,1)S(1)}, u32[]{:S(2)}) copy-start(bf16[16,32,256]{2,1,0:T(8,128)(2,1)S(1)} %all-to-all-done.inner) | copy-start | bytes 786436
  36.7 15.4 %copy-start.1 = (bf16[64,5120]{1,0:T(8,128)(2,1)}, bf16[64,5120]{1,0:T(8,128)(2,1)S(1)}, u32[]{:S(2)}) copy-start(bf16[64,5120]{1,0:T(8,128)(2,1)S(1)} %collective-permute-done.1.refs_1_) | copy-start | bytes 1966084
  36.7 15.3 %copy-start.2 = (bf16[64,5120]{1,0:T(8,128)(2,1)}, bf16[64,5120]{1,0:T(8,128)(2,1)S(1)}, u32[]{:S(2)}) copy-start(bf16[64,5120]{1,0:T(8,128)(2,1)S(1)} %collective-permute-done.2.refs_2_) | copy-start | bytes 1966084
  36.7 10.3 %collective-permute-start.7 = (bf16[256,4096]{1,0:T(8,128)(2,1)}, bf16[256,4096]{1,0:T(8,128)(2,1)}, u32[]{:S(2)}, u32[]{:S(2)}) collective-permute-start(bf16[256,4096]{1,0:T(8,128)(2,1)} %get-tuple-element.59), channel_id=1, source_target_pairs={{0,1},{1,0},{2,3},{3,2},{4,5},{5,4},{6,7},{7,6},{8,9},{9,8},{10,11... | collective-permute-start | bytes 6291464 | tf_op jit(solution)/shard_map/ppermute | solution.py:393
  37.3 14.8 %collective-permute-start.4 = (bf16[64,5120]{1,0:T(8,128)(2,1)S(1)}, bf16[64,5120]{1,0:T(8,128)(2,1)S(1)}, u32[]{:S(2)}, u32[]{:S(2)}) collective-permute-start(bf16[64,5120]{1,0:T(8,128)(2,1)S(1)} %constant_dynamic-update-slice_fusion.1.refs_0_), channel_id=1, source_target_pairs={{0,1},{1,0},{2,3},{3,2},{4,5},{5,4},{6,7},{7,6},{8,9},{9,8},{10,11... | collective-permute-start | bytes 1966088 | tf_op jit(solution)/shard_map/ppermute | solution.py:396
  37.4 14.7 %collective-permute-start.5 = (bf16[64,5120]{1,0:T(8,128)(2,1)S(1)}, bf16[64,5120]{1,0:T(8,128)(2,1)S(1)}, u32[]{:S(2)}, u32[]{:S(2)}) collective-permute-start(bf16[64,5120]{1,0:T(8,128)(2,1)S(1)} %collective-permute-done.1.refs_1_), channel_id=1, source_target_pairs={{0,1},{1,0},{2,3},{3,2},{4,5},{5,4},{6,7},{7,6},{8,9},{9,8},{10,11... | collective-permute-start | bytes 1966088 | tf_op jit(solution)/shard_map/ppermute | solution.py:396
  37.8 14.3 %collective-permute-start.6 = (bf16[64,5120]{1,0:T(8,128)(2,1)S(1)}, bf16[64,5120]{1,0:T(8,128)(2,1)}, u32[]{:S(2)}, u32[]{:S(2)}) collective-permute-start(bf16[64,5120]{1,0:T(8,128)(2,1)S(1)} %collective-permute-done.2.refs_2_), channel_id=1, source_target_pairs={{0,1},{1,0},{2,3},{3,2},{4,5},{5,4},{6,7},{7,6},{8,9},{9,8},{10,11... | collective-permute-start | bytes 1966088 | tf_op jit(solution)/shard_map/ppermute | solution.py:396
  38.7 13.4 %collective-permute-start.3 = (bf16[32,5120]{1,0:T(8,128)(2,1)}, bf16[32,5120]{1,0:T(8,128)(2,1)S(1)}, u32[]{:S(2)}, u32[]{:S(2)}) collective-permute-start(bf16[32,5120]{1,0:T(8,128)(2,1)} %slice.23), channel_id=1, source_target_pairs={{0,4},{2,6},{4,0},{6,2},{1,5},{3,7},{5,1},{7,3},{8,12},{10,14},{12... | collective-permute-start | bytes 983048 | tf_op jit(solution)/shard_map/ppermute | solution.py:32
  47.0 8.1 %copy-start.10 = (bf16[32,32,128]{2,1,0:T(8,128)(2,1)S(1)}, bf16[32,32,128]{2,1,0:T(8,128)(2,1)}, u32[]{:S(2)}) copy-start(bf16[32,32,128]{2,1,0:T(8,128)(2,1)} %reorder.1.mixed) | copy-start | bytes 786436
  52.1 2.4 %copy-start.6 = (bf16[32,5120]{1,0:T(8,128)(2,1)}, bf16[32,5120]{1,0:T(8,128)(2,1)S(1)}, u32[]{:S(2)}) copy-start(bf16[32,5120]{1,0:T(8,128)(2,1)S(1)} %collective-permute-done.3.refs_3_) | copy-start | bytes 983044
  52.1 21.1 %copy-start.3 = (bf16[64,5120]{1,0:T(8,128)(2,1)}, bf16[64,5120]{1,0:T(8,128)(2,1)S(1)}, u32[]{:S(2)}) copy-start(bf16[64,5120]{1,0:T(8,128)(2,1)S(1)} %collective-permute-done.4.refs_5_) | copy-start | bytes 1966084
  52.1 21.1 %copy-start.4 = (bf16[64,5120]{1,0:T(8,128)(2,1)}, bf16[64,5120]{1,0:T(8,128)(2,1)S(1)}, u32[]{:S(2)}) copy-start(bf16[64,5120]{1,0:T(8,128)(2,1)S(1)} %collective-permute-done.5.refs_6_) | copy-start | bytes 1966084
  52.1 18.5 %collective-permute-start.8 = (bf16[128,2048]{1,0:T(8,128)(2,1)}, bf16[128,2048]{1,0:T(8,128)(2,1)S(1)}, u32[]{:S(2)}, u32[]{:S(2)}) collective-permute-start(bf16[128,2048]{1,0:T(8,128)(2,1)} %get-tuple-element.64), channel_id=1, source_target_pairs={{0,8},{8,0},{1,9},{9,1},{2,10},{10,2},{3,11},{11,3},{4,12},{12,4},... | collective-permute-start | bytes 1572872 | tf_op jit(solution)/shard_map/ppermute | solution.py:401
  54.5 16.2 %collective-permute-start.9 = (bf16[32,5120]{1,0:T(8,128)(2,1)S(1)}, bf16[32,5120]{1,0:T(8,128)(2,1)S(1)}, u32[]{:S(2)}, u32[]{:S(2)}) collective-permute-start(bf16[32,5120]{1,0:T(8,128)(2,1)S(1)} %slice.24), channel_id=1, source_target_pairs={{0,4},{2,6},{4,0},{6,2},{1,5},{3,7},{5,1},{7,3},{8,12},{10,14},{12... | collective-permute-start | bytes 983048 | tf_op jit(solution)/shard_map/ppermute | solution.py:32
  70.7 2.6 %copy-start.7 = (bf16[32,5120]{1,0:T(8,128)(2,1)}, bf16[32,5120]{1,0:T(8,128)(2,1)S(1)}, u32[]{:S(2)}) copy-start(bf16[32,5120]{1,0:T(8,128)(2,1)S(1)} %collective-permute-done.9.refs_4_) | copy-start | bytes 983044
  70.7 27.8 %copy-start.12 = (bf16[128,2048]{1,0:T(8,128)(2,1)}, bf16[128,2048]{1,0:T(8,128)(2,1)S(1)}, u32[]{:S(2)}) copy-start(bf16[128,2048]{1,0:T(8,128)(2,1)S(1)} %collective-permute-done.8.left) | copy-start | bytes 1572868
  70.7 2.5 %collective-permute-start.11 = (bf16[32,5120]{1,0:T(8,128)(2,1)}, bf16[32,5120]{1,0:T(8,128)(2,1)S(1)}, u32[]{:S(2)}, u32[]{:S(2)}) collective-permute-start(bf16[32,5120]{1,0:T(8,128)(2,1)} %copy-done.6), channel_id=1, source_target_pairs={{0,1},{1,0},{2,3},{3,2},{4,5},{5,4},{6,7},{7,6},{8,9},{9,8},{10,11... | collective-permute-start | bytes 983048 | tf_op jit(solution)/shard_map/ppermute | solution.py:408
  70.9 2.4 %collective-permute-start.12 = (bf16[32,5120]{1,0:T(8,128)(2,1)S(1)}, bf16[32,5120]{1,0:T(8,128)(2,1)S(1)}, u32[]{:S(2)}, u32[]{:S(2)}) collective-permute-start(bf16[32,5120]{1,0:T(8,128)(2,1)S(1)} %collective-permute-done.9.refs_4_), channel_id=1, source_target_pairs={{0,1},{1,0},{2,3},{3,2},{4,5},{5,4},{6,7},{7,6},{8,9},{9,8},{10,11... | collective-permute-start | bytes 983048 | tf_op jit(solution)/shard_map/ppermute | solution.py:408
  71.3 15.8 %collective-permute-start.10 = (bf16[128,2048]{1,0:T(8,128)(2,1)}, bf16[128,2048]{1,0:T(8,128)(2,1)}, u32[]{:S(2)}, u32[]{:S(2)}) collective-permute-start(bf16[128,2048]{1,0:T(8,128)(2,1)} %get-tuple-element.70), channel_id=1, source_target_pairs={{0,8},{8,0},{1,9},{9,1},{2,10},{10,2},{3,11},{11,3},{4,12},{12,4},... | collective-permute-start | bytes 1572872 | tf_op jit(solution)/shard_map/ppermute | solution.py:407
  81.1 12.1 %all-to-all-start.2 = ((bf16[8,160,128]{2,1,0:T(8,128)(2,1)}), bf16[8,160,128]{2,1,0:T(8,128)(2,1)S(1)}, u32[]{:S(2)}, u32[]{:S(2)}) async-start(bf16[8,160,128]{2,1,0:T(8,128)(2,1)} %bitcast.34), calls=%async_computation.2 | async-start | bytes 655360 | tf_op jit(solution)/shard_map/all_to_all | solution.py:411
  94.0 23.1 %all-to-all-start.3 = ((bf16[8,160,128]{2,1,0:T(8,128)(2,1)}), bf16[8,160,128]{2,1,0:T(8,128)(2,1)S(1)}, u32[]{:S(2)}, u32[]{:S(2)}) async-start(bf16[8,160,128]{2,1,0:T(8,128)(2,1)} %broadcast_in_dim.2), calls=%async_computation.3 | async-start | bytes 655360 | tf_op jit(solution)/shard_map/all_to_all | solution.py:37
  102.4 14.1 %collective-permute-start.13 = (bf16[32,4096]{1,0:T(8,128)(2,1)}, bf16[32,4096]{1,0:T(8,128)(2,1)S(1)}, u32[]{:S(2)}, u32[]{:S(2)}) collective-permute-start(bf16[32,4096]{1,0:T(8,128)(2,1)} %get-tuple-element.81), channel_id=1, source_target_pairs={{0,2},{2,4},{4,6},{6,0},{1,3},{3,5},{5,7},{7,1},{8,10},{10,12},{12... | collective-permute-start | bytes 786440 | tf_op jit(solution)/shard_map/ppermute | solution.py:32
  103.5 13.5 %collective-permute-start.14 = (bf16[32,4096]{1,0:T(8,128)(2,1)}, bf16[32,4096]{1,0:T(8,128)(2,1)S(1)}, u32[]{:S(2)}, u32[]{:S(2)}) collective-permute-start(bf16[32,4096]{1,0:T(8,128)(2,1)} %get-tuple-element.82), channel_id=1, source_target_pairs={{0,4},{2,6},{4,0},{6,2},{1,5},{3,7},{5,1},{7,3},{8,12},{10,14},{12... | collective-permute-start | bytes 786440 | tf_op jit(solution)/shard_map/ppermute | solution.py:32
  105.6 11.4 %collective-permute-start.15 = (bf16[32,4096]{1,0:T(8,128)(2,1)}, bf16[32,4096]{1,0:T(8,128)(2,1)S(1)}, u32[]{:S(2)}, u32[]{:S(2)}) collective-permute-start(bf16[32,4096]{1,0:T(8,128)(2,1)} %get-tuple-element.83), channel_id=1, source_target_pairs={{0,6},{2,0},{4,2},{6,4},{1,7},{3,1},{5,3},{7,5},{8,14},{10,8},{12,... | collective-permute-start | bytes 786440 | tf_op jit(solution)/shard_map/ppermute | solution.py:32
  116.6 2.3 %copy-start.13 = (bf16[32,4096]{1,0:T(8,128)(2,1)}, bf16[32,4096]{1,0:T(8,128)(2,1)S(1)}, u32[]{:S(2)}) copy-start(bf16[32,4096]{1,0:T(8,128)(2,1)S(1)} %collective-permute-done.13.one) | copy-start | bytes 786436
  117.0 1.8 %copy-start.14 = (bf16[32,4096]{1,0:T(8,128)(2,1)}, bf16[32,4096]{1,0:T(8,128)(2,1)S(1)}, u32[]{:S(2)}) copy-start(bf16[32,4096]{1,0:T(8,128)(2,1)S(1)} %collective-permute-done.14.two) | copy-start | bytes 786436
  (3 other events, 3.4 us)

commit v3 on v2

v3 whole, which is shorter than its diff:
```python
import jax
import jax.numpy as jnp
from jax import lax
from jax.experimental import pallas as pl
from jax.experimental.pallas import tpu as pltpu
from jax.sharding import Mesh, PartitionSpec as P

F32 = jnp.float32
BF16 = jnp.bfloat16
DP = ("zl", "x")
TENSOR = ("zh", "y", "c")
SWAP = [(0, 1), (1, 0)]
TURNS = (1, 3, 2)
VMEM = pl.BlockSpec(memory_space=pltpu.VMEM)
ANY = pl.BlockSpec(memory_space=pl.ANY)
MIB = 1 << 20
CHUNKS = 10
HELD = ((0, 0, 0), (0, 1, 0), (1, 0, 1), (1, 1, 1), (2, 0, 3), (2, 1, 3), (3, 0, 2), (4, 0, 2))
SCALE = 100
KEPT = BF16
LEFT = 1
TILE = 2048


def params(mib):
    return pltpu.CompilerParams(vmem_limit_bytes=mib * MIB)


def cost(flops, moved):
    return pl.CostEstimate(flops=flops // SCALE, bytes_accessed=moved // SCALE, transcendentals=0)


def turn(value, by):
    return lax.ppermute(value, "y", [(i, (i + by) % 4) for i in range(4)])


def spread(value, axes, count):
    whole = jnp.broadcast_to(value[None], (count,) + value.shape)
    return lax.all_to_all(whole, axes, 0, 0)


def place_of():
    return lax.axis_index("c"), lax.axis_index("zh"), lax.axis_index("y")


def dot(a, b):
    return jnp.dot(a, b, preferred_element_type=F32)


def dot_nt(a, b):
    return lax.dot_general(a, b, (((1,), (1,)), ((), ())), preferred_element_type=F32)


def pack(cotangent, second, out):
    share, width = cotangent.shape
    block = second.shape[1]
    out[:, :width] = cotangent[...]
    for q in range(second.shape[0] // share):
        out[:, width + q * block : width + (q + 1) * block] = second[q * share : (q + 1) * share, :]


def call_pack(cotangent, second):
    share, width = cotangent.shape
    return pl.pallas_call(
        pack,
        in_specs=[VMEM] * 2,
        out_specs=VMEM,
        out_shape=jax.ShapeDtypeStruct((share, width + second.size // share), BF16),
        compiler_params=params(60),
        name="pack",
        cost_estimate=cost(share, share * width * 4),
    )(cotangent, second)


def base_rows(tokens, weight, other, own, held):
    step = pl.program_id(0)
    share = tokens.shape[0] // 16
    half = tokens.shape[0] // 2

    @pl.when(step == 0)
    def _():
        core, zh, y = place_of()
        for p in range(2):
            for z in range(2):
                for k in range(4):
                    c = 1 - core if p == 0 else core
                    zz = 1 - zh if z == 0 else zh
                    g = zz * 8 + lax.rem(y + (k + 1) % 4, 4) * 2 + c
                    at = p * half + (z * 4 + k) * share
                    held[at : at + share, :] = tokens[pl.ds(pl.multiple_of(g * share, share), share), :]

    total = dot(held[...], weight[...])
    other[...] = total[:half].astype(BF16)
    own[...] = total[half:].astype(own.dtype)


def call_base_rows(tokens, weight, tile=1024):
    rows, hidden = tokens.shape
    width = weight.shape[1]
    half = rows // 2
    return pl.pallas_call(
        base_rows,
        grid=(width // tile,),
        in_specs=[
            pl.BlockSpec((rows, hidden), lambda j: (0, 0)),
            pl.BlockSpec((hidden, tile), lambda j: (0, j)),
        ],
        out_specs=[pl.BlockSpec((half, tile), lambda j: (0, j))] * 2,
        out_shape=[
            jax.ShapeDtypeStruct((half, width), BF16),
            jax.ShapeDtypeStruct((half, width), KEPT),
        ],
        scratch_shapes=[pltpu.VMEM((rows, hidden), BF16)],
        compiler_params=params(60),
        name="base_rows",
        cost_estimate=cost(2 * rows * hidden * width, hidden * width * 2),
    )(tokens, weight)


def pair_sum(own, got, left, right, kept):
    total = own[...].astype(F32) + got[...].astype(F32)
    quarter = kept.shape[0]
    kept[...] = total[quarter:].astype(kept.dtype)
    step = pl.program_id(0)

    @pl.when(step < LEFT)
    def _():
        left[...] = total[:quarter].astype(BF16)

    @pl.when(step >= LEFT)
    def _():
        right[...] = total[:quarter].astype(BF16)


def call_pair_sum(own, got, tile=1024):
    half, width = own.shape
    steps = width // tile
    out = (half // 2, tile)
    *sent, kept = pl.pallas_call(
        pair_sum,
        grid=(steps,),
        in_specs=[pl.BlockSpec((half, tile), lambda j: (0, j))] * 2,
        out_specs=[
            pl.BlockSpec(out, lambda j: (0, jnp.minimum(j, LEFT - 1))),
            pl.BlockSpec(out, lambda j: (0, jnp.maximum(j - LEFT, 0))),
            pl.BlockSpec(out, lambda j: (0, j)),
        ],
        out_shape=[
            jax.ShapeDtypeStruct((half // 2, LEFT * tile), BF16),
            jax.ShapeDtypeStruct((half // 2, width - LEFT * tile), BF16),
            jax.ShapeDtypeStruct((half // 2, width), KEPT),
        ],
        compiler_params=params(12),
        name="pair_sum",
        cost_estimate=cost(half * width, half * width * 6),
    )(own, got)
    return sent, kept


def quad_sum(kept, left, right, one, two, three, own):
    share = own.shape[0]
    cut = left.shape[1]
    for k, out in enumerate((one, two, three, own)):
        rows = slice(k * share, (k + 1) * share)
        out[:, :cut] = (kept[rows, :cut].astype(F32) + left[rows, :].astype(F32)).astype(out.dtype)
        out[:, cut:] = (kept[rows, cut:].astype(F32) + right[rows, :].astype(F32)).astype(out.dtype)


def call_quad_sum(kept, got):
    quarter, width = kept.shape
    share = quarter // 4
    return pl.pallas_call(
        quad_sum,
        in_specs=[VMEM] * 3,
        out_specs=[VMEM] * 4,
        out_shape=[jax.ShapeDtypeStruct((share, width), BF16)] * 3
        + [jax.ShapeDtypeStruct((share, width), F32)],
        compiler_params=params(60),
        name="quad_sum",
        cost_estimate=cost(quarter * width, quarter * width * 8),
    )(kept, *got)


def reorder(order, inner, out, flat):
    count, share, channels = inner.shape
    block = order.shape[1]
    per = channels // block
    tiles = count * per
    for t in range(tiles):
        flat[t] = inner[t // per, :, (t % per) * block : (t % per + 1) * block].astype(F32)

    def one(j):
        wanted = jnp.broadcast_to(order[pl.ds(j, 1), :], (share, block))
        lane = wanted % block
        tile = wanted // block
        total = jnp.zeros((share, block), F32)
        for t in range(tiles):
            found = jnp.take_along_axis(flat[t], lane, axis=1, mode="promise_in_bounds")
            total = jnp.where(tile == t, found, total)
        return total.astype(BF16)

    def group(g, _):
        for i in range(per):
            out[g, :, i * block : (i + 1) * block] = one(g * per + i)
        return 0

    lax.fori_loop(0, count, group, 0)


def call_reorder(order, inner):
    count, share, channels = inner.shape
    tiles, block = order.shape
    return pl.pallas_call(
        reorder,
        in_specs=[VMEM] * 2,
        out_specs=VMEM,
        out_shape=jax.ShapeDtypeStruct(inner.shape, BF16),
        scratch_shapes=[pltpu.VMEM((tiles, share, block), F32)],
        compiler_params=params(6),
        name="reorder",
        cost_estimate=cost(tiles * tiles * share * block * 4, count * share * channels * 4),
    )(order, inner)


def sources():
    core, zh, y = place_of()
    found = []
    for c in range(2):
        for slot, (chunk, row, back) in enumerate(HELD):
            cc = core if c == 0 else 1 - core
            zz = zh if slot % 2 == 0 else 1 - zh
            place = zz * 8 + lax.rem(y + 4 - back, 4) * 2 + cc
            found.append((c * 5 + chunk, row, place))
    return found


def block_of(ref, z, i, share, block, base=0):
    each = block // share
    parts = [
        ref[z * share : (z + 1) * share, base + (i * each + q) * block : base + (i * each + q + 1) * block]
        for q in range(each)
    ]
    return jnp.concatenate(parts, axis=0)


def delta_rows(mixed, *refs):
    chunks, out = refs[:CHUNKS], refs[CHUNKS]
    share = out.shape[0]
    block = mixed.shape[2] // 2
    for chunk, z, g in sources():
        for i in range(2):
            cols = pl.ds(pl.multiple_of((g * 2 + i) * block, block), block)
            factor = block_of(chunks[chunk], z, i, share, block)
            out[:, cols] = dot(mixed[g, :, i * block : (i + 1) * block], factor)


def call_delta_rows(mixed, chunks):
    groups, share, channels = mixed.shape
    width = groups * channels
    per = chunks[0].shape[1] - width
    second = [pl.BlockSpec((v.shape[0], per), lambda j: (0, width // per)) for v in chunks]
    return pl.pallas_call(
        delta_rows,
        grid=(1,),
        in_specs=[pl.BlockSpec(mixed.shape, lambda j: (0, 0, 0))] + second,
        out_specs=pl.BlockSpec((share, width), lambda j: (0, 0)),
        out_shape=jax.ShapeDtypeStruct((share, width), F32),
        compiler_params=params(60),
        name="delta_rows",
        cost_estimate=cost(share * width * channels, share * width * 6),
    )(mixed, *chunks)


def factor_grads(order, mixed, tokens_t, *refs):
    chunks, (d_inner, sums, cot_out, cot, routed, sem) = refs[:CHUNKS], refs[CHUNKS:]
    core, zh, y = place_of()
    block = order.shape[1]
    rows, channels = d_inner.shape
    share = rows // 16
    width = cot.shape[1]
    hidden = tokens_t.shape[0]
    found = sources()
    place = zh * 8 + y * 2 + core
    row = lax.broadcasted_iota(jnp.int32, (channels, block), 0) + place * channels
    for chunk, z, g in found:
        cot[pl.ds(pl.multiple_of(g * share, share), share), :] = chunks[chunk][
            z * share : (z + 1) * share, :width
        ]
        for i in range(2):
            n = g * 2 + i
            hits = jnp.where(row == order[pl.ds(n, 1), :], 1.0, 0.0).astype(BF16)
            factor = block_of(chunks[chunk], z, i, share, block, width)
            cols = pl.ds(pl.multiple_of(n * block, block), block)
            routed[:, cols] = dot(hits, factor).astype(BF16)
    copy = pltpu.make_async_copy(cot, cot_out, sem)
    copy.start()
    grad = dot_nt(cot[...], routed[...]).astype(BF16)
    d_inner[...] = grad
    whole = dot(tokens_t[...], grad)
    unit = lax.broadcasted_iota(jnp.int32, (hidden, block), 0)
    d_first = jnp.where(unit < hidden // 2, whole[:, :block], whole[:, block:]).astype(BF16)
    each = sums.shape[0] // 8
    few = channels // 8
    room = each - few
    for k in range(8):
        have = min(room, hidden - k * room)
        if have < room:
            sums[k * each : k * each + room, :] = jnp.zeros((room, block), BF16)
        sums[k * each : k * each + have, :] = d_first[k * room : k * room + have]
    mixed_t = mixed[...].reshape(rows, channels).T
    for i in range(channels // block):
        n = place * 2 + i
        cols = pl.ds(pl.multiple_of(n * block, block), block)
        d_second = dot(mixed_t[i * block : (i + 1) * block, :], cot[:, cols]).astype(BF16)
        for q in range(block // few):
            k = i * (block // few) + q
            sums[k * each + room : (k + 1) * each, :] = d_second[q * few : (q + 1) * few]
    copy.wait()


def call_factor_grads(order, mixed, tokens_t, chunks, room):
    groups, share, channels = mixed.shape
    rows = groups * share
    tiles, block = order.shape
    width = tiles * block
    each = room + channels // 8
    return pl.pallas_call(
        factor_grads,
        in_specs=[VMEM] * (3 + CHUNKS),
        out_specs=[VMEM, VMEM, ANY],
        out_shape=[
            jax.ShapeDtypeStruct((rows, channels), BF16),
            jax.ShapeDtypeStruct((8 * each, block), BF16),
            jax.ShapeDtypeStruct((rows, width), BF16),
        ],
        scratch_shapes=[
            pltpu.VMEM((rows, width), BF16),
            pltpu.VMEM((channels, width), BF16),
            pltpu.SemaphoreType.DMA,
        ],
        compiler_params=params(60),
        name="factor_grads",
        cost_estimate=cost(4 * rows * channels * width, rows * width * 2),
    )(order, mixed, tokens_t, *chunks)


def token_grads(weight, cot, factor, d_inner, out, weight_held, cot_held, weight_sems, cot_sems):
    steps = weight_sems.shape[0]
    tile = weight.shape[1] // steps
    cols = [slice(k * tile, (k + 1) * tile) for k in range(steps)]
    copies = []
    for k, c in enumerate(cols):
        copies.append(pltpu.make_async_copy(cot.at[:, c], cot_held.at[:, c], cot_sems.at[k]))
        copies.append(pltpu.make_async_copy(weight.at[:, c], weight_held.at[:, c], weight_sems.at[k]))
    for copy in copies:
        copy.start()
    hidden, block = factor.shape
    unit = lax.broadcasted_iota(jnp.int32, (hidden, block), 0)
    zero = jnp.zeros((hidden, block), BF16)
    first = jnp.where(unit < hidden // 2, factor[...], zero)
    second = jnp.where(unit < hidden // 2, zero, factor[...])
    out[...] = dot_nt(jnp.concatenate([first, second], axis=1), d_inner[...])
    for k, c in enumerate(cols):
        copies[2 * k].wait()
        copies[2 * k + 1].wait()
        out[...] += dot_nt(weight_held[:, c], cot_held[:, c])


def call_token_grads(weight, cot, factor, d_inner, tile=1024):
    hidden, width = weight.shape
    rows, channels = d_inner.shape
    return pl.pallas_call(
        token_grads,
        in_specs=[ANY, ANY, VMEM, VMEM],
        out_specs=VMEM,
        out_shape=jax.ShapeDtypeStruct((hidden, rows), F32),
        scratch_shapes=[
            pltpu.VMEM((hidden, width), BF16),
            pltpu.VMEM((rows, width), BF16),
            pltpu.SemaphoreType.DMA((width // tile,)),
            pltpu.SemaphoreType.DMA((width // tile,)),
        ],
        compiler_params=params(60),
        name="token_grads",
        cost_estimate=cost(2 * rows * hidden * width, hidden * width * 2),
    )(weight, cot, factor, d_inner)


def per_device(tokens, base_weight, first_factor, second_factor, channel_order, cotangent):
    rows, hidden = tokens.shape
    blocks, block_in, block_out = first_factor.shape
    width = base_weight.shape[1]
    channels = blocks * block_out
    share = rows // 16
    room = -(-hidden // 128) * 16
    hold = lax.optimization_barrier
    order = channel_order.reshape(-1, block_out)

    bundle = call_pack(cotangent, second_factor.reshape(channels, block_out))
    partner = lax.ppermute(bundle, "zh", SWAP)
    factor = first_factor.reshape(hidden, block_out)
    block = jnp.arange(hidden, dtype=jnp.int32)[:, None] // block_in
    wide = jnp.concatenate([jnp.where(block == n, factor, 0) for n in range(blocks)], axis=1)
    inner = dot(tokens, wide).astype(BF16).reshape(16, share, channels)
    inner = lax.all_to_all(inner, TENSOR, 0, 0)
    other, own = call_base_rows(tokens, base_weight)
    bundle, partner, factor, inner, other, own = hold((bundle, partner, factor, inner, other, own))

    pair = jnp.concatenate([bundle, partner], axis=0)
    next_y, last_y = turn(pair, 1), turn(pair, 3)
    mixed = call_reorder(order, inner)
    sent, kept = call_pair_sum(own, lax.ppermute(other, "c", SWAP))
    left = lax.ppermute(sent[0], "zh", SWAP)
    theirs = [lax.ppermute(pair, "c", SWAP)]
    pair, next_y, last_y, mixed, left, right, kept, theirs = hold(
        (pair, next_y, last_y, mixed, left, sent[1], kept, theirs)
    )

    far = [turn(next_y[:share], 1), turn(last_y[share:], 3)]
    mine = [pair, next_y, last_y]
    theirs = theirs + [lax.ppermute(v, "c", SWAP) for v in mine[1:]]
    right = lax.ppermute(right, "zh", SWAP)
    mixed_mine = lax.all_to_all(mixed, TENSOR, 0, 0)
    far, theirs, left, right, mixed_mine = hold((far, theirs, left, right, mixed_mine))

    chunks = mine + far + theirs + [lax.ppermute(v, "c", SWAP) for v in far]
    d_inner, sums, cot = call_factor_grads(order, mixed_mine, tokens.T, chunks, room)
    sums = lax.all_to_all(sums.reshape(8, -1, block_out), DP, 0, 0)
    terms = call_quad_sum(kept, [left, right])
    delta = call_delta_rows(mixed, chunks)
    terms, sums, cot, delta = hold((terms, sums, cot, delta))

    parts = [turn(terms[d - 1], d) for d in (1, 2, 3)]
    sums = jnp.sum(sums.astype(F32), axis=0).astype(BF16)
    final = spread(sums, DP, 8)
    d_tokens = call_token_grads(base_weight, cot, factor, d_inner).T
    parts, d_tokens = hold((parts, d_tokens))

    output = terms[3] + delta
    for part in parts:
        output = output + part.astype(F32)
    d_first = final[:, :room].reshape(-1, block_out)[:hidden].astype(F32)
    d_second = final[:, room:].astype(F32)
    return (
        output,
        d_tokens,
        d_first.reshape(blocks, block_in, block_out),
        d_second.reshape(blocks, block_out, block_out),
    )


def solution(mesh):
    fine = Mesh(mesh.devices.reshape(2, 4, 2, 4, 2), ("zl", "x", "zh", "y", "c"))
    return jax.shard_map(
        per_device,
        mesh=fine,
        in_specs=(
            P(DP, TENSOR),
            P(TENSOR, None),
            P(TENSOR, None, None),
            P(TENSOR, None, None),
            P(),
            P(DP + TENSOR, None),
        ),
        out_specs=(
            P(DP + TENSOR, None),
            P(DP, TENSOR),
            P(TENSOR, None, None),
            P(TENSOR, None, None),
        ),
        check_vma=False,
    )
```

time: 123 us -> 113 us (0.919)
  Pallas kernels: 44.3 us -> 36.7 us
  waiting for transfers between devices: 13.5 us -> 10.8 us
  blocking collectives: 15.1 us -> 17.1 us
  starting transfers between devices: 35.8 us -> 34.5 us
    ppermute x7, waiting for transfers between devices: 0.48 us -> 6.35 us  [turn(): return lax.ppermute(value, 'y', [(i, (i + by) % 4) for i in range(4)])]
    unnamed x35 -> x52, local copies, waits for them, and re-layouts: 2.94 us -> 7.88 us
    all_to_all x1, waiting for transfers between devices: 6.12 us -> 1.85 us  [per_device(): sums = lax.all_to_all(sums.reshape(8, -1, block_out), DP, 0, 0)]
    ppermute x1, waiting for transfers between devices: 4.05 us -> 0.01 us  [per_device(): partner = lax.ppermute(bundle, 'zh', SWAP)]
    pallas_call x1, Pallas kernels: 5.03 us -> 1.24 us  [call_pair_sum(): pl.pallas_call(pair_sum, grid=(steps,), in_specs=[pl.BlockSpec((half, til...]
    pallas_call x1, Pallas kernels: 6.41 us -> 3.52 us  [call_reorder(): pl.pallas_call(reorder, in_specs=[VMEM] * 2, out_specs=VMEM, out_shape=ja...]
    ppermute x6, waiting for transfers between devices: 0.02 us -> 2.57 us  [the longest x2 1.58 us: per_device(): chunks = mine + far + theirs + [lax.ppermute(v, 'c', SWAP) for v in far]]
    slice x3 -> x2, local copies, waits for them, and re-layouts: 2.24 us -> 0.05 us  [per_device(): far = [turn(next_y[:share], 1), turn(last_y[share:], 3)]]
  transfers between devices with their start and end apart: 19 -> 19, of which waited for: 5 -> 6; matrix products, arithmetic and copies ran while one was open for 6% -> 5% of each run, Pallas kernels for 34% -> 25%
where the time goes in v3:
time: 113 us; the launch traced here: 112 us
  Pallas kernels  36.7 us (32%)
  starting transfers between devices  34.5 us (31%)
  blocking collectives  17.1 us (15%)
  waiting for transfers between devices  10.8 us (10%)
  local copies, waits for them, and re-layouts  9.66 us (9%)
  other arithmetic  1.99 us (2%)
    all_to_all x1, blocking collectives, per_device(): mixed_mine = lax.all_to_all(mixed, TENSOR, 0, 0)  17.1 us
    pallas_call x1, Pallas kernels, call_token_grads(): pl.pallas_call(token_grads, in_specs=[ANY, ANY, VMEM, VMEM], out_specs=VM...  9.06 us
    pallas_call x1, Pallas kernels, call_base_rows(): pl.pallas_call(base_rows, grid=(width // tile,), in_specs=[pl.BlockSpec((...  8.7 us
    ppermute x7, starting transfers between devices, turn(): return lax.ppermute(value, 'y', [(i, (i + by) % 4) for i in range(4)])  8.54 us
    unnamed x52, local copies, waits for them, and re-layouts  7.88 us
    pallas_call x1, Pallas kernels, call_factor_grads(): pl.pallas_call(factor_grads, in_specs=[VMEM] * (3 + CHUNKS), out_specs=[V...  7.11 us
    ppermute x7, waiting for transfers between devices, turn(): return lax.ppermute(value, 'y', [(i, (i + by) % 4) for i in range(4)])  6.35 us
    all_to_all x1, starting transfers between devices, per_device(): sums = lax.all_to_all(sums.reshape(8, -1, block_out), DP, 0, 0)  5.3 us
  transfers between devices with their start and end apart: 19, of which 6 were waited for; matrix products, arithmetic and copies ran while one was open for 5% of the time, Pallas kernels for 25%

profile of v3, /device:TPU:2, one launch (start us, length us, event | category | flops | bytes accessed | tf_op | source)
XLA Modules:
  0.0 112.2 jit_solution(13830895573794037097)
XLA Ops:
  0.6 1.8 %pack.1 = bf16[32,5120]{1,0:T(8,128)(2,1)} custom-call(bf16[32,4096]{1,0:T(8,128)(2,1)} %cotangent.1, bf16[256,128]{1,0:T(8,128)(2,1)} %bitcast.21), custom_call_target="tpu_custom_call" | custom-call | bytes 5242 | tf_op jit(solution)/shard_map/pack/pallas_call | solution.py:64
  2.4 3.9 %collective-permute-start = (bf16[32,5120]{1,0:T(8,128)(2,1)}, bf16[32,5120]{1,0:T(8,128)(2,1)S(1)}, u32[]{:S(2)}, u32[]{:S(2)}) collective-permute-start(bf16[32,5120]{1,0:T(8,128)(2,1)} %pack.1), channel_id=1, source_target_pairs={{0,8},{8,0},{1,9},{9,1},{2,10},{10,2},{3,11},{11,3},{4,12},{12,4},... | collective-permute-start | bytes 983048 | tf_op jit(solution)/shard_map/ppermute | solution.py:400
  6.3 1.0 copy.13
  8.2 0.8 copy.14
  9.0 4.6 %all-to-all-start = ((bf16[16,32,256]{2,1,0:T(8,128)(2,1)}), bf16[16,32,256]{2,1,0:T(8,128)(2,1)S(1)}, u32[]{:S(2)}, u32[]{:S(2)}) async-start(bf16[16,32,256]{2,1,0:T(8,128)(2,1)} %bitcast.2), calls=%async_computation | async-start | bytes 524288 | tf_op jit(solution)/shard_map/all_to_all | solution.py:405
  13.6 1.3 %copy.15.tokens = bf16[512,924]{1,0:T(8,128)(2,1)} copy(bf16[512,924]{0,1:T(8,128)(2,1)S(1)} %copy-done.7) | data formatting | bytes 1892352 | tf_op args[0]
  14.9 8.7 %base_rows.1 = (bf16[256,4096]{1,0:T(8,128)(2,1)}, bf16[256,4096]{1,0:T(8,128)(2,1)}) custom-call(bf16[512,924]{1,0:T(8,128)(2,1)} %copy.15.tokens, bf16[924,4096]{1,0:T(8,128)(2,1)} %weight.3), custom_call_target="tpu_custom_call" | custom-call | flops 38755368 | bytes 75694 | tf_op jit(solution)/shard_map/base_rows/pallas_call | solution.py:101
  24.4 3.1 %collective-permute-start.2 = (bf16[64,5120]{1,0:T(8,128)(2,1)S(1)}, bf16[64,5120]{1,0:T(8,128)(2,1)S(1)}, u32[]{:S(2)}, u32[]{:S(2)}) collective-permute-start(bf16[64,5120]{1,0:T(8,128)(2,1)S(1)} %constant_dynamic-update-slice_fusion.refs_0_), channel_id=1, source_target_pairs={{0,6},{2,0},{4,2},{6,4},{1,7},{3,1},{5,3},{7,5},{8,14},{10,8},{12,... | collective-permute-start | bytes 1966088 | tf_op jit(solution)/shard_map/ppermute | solution.py:34
  27.5 1.0 collective-permute-done.3.got
  28.5 1.6 %copy-done.1 = bf16[256,4096]{1,0:T(8,128)(2,1)S(1)} copy-done((bf16[256,4096]{1,0:T(8,128)(2,1)S(1)}, bf16[256,4096]{1,0:T(8,128)(2,1)}, u32[]{:S(2)}) %copy-start.1) | copy-done | bytes 2097176
  30.1 1.2 %pair_sum.1 = (bf16[128,1024]{1,0:T(8,128)(2,1)S(1)}, bf16[128,3072]{1,0:T(8,128)(2,1)S(1)}, bf16[128,4096]{1,0:T(8,128)(2,1)S(1)}) custom-call(bf16[256,4096]{1,0:T(8,128)(2,1)S(1)} %copy-done.1, bf16[256,4096]{1,0:T(8,128)(2,1)S(1)} %collective-permute-done.3.got), custom_call_target="tpu_custom_call" | custom-call | flops 10485 | bytes 62914 | tf_op jit(solution)/shard_map/pair_sum/pallas_call | solution.py:139
  31.4 1.0 copy-done.2
  32.3 3.0 %collective-permute-start.4 = (bf16[128,1024]{1,0:T(8,128)(2,1)S(1)}, bf16[128,1024]{1,0:T(8,128)(2,1)S(1)}, u32[]{:S(2)}, u32[]{:S(2)}) collective-permute-start(bf16[128,1024]{1,0:T(8,128)(2,1)S(1)} %get-tuple-element.56), channel_id=1, source_target_pairs={{0,8},{8,0},{1,9},{9,1},{2,10},{10,2},{3,11},{11,3},{4,12},{12,4},... | collective-permute-start | bytes 786440 | tf_op jit(solution)/shard_map/ppermute | solution.py:413
  35.3 3.5 %reorder.1.mixed = bf16[16,32,256]{2,1,0:T(8,128)(2,1)S(1)} custom-call(s32[32,128]{1,0:T(8,128)S(1)} %bitcast.15, bf16[16,32,256]{2,1,0:T(8,128)(2,1)S(1)} %all-to-all-done.inner), custom_call_target="tpu_custom_call" | custom-call | flops 167772 | bytes 5242 | tf_op jit(solution)/shard_map/reorder/pallas_call | solution.py:213
  38.9 2.9 %collective-permute-done.2.refs_2_ = bf16[64,5120]{1,0:T(8,128)(2,1)S(1)} collective-permute-done((bf16[64,5120]{1,0:T(8,128)(2,1)S(1)}, bf16[64,5120]{1,0:T(8,128)(2,1)S(1)}, u32[]{:S(2)}, u32[]{:S(2)}) %collective-permute-start.2) | collective-permute-done | bytes 655392 | tf_op jit(solution)/shard_map/ppermute | solution.py:34
  41.8 3.4 %collective-permute-done.1.refs_1_ = bf16[64,5120]{1,0:T(8,128)(2,1)S(1)} collective-permute-done((bf16[64,5120]{1,0:T(8,128)(2,1)S(1)}, bf16[64,5120]{1,0:T(8,128)(2,1)S(1)}, u32[]{:S(2)}, u32[]{:S(2)}) %collective-permute-start.1) | collective-permute-done | bytes 655392 | tf_op jit(solution)/shard_map/ppermute | solution.py:34
  45.2 3.0 %collective-permute-start.10 = (bf16[128,3072]{1,0:T(8,128)(2,1)S(1)}, bf16[128,3072]{1,0:T(8,128)(2,1)S(1)}, u32[]{:S(2)}, u32[]{:S(2)}) collective-permute-start(bf16[128,3072]{1,0:T(8,128)(2,1)S(1)} %get-tuple-element.64), channel_id=1, source_target_pairs={{0,8},{8,0},{1,9},{9,1},{2,10},{10,2},{3,11},{11,3},{4,12},{12,4},... | collective-permute-start | bytes 2359304 | tf_op jit(solution)/shard_map/ppermute | solution.py:422
  49.2 1.7 %collective-permute-start.6 = (bf16[32,5120]{1,0:T(8,128)(2,1)S(1)}, bf16[32,5120]{1,0:T(8,128)(2,1)S(1)}, u32[]{:S(2)}, u32[]{:S(2)}) collective-permute-start(bf16[32,5120]{1,0:T(8,128)(2,1)S(1)} %slice.15), channel_id=1, source_target_pairs={{0,2},{2,4},{4,6},{6,0},{1,3},{3,5},{5,7},{7,1},{8,10},{10,12},{12... | collective-permute-start | bytes 983048 | tf_op jit(solution)/shard_map/ppermute | solution.py:34
  51.0 17.1 %all_to_all.20.mixed = bf16[16,32,256]{2,1,0:T(8,128)(2,1)} all-to-all(bf16[16,32,256]{2,1,0:T(8,128)(2,1)S(1)} %reorder.1.mixed), channel_id=1, replica_groups=mesh['zl'=2,'x'=4,'zh'=2,'y'=4,'c'=2] {'zh','y','c'}, dimensions={0} | all-to-all | bytes 524288 | tf_op jit(solution)/shard_map/all_to_all | solution.py:423
  68.1 0.9 copy-done.10
  69.5 1.1 collective-permute-done.11.refs_8_
  72.1 7.1 %factor_grads.1 = (bf16[512,256]{1,0:T(8,128)(2,1)}, bf16[1280,128]{1,0:T(8,128)(2,1)}, bf16[512,4096]{1,0:T(8,128)(2,1)}) custom-call(s32[32,128]{1,0:T(8,128)} %bitcast.14, bf16[16,32,256]{2,1,0:T(8,128)(2,1)} %all_to_all.20.mixed, bf16[924,512]{1,0:T(8,128)(2,1)} %bitcast.16, bf16[64,5120]{1,0:T(8,128)(2,1)} %copy-done.6, bf16[64,5120]{1,0:T(8,128)(2,1)} %copy-done.5, ...), custom_call_target="tpu_custom_call" | custom-call | flops 21474836 | bytes 41943 | tf_op jit(solution)/shard_map/factor_grads/pallas_call | solution.py:327
  79.3 5.3 %all-to-all-start.2 = ((bf16[8,160,128]{2,1,0:T(8,128)(2,1)}), bf16[8,160,128]{2,1,0:T(8,128)(2,1)S(1)}, u32[]{:S(2)}, u32[]{:S(2)}) async-start(bf16[8,160,128]{2,1,0:T(8,128)(2,1)} %bitcast.19), calls=%async_computation.2 | async-start | bytes 655360 | tf_op jit(solution)/shard_map/all_to_all | solution.py:428
  84.6 2.6 %quad_sum.1 = (bf16[32,4096]{1,0:T(8,128)(2,1)}, bf16[32,4096]{1,0:T(8,128)(2,1)}, bf16[32,4096]{1,0:T(8,128)(2,1)}, f32[32,4096]{1,0:T(8,128)}) custom-call(bf16[128,4096]{1,0:T(8,128)(2,1)} %copy-done.2, bf16[128,1024]{1,0:T(8,128)(2,1)} %copy-done.20, bf16[128,3072]{1,0:T(8,128)(2,1)} %copy-done.18), custom_call_target="tpu_custom_call" | custom-call | flops 5242 | bytes 41943 | tf_op jit(solution)/shard_map/quad_sum/pallas_call | solution.py:172
  87.2 2.6 %delta_rows.1 = f32[32,4096]{1,0:T(8,128)} custom-call(bf16[16,32,256]{2,1,0:T(8,128)(2,1)} %copy-done, bf16[64,5120]{1,0:T(8,128)(2,1)} %copy-done.6, bf16[64,5120]{1,0:T(8,128)(2,1)} %copy-done.5, bf16[64,5120]{1,0:T(8,128)(2,1)} %copy-done.4, bf16[32,5120]{1,0:T(8,128)(2,1)} %copy-done.14, bf16[32,5120]{1,0:T(8,128)(2,1)} %copy-done.13, ...), custom_call_target="tpu_custom_call" | custom-call | flops 335544 | bytes 7864 | tf_op jit(solution)/shard_map/delta_rows/pallas_call | solution.py:262
  89.8 1.8 %all-to-all-done.2 = bf16[8,160,128]{2,1,0:T(8,128)(2,1)S(1)} async-done(((bf16[8,160,128]{2,1,0:T(8,128)(2,1)}), bf16[8,160,128]{2,1,0:T(8,128)(2,1)S(1)}, u32[]{:S(2)}, u32[]{:S(2)}) %all-to-all-start.2) | async-done | bytes 327712 | tf_op jit(solution)/shard_map/all_to_all | solution.py:428
  91.7 2.1 %collective-permute-start.14 = (bf16[32,4096]{1,0:T(8,128)(2,1)S(1)}, bf16[32,4096]{1,0:T(8,128)(2,1)S(1)}, u32[]{:S(2)}, u32[]{:S(2)}) collective-permute-start(bf16[32,4096]{1,0:T(8,128)(2,1)S(1)} %copy-done.22), channel_id=1, source_target_pairs={{0,4},{2,6},{4,0},{6,2},{1,5},{3,7},{5,1},{7,3},{8,12},{10,14},{12... | collective-permute-start | bytes 786440 | tf_op jit(solution)/shard_map/ppermute | solution.py:34
  93.8 1.2 %collective-permute-start.15 = (bf16[32,4096]{1,0:T(8,128)(2,1)S(1)}, bf16[32,4096]{1,0:T(8,128)(2,1)S(1)}, u32[]{:S(2)}, u32[]{:S(2)}) collective-permute-start(bf16[32,4096]{1,0:T(8,128)(2,1)S(1)} %copy-done.21), channel_id=1, source_target_pairs={{0,6},{2,0},{4,2},{6,4},{1,7},{3,1},{5,3},{7,5},{8,14},{10,8},{12,... | collective-permute-start | bytes 786440 | tf_op jit(solution)/shard_map/ppermute | solution.py:34
  95.8 4.5 %all-to-all-start.3 = ((bf16[8,160,128]{2,1,0:T(8,128)(2,1)}), bf16[8,160,128]{2,1,0:T(8,128)(2,1)S(1)}, u32[]{:S(2)}, u32[]{:S(2)}) async-start(bf16[8,160,128]{2,1,0:T(8,128)(2,1)} %broadcast_in_dim.28), calls=%async_computation.3 | async-start | bytes 655360 | tf_op jit(solution)/shard_map/all_to_all | solution.py:39
  100.3 9.1 %token_grads.1 = f32[924,512]{1,0:T(8,128)} custom-call(bf16[924,4096]{1,0:T(8,128)(2,1)} %weight.3, bf16[512,4096]{1,0:T(8,128)(2,1)} %get-tuple-element.86.cot, bf16[924,128]{1,0:T(8,128)(2,1)} %copy-done.11, bf16[512,256]{1,0:T(8,128)(2,1)} %get-tuple-element.88.d_inner), custom_call_target="tpu_custom_call" | custom-call | flops 38755368 | bytes 75694 | tf_op jit(solution)/shard_map/token_grads/pallas_call | solution.py:372
  109.5 0.9 convert_add_fusion
  111.2 1.0 copy.16
  (83 shorter events, 6.2 us)
Async XLA Ops:
  0.6 7.1 %copy-start.7 = (bf16[512,924]{0,1:T(8,128)(2,1)S(1)}, bf16[512,924]{0,1:T(8,128)(2,1)}, u32[]{:S(2)}) copy-start(bf16[512,924]{0,1:T(8,128)(2,1)} %param.6) | copy-start | bytes 2838532
  2.4 21.2 %collective-permute-start = (bf16[32,5120]{1,0:T(8,128)(2,1)}, bf16[32,5120]{1,0:T(8,128)(2,1)S(1)}, u32[]{:S(2)}, u32[]{:S(2)}) collective-permute-start(bf16[32,5120]{1,0:T(8,128)(2,1)} %pack.1), channel_id=1, source_target_pairs={{0,8},{8,0},{1,9},{9,1},{2,10},{10,2},{3,11},{11,3},{4,12},{12,4},... | collective-permute-start | bytes 983048 | tf_op jit(solution)/shard_map/ppermute | solution.py:400
  7.4 7.6 %copy-start.11 = (bf16[924,128]{1,0:T(8,128)(2,1)}, bf16[924,128]{1,0:T(8,128)(2,1)S(1)}, u32[]{:S(2)}) copy-start(bf16[924,128]{1,0:T(8,128)(2,1)S(1)} %reshape.68.factor) | copy-start | bytes 709636
  9.0 14.6 %all-to-all-start = ((bf16[16,32,256]{2,1,0:T(8,128)(2,1)}), bf16[16,32,256]{2,1,0:T(8,128)(2,1)S(1)}, u32[]{:S(2)}, u32[]{:S(2)}) async-start(bf16[16,32,256]{2,1,0:T(8,128)(2,1)} %bitcast.2), calls=%async_computation | async-start | bytes 524288 | tf_op jit(solution)/shard_map/all_to_all | solution.py:405
  14.9 9.2 %copy-start.17 = (bf16[32,5120]{1,0:T(8,128)(2,1)S(1)}, bf16[32,5120]{1,0:T(8,128)(2,1)}, u32[]{:S(2)}) copy-start(bf16[32,5120]{1,0:T(8,128)(2,1)} %pack.1) | copy-start | bytes 983044
  23.6 4.9 %collective-permute-start.3 = (bf16[256,4096]{1,0:T(8,128)(2,1)}, bf16[256,4096]{1,0:T(8,128)(2,1)S(1)}, u32[]{:S(2)}, u32[]{:S(2)}) collective-permute-start(bf16[256,4096]{1,0:T(8,128)(2,1)} %get-tuple-element.55), channel_id=1, source_target_pairs={{0,1},{1,0},{2,3},{3,2},{4,5},{5,4},{6,7},{7,6},{8,9},{9,8},{10,11... | collective-permute-start | bytes 6291464 | tf_op jit(solution)/shard_map/ppermute | solution.py:412
  24.2 11.2 %copy-start.3 = (s32[4096]{0:T(1024)S(1)}, s32[4096]{0:T(1024)}, u32[]{:S(2)}) copy-start(s32[4096]{0:T(1024)} %param.10) | copy-start | bytes 49156
  24.2 8.1 %copy-start.6 = (bf16[64,5120]{1,0:T(8,128)(2,1)}, bf16[64,5120]{1,0:T(8,128)(2,1)S(1)}, u32[]{:S(2)}) copy-start(bf16[64,5120]{1,0:T(8,128)(2,1)S(1)} %constant_dynamic-update-slice_fusion.refs_0_) | copy-start | bytes 1966084
  24.2 14.7 %collective-permute-start.5 = (bf16[64,5120]{1,0:T(8,128)(2,1)S(1)}, bf16[64,5120]{1,0:T(8,128)(2,1)S(1)}, u32[]{:S(2)}, u32[]{:S(2)}) collective-permute-start(bf16[64,5120]{1,0:T(8,128)(2,1)S(1)} %constant_dynamic-update-slice_fusion.refs_0_), channel_id=1, source_target_pairs={{0,1},{1,0},{2,3},{3,2},{4,5},{5,4},{6,7},{7,6},{8,9},{9,8},{10,11... | collective-permute-start | bytes 1966088 | tf_op jit(solution)/shard_map/ppermute | solution.py:414
  24.4 17.4 %collective-permute-start.2 = (bf16[64,5120]{1,0:T(8,128)(2,1)S(1)}, bf16[64,5120]{1,0:T(8,128)(2,1)S(1)}, u32[]{:S(2)}, u32[]{:S(2)}) collective-permute-start(bf16[64,5120]{1,0:T(8,128)(2,1)S(1)} %constant_dynamic-update-slice_fusion.refs_0_), channel_id=1, source_target_pairs={{0,6},{2,0},{4,2},{6,4},{1,7},{3,1},{5,3},{7,5},{8,14},{10,8},{12,... | collective-permute-start | bytes 1966088 | tf_op jit(solution)/shard_map/ppermute | solution.py:34
  27.5 17.7 %collective-permute-start.1 = (bf16[64,5120]{1,0:T(8,128)(2,1)S(1)}, bf16[64,5120]{1,0:T(8,128)(2,1)S(1)}, u32[]{:S(2)}, u32[]{:S(2)}) collective-permute-start(bf16[64,5120]{1,0:T(8,128)(2,1)S(1)} %constant_dynamic-update-slice_fusion.refs_0_), channel_id=1, source_target_pairs={{0,2},{2,4},{4,6},{6,0},{1,3},{3,5},{5,7},{7,1},{8,10},{10,12},{12... | collective-permute-start | bytes 1966088 | tf_op jit(solution)/shard_map/ppermute | solution.py:34
  32.3 12.9 %collective-permute-start.4 = (bf16[128,1024]{1,0:T(8,128)(2,1)S(1)}, bf16[128,1024]{1,0:T(8,128)(2,1)S(1)}, u32[]{:S(2)}, u32[]{:S(2)}) collective-permute-start(bf16[128,1024]{1,0:T(8,128)(2,1)S(1)} %get-tuple-element.56), channel_id=1, source_target_pairs={{0,8},{8,0},{1,9},{9,1},{2,10},{10,2},{3,11},{11,3},{4,12},{12,4},... | collective-permute-start | bytes 786440 | tf_op jit(solution)/shard_map/ppermute | solution.py:413
  38.9 40.4 %copy-start = (bf16[16,32,256]{2,1,0:T(8,128)(2,1)}, bf16[16,32,256]{2,1,0:T(8,128)(2,1)S(1)}, u32[]{:S(2)}) copy-start(bf16[16,32,256]{2,1,0:T(8,128)(2,1)S(1)} %reorder.1.mixed) | copy-start | bytes 786436
  38.9 33.2 %copy-start.8 = (bf16[64,5120]{1,0:T(8,128)(2,1)}, bf16[64,5120]{1,0:T(8,128)(2,1)S(1)}, u32[]{:S(2)}) copy-start(bf16[64,5120]{1,0:T(8,128)(2,1)S(1)} %collective-permute-done.5.refs_5_) | copy-start | bytes 1966084
  41.8 30.3 %copy-start.4 = (bf16[64,5120]{1,0:T(8,128)(2,1)}, bf16[64,5120]{1,0:T(8,128)(2,1)S(1)}, u32[]{:S(2)}) copy-start(bf16[64,5120]{1,0:T(8,128)(2,1)S(1)} %collective-permute-done.2.refs_2_) | copy-start | bytes 1966084
  45.2 26.9 %copy-start.5 = (bf16[64,5120]{1,0:T(8,128)(2,1)}, bf16[64,5120]{1,0:T(8,128)(2,1)S(1)}, u32[]{:S(2)}) copy-start(bf16[64,5120]{1,0:T(8,128)(2,1)S(1)} %collective-permute-done.1.refs_1_) | copy-start | bytes 1966084
  45.2 34.0 %copy-start.20 = (bf16[128,1024]{1,0:T(8,128)(2,1)}, bf16[128,1024]{1,0:T(8,128)(2,1)S(1)}, u32[]{:S(2)}) copy-start(bf16[128,1024]{1,0:T(8,128)(2,1)S(1)} %collective-permute-done.4.left) | copy-start | bytes 786436
  45.2 22.8 %collective-permute-start.10 = (bf16[128,3072]{1,0:T(8,128)(2,1)S(1)}, bf16[128,3072]{1,0:T(8,128)(2,1)S(1)}, u32[]{:S(2)}, u32[]{:S(2)}) collective-permute-start(bf16[128,3072]{1,0:T(8,128)(2,1)S(1)} %get-tuple-element.64), channel_id=1, source_target_pairs={{0,8},{8,0},{1,9},{9,1},{2,10},{10,2},{3,11},{11,3},{4,12},{12,4},... | collective-permute-start | bytes 2359304 | tf_op jit(solution)/shard_map/ppermute | solution.py:422
  48.3 19.7 %collective-permute-start.8 = (bf16[64,5120]{1,0:T(8,128)(2,1)S(1)}, bf16[64,5120]{1,0:T(8,128)(2,1)S(1)}, u32[]{:S(2)}, u32[]{:S(2)}) collective-permute-start(bf16[64,5120]{1,0:T(8,128)(2,1)S(1)} %collective-permute-done.1.refs_1_), channel_id=1, source_target_pairs={{0,1},{1,0},{2,3},{3,2},{4,5},{5,4},{6,7},{7,6},{8,9},{9,8},{10,11... | collective-permute-start | bytes 1966088 | tf_op jit(solution)/shard_map/ppermute | solution.py:421
  48.3 19.8 %collective-permute-start.9 = (bf16[64,5120]{1,0:T(8,128)(2,1)S(1)}, bf16[64,5120]{1,0:T(8,128)(2,1)S(1)}, u32[]{:S(2)}, u32[]{:S(2)}) collective-permute-start(bf16[64,5120]{1,0:T(8,128)(2,1)S(1)} %collective-permute-done.2.refs_2_), channel_id=1, source_target_pairs={{0,1},{1,0},{2,3},{3,2},{4,5},{5,4},{6,7},{7,6},{8,9},{9,8},{10,11... | collective-permute-start | bytes 1966088 | tf_op jit(solution)/shard_map/ppermute | solution.py:421
  48.9 19.2 %collective-permute-start.7 = (bf16[32,5120]{1,0:T(8,128)(2,1)S(1)}, bf16[32,5120]{1,0:T(8,128)(2,1)S(1)}, u32[]{:S(2)}, u32[]{:S(2)}) collective-permute-start(bf16[32,5120]{1,0:T(8,128)(2,1)S(1)} %slice.16), channel_id=1, source_target_pairs={{0,6},{2,0},{4,2},{6,4},{1,7},{3,1},{5,3},{7,5},{8,14},{10,8},{12,... | collective-permute-start | bytes 983048 | tf_op jit(solution)/shard_map/ppermute | solution.py:34
  49.2 18.8 %collective-permute-start.6 = (bf16[32,5120]{1,0:T(8,128)(2,1)S(1)}, bf16[32,5120]{1,0:T(8,128)(2,1)S(1)}, u32[]{:S(2)}, u32[]{:S(2)}) collective-permute-start(bf16[32,5120]{1,0:T(8,128)(2,1)S(1)} %slice.15), channel_id=1, source_target_pairs={{0,2},{2,4},{4,6},{6,0},{1,3},{3,5},{5,7},{7,1},{8,10},{10,12},{12... | collective-permute-start | bytes 983048 | tf_op jit(solution)/shard_map/ppermute | solution.py:34
  69.0 1.6 %collective-permute-start.11 = (bf16[32,5120]{1,0:T(8,128)(2,1)S(1)}, bf16[32,5120]{1,0:T(8,128)(2,1)S(1)}, u32[]{:S(2)}, u32[]{:S(2)}) collective-permute-start(bf16[32,5120]{1,0:T(8,128)(2,1)S(1)} %collective-permute-done.6.refs_3_), channel_id=1, source_target_pairs={{0,1},{1,0},{2,3},{3,2},{4,5},{5,4},{6,7},{7,6},{8,9},{9,8},{10,11... | collective-permute-start | bytes 983048 | tf_op jit(solution)/shard_map/ppermute | solution.py:426
  69.1 2.0 %collective-permute-start.12 = (bf16[32,5120]{1,0:T(8,128)(2,1)S(1)}, bf16[32,5120]{1,0:T(8,128)(2,1)S(1)}, u32[]{:S(2)}, u32[]{:S(2)}) collective-permute-start(bf16[32,5120]{1,0:T(8,128)(2,1)S(1)} %collective-permute-done.7.refs_4_), channel_id=1, source_target_pairs={{0,1},{1,0},{2,3},{3,2},{4,5},{5,4},{6,7},{7,6},{8,9},{9,8},{10,11... | collective-permute-start | bytes 983048 | tf_op jit(solution)/shard_map/ppermute | solution.py:426
  79.3 12.4 %all-to-all-start.2 = ((bf16[8,160,128]{2,1,0:T(8,128)(2,1)}), bf16[8,160,128]{2,1,0:T(8,128)(2,1)S(1)}, u32[]{:S(2)}, u32[]{:S(2)}) async-start(bf16[8,160,128]{2,1,0:T(8,128)(2,1)} %bitcast.19), calls=%async_computation.2 | async-start | bytes 655360 | tf_op jit(solution)/shard_map/all_to_all | solution.py:428
  87.2 6.6 %copy-start.21 = (bf16[32,4096]{1,0:T(8,128)(2,1)S(1)}, bf16[32,4096]{1,0:T(8,128)(2,1)}, u32[]{:S(2)}) copy-start(bf16[32,4096]{1,0:T(8,128)(2,1)} %get-tuple-element.85) | copy-start | bytes 786436
  91.7 17.7 %collective-permute-start.13 = (bf16[32,4096]{1,0:T(8,128)(2,1)S(1)}, bf16[32,4096]{1,0:T(8,128)(2,1)S(1)}, u32[]{:S(2)}, u32[]{:S(2)}) collective-permute-start(bf16[32,4096]{1,0:T(8,128)(2,1)S(1)} %copy-done.23), channel_id=1, source_target_pairs={{0,2},{2,4},{4,6},{6,0},{1,3},{3,5},{5,7},{7,1},{8,10},{10,12},{12... | collective-permute-start | bytes 786440 | tf_op jit(solution)/shard_map/ppermute | solution.py:34
  91.7 17.7 %collective-permute-start.14 = (bf16[32,4096]{1,0:T(8,128)(2,1)S(1)}, bf16[32,4096]{1,0:T(8,128)(2,1)S(1)}, u32[]{:S(2)}, u32[]{:S(2)}) collective-permute-start(bf16[32,4096]{1,0:T(8,128)(2,1)S(1)} %copy-done.22), channel_id=1, source_target_pairs={{0,4},{2,6},{4,0},{6,2},{1,5},{3,7},{5,1},{7,3},{8,12},{10,14},{12... | collective-permute-start | bytes 786440 | tf_op jit(solution)/shard_map/ppermute | solution.py:34
  93.8 15.6 %collective-permute-start.15 = (bf16[32,4096]{1,0:T(8,128)(2,1)S(1)}, bf16[32,4096]{1,0:T(8,128)(2,1)S(1)}, u32[]{:S(2)}, u32[]{:S(2)}) collective-permute-start(bf16[32,4096]{1,0:T(8,128)(2,1)S(1)} %copy-done.21), channel_id=1, source_target_pairs={{0,6},{2,0},{4,2},{6,4},{1,7},{3,1},{5,3},{7,5},{8,14},{10,8},{12,... | collective-permute-start | bytes 786440 | tf_op jit(solution)/shard_map/ppermute | solution.py:34
  95.8 14.6 %all-to-all-start.3 = ((bf16[8,160,128]{2,1,0:T(8,128)(2,1)}), bf16[8,160,128]{2,1,0:T(8,128)(2,1)S(1)}, u32[]{:S(2)}, u32[]{:S(2)}) async-start(bf16[8,160,128]{2,1,0:T(8,128)(2,1)} %broadcast_in_dim.28), calls=%async_computation.3 | async-start | bytes 655360 | tf_op jit(solution)/shard_map/all_to_all | solution.py:39
  100.3 9.1 %copy-start.12 = (f32[32,4096]{1,0:T(8,128)S(1)}, f32[32,4096]{1,0:T(8,128)}, u32[]{:S(2)}) copy-start(f32[32,4096]{1,0:T(8,128)} %delta_rows.1) | copy-start | bytes 1572868
  100.3 9.1 %copy-start.19 = (f32[32,4096]{1,0:T(8,128)S(1)}, f32[32,4096]{1,0:T(8,128)}, u32[]{:S(2)}) copy-start(f32[32,4096]{1,0:T(8,128)} %get-tuple-element.81) | copy-start | bytes 1572868
  (11 other events, 28.3 us)

commit v4 on v3

--- a/solution.py
+++ b/solution.py
@@ -272,7 +272,8 @@
 
 
 def factor_grads(order, mixed, tokens_t, *refs):
-    chunks, (d_inner, sums, cot_out, cot, routed, sem) = refs[:CHUNKS], refs[CHUNKS:]
+    chunks, refs = refs[:CHUNKS], refs[CHUNKS:]
+    d_inner, sums, cot_out, cot, routed, second, sem, cot_sems, second_sems = refs
     core, zh, y = place_of()
     block = order.shape[1]
     rows, channels = d_inner.shape
@@ -281,17 +282,33 @@
     hidden = tokens_t.shape[0]
     found = sources()
     place = zh * 8 + y * 2 + core
+    second_copies, cot_copies = [], []
+    for k, (chunk, z, g) in enumerate(found):
+        held = chunks[chunk].at[z * share : (z + 1) * share, :]
+        rows_of = pl.ds(pl.multiple_of(g * share, share), share)
+        second_copies.append(
+            pltpu.make_async_copy(held.at[:, width:], second.at[k], second_sems.at[k])
+        )
+        cot_copies.append(
+            pltpu.make_async_copy(held.at[:, :width], cot.at[rows_of, :], cot_sems.at[k])
+        )
+    for copy in second_copies + cot_copies:
+        copy.start()
     row = lax.broadcasted_iota(jnp.int32, (channels, block), 0) + place * channels
-    for chunk, z, g in found:
-        cot[pl.ds(pl.multiple_of(g * share, share), share), :] = chunks[chunk][
-            z * share : (z + 1) * share, :width
-        ]
+    each = block // share
+    for k, (chunk, z, g) in enumerate(found):
+        second_copies[k].wait()
         for i in range(2):
             n = g * 2 + i
             hits = jnp.where(row == order[pl.ds(n, 1), :], 1.0, 0.0).astype(BF16)
-            factor = block_of(chunks[chunk], z, i, share, block, width)
+            factor = jnp.concatenate(
+                [second[k, :, q * block : (q + 1) * block] for q in range(i * each, (i + 1) * each)],
+                axis=0,
+            )
             cols = pl.ds(pl.multiple_of(n * block, block), block)
             routed[:, cols] = dot(hits, factor).astype(BF16)
+    for copy in cot_copies:
+        copy.wait()
     copy = pltpu.make_async_copy(cot, cot_out, sem)
     copy.start()
     grad = dot_nt(cot[...], routed[...]).astype(BF16)
@@ -326,7 +343,7 @@
     each = room + channels // 8
     return pl.pallas_call(
         factor_grads,
-        in_specs=[VMEM] * (3 + CHUNKS),
+        in_specs=[VMEM] * 3 + [ANY] * CHUNKS,
         out_specs=[VMEM, VMEM, ANY],
         out_shape=[
             jax.ShapeDtypeStruct((rows, channels), BF16),
@@ -336,7 +353,10 @@
         scratch_shapes=[
             pltpu.VMEM((rows, width), BF16),
             pltpu.VMEM((channels, width), BF16),
+            pltpu.VMEM((16, share, 2 * block * block // share), BF16),
             pltpu.SemaphoreType.DMA,
+            pltpu.SemaphoreType.DMA((16,)),
+            pltpu.SemaphoreType.DMA((16,)),
         ],
         compiler_params=params(60),
         name="factor_grads",
@@ -419,10 +439,10 @@
     far = [turn(next_y[:share], 1), turn(last_y[share:], 3)]
     mine = [pair, next_y, last_y]
     theirs = theirs + [lax.ppermute(v, "c", SWAP) for v in mine[1:]]
-    right = lax.ppermute(right, "zh", SWAP)
     mixed_mine = lax.all_to_all(mixed, TENSOR, 0, 0)
     far, theirs, left, right, mixed_mine = hold((far, theirs, left, right, mixed_mine))
 
+    right = lax.ppermute(right, "zh", SWAP)
     chunks = mine + far + theirs + [lax.ppermute(v, "c", SWAP) for v in far]
     d_inner, sums, cot = call_factor_grads(order, mixed_mine, tokens.T, chunks, room)
     sums = lax.all_to_all(sums.reshape(8, -1, block_out), DP, 0, 0)

time: 113 us -> 108 us (0.956)
  waiting for transfers between devices: 10.8 us -> 7.91 us
  blocking collectives: 17.1 us -> 14.8 us
  Pallas kernels: 36.7 us -> 38.2 us
    ppermute x7, waiting for transfers between devices: 6.35 us -> 3.79 us  [turn(): return lax.ppermute(value, 'y', [(i, (i + by) % 4) for i in range(4)])]
    ppermute x1, starting transfers between devices: 3.05 us -> 0.64 us  [per_device(): right = lax.ppermute(right, 'zh', SWAP)]
    all_to_all x1, blocking collectives: 17.1 us -> 14.8 us  [per_device(): mixed_mine = lax.all_to_all(mixed, TENSOR, 0, 0)]
    ppermute x7, starting transfers between devices: 8.54 us -> 10.4 us  [turn(): return lax.ppermute(value, 'y', [(i, (i + by) % 4) for i in range(4)])]
    pallas_call x1, Pallas kernels: 7.11 us -> 8.69 us  [call_factor_grads(): pl.pallas_call(factor_grads, in_specs=[VMEM] * 3 + [ANY] * CHUNKS, out_sp...]
    unnamed x52 -> x44, local copies, waits for them, and re-layouts: 7.88 us -> 7.31 us
  transfers between devices with their start and end apart: 19 -> 19, of which waited for: 6 -> 7; matrix products, arithmetic and copies ran while one was open for 5% -> 5% of each run, Pallas kernels for 25% -> 34%
where the time goes in v4:
time: 108 us; the launch traced here: 107 us
  Pallas kernels  38.2 us (35%)
  starting transfers between devices  33.9 us (31%)
  blocking collectives  14.8 us (14%)
  local copies, waits for them, and re-layouts  9.1 us (8%)
  waiting for transfers between devices  7.91 us (7%)
  other arithmetic  2 us (2%)
    all_to_all x1, blocking collectives, per_device(): mixed_mine = lax.all_to_all(mixed, TENSOR, 0, 0)  14.8 us
    ppermute x7, starting transfers between devices, turn(): return lax.ppermute(value, 'y', [(i, (i + by) % 4) for i in range(4)])  10.4 us
    pallas_call x1, Pallas kernels, call_token_grads(): pl.pallas_call(token_grads, in_specs=[ANY, ANY, VMEM, VMEM], out_specs=VM...  9.06 us
    pallas_call x1, Pallas kernels, call_base_rows(): pl.pallas_call(base_rows, grid=(width // tile,), in_specs=[pl.BlockSpec((...  8.71 us
    pallas_call x1, Pallas kernels, call_factor_grads(): pl.pallas_call(factor_grads, in_specs=[VMEM] * 3 + [ANY] * CHUNKS, out_sp...  8.69 us
    unnamed x44, local copies, waits for them, and re-layouts  7.31 us
    all_to_all x1, starting transfers between devices, per_device(): sums = lax.all_to_all(sums.reshape(8, -1, block_out), DP, 0, 0)  5.3 us
    all_to_all x1, starting transfers between devices, per_device(): inner = lax.all_to_all(inner, TENSOR, 0, 0)  4.57 us
  transfers between devices with their start and end apart: 19, of which 7 were waited for; matrix products, arithmetic and copies ran while one was open for 5% of the time, Pallas kernels for 34%

profile of v4, /device:TPU:2, one launch (start us, length us, event | category | flops | bytes accessed | tf_op | source)
XLA Modules:
  0.0 107.4 jit_solution(9316238958585499511)
XLA Ops:
  0.6 1.8 %pack.1 = bf16[32,5120]{1,0:T(8,128)(2,1)} custom-call(bf16[32,4096]{1,0:T(8,128)(2,1)} %cotangent.1, bf16[256,128]{1,0:T(8,128)(2,1)} %bitcast.21), custom_call_target="tpu_custom_call" | custom-call | bytes 5242 | tf_op jit(solution)/shard_map/pack/pallas_call | solution.py:64
  2.4 3.9 %collective-permute-start = (bf16[32,5120]{1,0:T(8,128)(2,1)}, bf16[32,5120]{1,0:T(8,128)(2,1)S(1)}, u32[]{:S(2)}, u32[]{:S(2)}) collective-permute-start(bf16[32,5120]{1,0:T(8,128)(2,1)} %pack.1), channel_id=1, source_target_pairs={{0,8},{8,0},{1,9},{9,1},{2,10},{10,2},{3,11},{11,3},{4,12},{12,4},... | collective-permute-start | bytes 983048 | tf_op jit(solution)/shard_map/ppermute | solution.py:420
  6.3 1.0 copy.13
  8.2 0.8 copy.14
  9.0 4.6 %all-to-all-start = ((bf16[16,32,256]{2,1,0:T(8,128)(2,1)}), bf16[16,32,256]{2,1,0:T(8,128)(2,1)S(1)}, u32[]{:S(2)}, u32[]{:S(2)}) async-start(bf16[16,32,256]{2,1,0:T(8,128)(2,1)} %bitcast.2), calls=%async_computation | async-start | bytes 524288 | tf_op jit(solution)/shard_map/all_to_all | solution.py:425
  13.6 1.3 %copy.15.tokens = bf16[512,924]{1,0:T(8,128)(2,1)} copy(bf16[512,924]{0,1:T(8,128)(2,1)S(1)} %copy-done.7) | data formatting | bytes 1892352 | tf_op args[0]
  14.9 8.7 %base_rows.1 = (bf16[256,4096]{1,0:T(8,128)(2,1)}, bf16[256,4096]{1,0:T(8,128)(2,1)}) custom-call(bf16[512,924]{1,0:T(8,128)(2,1)} %copy.15.tokens, bf16[924,4096]{1,0:T(8,128)(2,1)} %weight.3), custom_call_target="tpu_custom_call" | custom-call | flops 38755368 | bytes 75694 | tf_op jit(solution)/shard_map/base_rows/pallas_call | solution.py:101
  24.2 1.7 %collective-permute-start.1 = (bf16[64,5120]{1,0:T(8,128)(2,1)S(1)}, bf16[64,5120]{1,0:T(8,128)(2,1)S(1)}, u32[]{:S(2)}, u32[]{:S(2)}) collective-permute-start(bf16[64,5120]{1,0:T(8,128)(2,1)S(1)} %constant_dynamic-update-slice_fusion.refs_0_), channel_id=1, source_target_pairs={{0,2},{2,4},{4,6},{6,0},{1,3},{3,5},{5,7},{7,1},{8,10},{10,12},{12... | collective-permute-start | bytes 1966088 | tf_op jit(solution)/shard_map/ppermute | solution.py:34
  26.0 1.6 %collective-permute-start.2 = (bf16[64,5120]{1,0:T(8,128)(2,1)S(1)}, bf16[64,5120]{1,0:T(8,128)(2,1)S(1)}, u32[]{:S(2)}, u32[]{:S(2)}) collective-permute-start(bf16[64,5120]{1,0:T(8,128)(2,1)S(1)} %constant_dynamic-update-slice_fusion.refs_0_), channel_id=1, source_target_pairs={{0,6},{2,0},{4,2},{6,4},{1,7},{3,1},{5,3},{7,5},{8,14},{10,8},{12,... | collective-permute-start | bytes 1966088 | tf_op jit(solution)/shard_map/ppermute | solution.py:34
  28.1 1.6 %copy-done.1 = bf16[256,4096]{1,0:T(8,128)(2,1)S(1)} copy-done((bf16[256,4096]{1,0:T(8,128)(2,1)S(1)}, bf16[256,4096]{1,0:T(8,128)(2,1)}, u32[]{:S(2)}) %copy-start.1) | copy-done | bytes 2097176
  29.7 1.2 %pair_sum.1 = (bf16[128,1024]{1,0:T(8,128)(2,1)S(1)}, bf16[128,3072]{1,0:T(8,128)(2,1)S(1)}, bf16[128,4096]{1,0:T(8,128)(2,1)S(1)}) custom-call(bf16[256,4096]{1,0:T(8,128)(2,1)S(1)} %copy-done.1, bf16[256,4096]{1,0:T(8,128)(2,1)S(1)} %collective-permute-done.3.got), custom_call_target="tpu_custom_call" | custom-call | flops 10485 | bytes 62914 | tf_op jit(solution)/shard_map/pair_sum/pallas_call | solution.py:139
  31.0 1.0 copy-done.2
  31.9 3.4 %collective-permute-start.4 = (bf16[128,1024]{1,0:T(8,128)(2,1)S(1)}, bf16[128,1024]{1,0:T(8,128)(2,1)S(1)}, u32[]{:S(2)}, u32[]{:S(2)}) collective-permute-start(bf16[128,1024]{1,0:T(8,128)(2,1)S(1)} %get-tuple-element.56), channel_id=1, source_target_pairs={{0,8},{8,0},{1,9},{9,1},{2,10},{10,2},{3,11},{11,3},{4,12},{12,4},... | collective-permute-start | bytes 786440 | tf_op jit(solution)/shard_map/ppermute | solution.py:433
  35.3 3.5 %reorder.1.mixed = bf16[16,32,256]{2,1,0:T(8,128)(2,1)S(1)} custom-call(s32[32,128]{1,0:T(8,128)S(1)} %bitcast.15, bf16[16,32,256]{2,1,0:T(8,128)(2,1)S(1)} %all-to-all-done.inner), custom_call_target="tpu_custom_call" | custom-call | flops 167772 | bytes 5242 | tf_op jit(solution)/shard_map/reorder/pallas_call | solution.py:213
  38.9 3.5 %collective-permute-done.1.refs_1_ = bf16[64,5120]{1,0:T(8,128)(2,1)S(1)} collective-permute-done((bf16[64,5120]{1,0:T(8,128)(2,1)S(1)}, bf16[64,5120]{1,0:T(8,128)(2,1)S(1)}, u32[]{:S(2)}, u32[]{:S(2)}) %collective-permute-start.1) | collective-permute-done | bytes 655392 | tf_op jit(solution)/shard_map/ppermute | solution.py:34
  43.3 1.5 %collective-permute-start.6 = (bf16[32,5120]{1,0:T(8,128)(2,1)S(1)}, bf16[32,5120]{1,0:T(8,128)(2,1)S(1)}, u32[]{:S(2)}, u32[]{:S(2)}) collective-permute-start(bf16[32,5120]{1,0:T(8,128)(2,1)S(1)} %slice.15), channel_id=1, source_target_pairs={{0,2},{2,4},{4,6},{6,0},{1,3},{3,5},{5,7},{7,1},{8,10},{10,12},{12... | collective-permute-start | bytes 983048 | tf_op jit(solution)/shard_map/ppermute | solution.py:34
  44.9 1.8 %collective-permute-start.7 = (bf16[32,5120]{1,0:T(8,128)(2,1)S(1)}, bf16[32,5120]{1,0:T(8,128)(2,1)S(1)}, u32[]{:S(2)}, u32[]{:S(2)}) collective-permute-start(bf16[32,5120]{1,0:T(8,128)(2,1)S(1)} %slice.16), channel_id=1, source_target_pairs={{0,6},{2,0},{4,2},{6,4},{1,7},{3,1},{5,3},{7,5},{8,14},{10,8},{12,... | collective-permute-start | bytes 983048 | tf_op jit(solution)/shard_map/ppermute | solution.py:34
  46.6 14.8 %all_to_all.20.mixed = bf16[16,32,256]{2,1,0:T(8,128)(2,1)} all-to-all(bf16[16,32,256]{2,1,0:T(8,128)(2,1)S(1)} %reorder.1.mixed), channel_id=1, replica_groups=mesh['zl'=2,'x'=4,'zh'=2,'y'=4,'c'=2] {'zh','y','c'}, dimensions={0} | all-to-all | bytes 524288 | tf_op jit(solution)/shard_map/all_to_all | solution.py:442
  62.7 1.1 %collective-permute-done.11.refs_8_ = bf16[32,5120]{1,0:T(8,128)(2,1)S(1)} collective-permute-done((bf16[32,5120]{1,0:T(8,128)(2,1)S(1)}, bf16[32,5120]{1,0:T(8,128)(2,1)S(1)}, u32[]{:S(2)}, u32[]{:S(2)}) %collective-permute-start.11) | collective-permute-done | bytes 327712 | tf_op jit(solution)/shard_map/ppermute | solution.py:446
  64.6 0.7 copy-done.16
  65.3 8.7 %factor_grads.1 = (bf16[512,256]{1,0:T(8,128)(2,1)}, bf16[1280,128]{1,0:T(8,128)(2,1)}, bf16[512,4096]{1,0:T(8,128)(2,1)}) custom-call(s32[32,128]{1,0:T(8,128)} %bitcast.14, bf16[16,32,256]{2,1,0:T(8,128)(2,1)} %all_to_all.20.mixed, bf16[924,512]{1,0:T(8,128)(2,1)} %bitcast.16, bf16[64,5120]{1,0:T(8,128)(2,1)} %copy-done.6, bf16[64,5120]{1,0:T(8,128)(2,1)} %copy-done.4, ...), custom_call_target="tpu_custom_call" | custom-call | flops 21474836 | bytes 41943 | tf_op jit(solution)/shard_map/factor_grads/pallas_call | solution.py:344
  74.0 5.3 %all-to-all-start.2 = ((bf16[8,160,128]{2,1,0:T(8,128)(2,1)}), bf16[8,160,128]{2,1,0:T(8,128)(2,1)S(1)}, u32[]{:S(2)}, u32[]{:S(2)}) async-start(bf16[8,160,128]{2,1,0:T(8,128)(2,1)} %bitcast.19), calls=%async_computation.2 | async-start | bytes 655360 | tf_op jit(solution)/shard_map/all_to_all | solution.py:448
  79.3 2.5 %delta_rows.1 = f32[32,4096]{1,0:T(8,128)} custom-call(bf16[16,32,256]{2,1,0:T(8,128)(2,1)} %copy-done, bf16[64,5120]{1,0:T(8,128)(2,1)} %copy-done.6, bf16[64,5120]{1,0:T(8,128)(2,1)} %copy-done.4, bf16[64,5120]{1,0:T(8,128)(2,1)} %copy-done.5, bf16[32,5120]{1,0:T(8,128)(2,1)} %copy-done.13, bf16[32,5120]{1,0:T(8,128)(2,1)} %copy-done.14, ...), custom_call_target="tpu_custom_call" | custom-call | flops 335544 | bytes 7864 | tf_op jit(solution)/shard_map/delta_rows/pallas_call | solution.py:262
  82.4 2.6 %quad_sum.1 = (bf16[32,4096]{1,0:T(8,128)(2,1)}, bf16[32,4096]{1,0:T(8,128)(2,1)}, bf16[32,4096]{1,0:T(8,128)(2,1)}, f32[32,4096]{1,0:T(8,128)}) custom-call(bf16[128,4096]{1,0:T(8,128)(2,1)} %copy-done.2, bf16[128,1024]{1,0:T(8,128)(2,1)} %copy-done.19, bf16[128,3072]{1,0:T(8,128)(2,1)} %collective-permute-done.10.right), custom_call_target="tpu_custom_call" | custom-call | flops 5242 | bytes 41943 | tf_op jit(solution)/shard_map/quad_sum/pallas_call | solution.py:172
  85.0 1.4 %all-to-all-done.2 = bf16[8,160,128]{2,1,0:T(8,128)(2,1)S(1)} async-done(((bf16[8,160,128]{2,1,0:T(8,128)(2,1)}), bf16[8,160,128]{2,1,0:T(8,128)(2,1)S(1)}, u32[]{:S(2)}, u32[]{:S(2)}) %all-to-all-start.2) | async-done | bytes 327712 | tf_op jit(solution)/shard_map/all_to_all | solution.py:448
  86.7 2.2 %collective-permute-start.14 = (bf16[32,4096]{1,0:T(8,128)(2,1)}, bf16[32,4096]{1,0:T(8,128)(2,1)S(1)}, u32[]{:S(2)}, u32[]{:S(2)}) collective-permute-start(bf16[32,4096]{1,0:T(8,128)(2,1)} %get-tuple-element.84), channel_id=1, source_target_pairs={{0,4},{2,6},{4,0},{6,2},{1,5},{3,7},{5,1},{7,3},{8,12},{10,14},{12... | collective-permute-start | bytes 786440 | tf_op jit(solution)/shard_map/ppermute | solution.py:34
  88.9 1.3 %collective-permute-start.15 = (bf16[32,4096]{1,0:T(8,128)(2,1)}, bf16[32,4096]{1,0:T(8,128)(2,1)S(1)}, u32[]{:S(2)}, u32[]{:S(2)}) collective-permute-start(bf16[32,4096]{1,0:T(8,128)(2,1)} %get-tuple-element.85), channel_id=1, source_target_pairs={{0,6},{2,0},{4,2},{6,4},{1,7},{3,1},{5,3},{7,5},{8,14},{10,8},{12,... | collective-permute-start | bytes 786440 | tf_op jit(solution)/shard_map/ppermute | solution.py:34
  90.3 0.8 broadcast_in_dim.28
  91.0 4.5 %all-to-all-start.3 = ((bf16[8,160,128]{2,1,0:T(8,128)(2,1)}), bf16[8,160,128]{2,1,0:T(8,128)(2,1)S(1)}, u32[]{:S(2)}, u32[]{:S(2)}) async-start(bf16[8,160,128]{2,1,0:T(8,128)(2,1)} %broadcast_in_dim.28), calls=%async_computation.3 | async-start | bytes 655360 | tf_op jit(solution)/shard_map/all_to_all | solution.py:39
  95.5 9.1 %token_grads.1 = f32[924,512]{1,0:T(8,128)} custom-call(bf16[924,4096]{1,0:T(8,128)(2,1)} %weight.3, bf16[512,4096]{1,0:T(8,128)(2,1)} %get-tuple-element.86.cot, bf16[924,128]{1,0:T(8,128)(2,1)} %copy-done.11, bf16[512,256]{1,0:T(8,128)(2,1)} %get-tuple-element.88.d_inner), custom_call_target="tpu_custom_call" | custom-call | flops 38755368 | bytes 75694 | tf_op jit(solution)/shard_map/token_grads/pallas_call | solution.py:392
  104.7 0.9 convert_add_fusion
  105.7 1.0 copy.16
  (75 shorter events, 6.5 us)
Async XLA Ops:
  0.6 7.1 %copy-start.7 = (bf16[512,924]{0,1:T(8,128)(2,1)S(1)}, bf16[512,924]{0,1:T(8,128)(2,1)}, u32[]{:S(2)}) copy-start(bf16[512,924]{0,1:T(8,128)(2,1)} %param.6) | copy-start | bytes 2838532
  2.4 21.2 %collective-permute-start = (bf16[32,5120]{1,0:T(8,128)(2,1)}, bf16[32,5120]{1,0:T(8,128)(2,1)S(1)}, u32[]{:S(2)}, u32[]{:S(2)}) collective-permute-start(bf16[32,5120]{1,0:T(8,128)(2,1)} %pack.1), channel_id=1, source_target_pairs={{0,8},{8,0},{1,9},{9,1},{2,10},{10,2},{3,11},{11,3},{4,12},{12,4},... | collective-permute-start | bytes 983048 | tf_op jit(solution)/shard_map/ppermute | solution.py:420
  7.4 7.6 %copy-start.11 = (bf16[924,128]{1,0:T(8,128)(2,1)}, bf16[924,128]{1,0:T(8,128)(2,1)S(1)}, u32[]{:S(2)}) copy-start(bf16[924,128]{1,0:T(8,128)(2,1)S(1)} %reshape.68.factor) | copy-start | bytes 709636
  9.0 14.6 %all-to-all-start = ((bf16[16,32,256]{2,1,0:T(8,128)(2,1)}), bf16[16,32,256]{2,1,0:T(8,128)(2,1)S(1)}, u32[]{:S(2)}, u32[]{:S(2)}) async-start(bf16[16,32,256]{2,1,0:T(8,128)(2,1)} %bitcast.2), calls=%async_computation | async-start | bytes 524288 | tf_op jit(solution)/shard_map/all_to_all | solution.py:425
  14.9 9.2 %copy-start.17 = (bf16[32,5120]{1,0:T(8,128)(2,1)S(1)}, bf16[32,5120]{1,0:T(8,128)(2,1)}, u32[]{:S(2)}) copy-start(bf16[32,5120]{1,0:T(8,128)(2,1)} %pack.1) | copy-start | bytes 983044
  23.6 4.5 %collective-permute-start.3 = (bf16[256,4096]{1,0:T(8,128)(2,1)}, bf16[256,4096]{1,0:T(8,128)(2,1)S(1)}, u32[]{:S(2)}, u32[]{:S(2)}) collective-permute-start(bf16[256,4096]{1,0:T(8,128)(2,1)} %get-tuple-element.55), channel_id=1, source_target_pairs={{0,1},{1,0},{2,3},{3,2},{4,5},{5,4},{6,7},{7,6},{8,9},{9,8},{10,11... | collective-permute-start | bytes 6291464 | tf_op jit(solution)/shard_map/ppermute | solution.py:432
  24.2 11.2 %copy-start.3 = (s32[4096]{0:T(1024)S(1)}, s32[4096]{0:T(1024)}, u32[]{:S(2)}) copy-start(s32[4096]{0:T(1024)} %param.10) | copy-start | bytes 49156
  24.2 7.7 %copy-start.6 = (bf16[64,5120]{1,0:T(8,128)(2,1)}, bf16[64,5120]{1,0:T(8,128)(2,1)S(1)}, u32[]{:S(2)}) copy-start(bf16[64,5120]{1,0:T(8,128)(2,1)S(1)} %constant_dynamic-update-slice_fusion.refs_0_) | copy-start | bytes 1966084
  24.2 18.2 %collective-permute-start.1 = (bf16[64,5120]{1,0:T(8,128)(2,1)S(1)}, bf16[64,5120]{1,0:T(8,128)(2,1)S(1)}, u32[]{:S(2)}, u32[]{:S(2)}) collective-permute-start(bf16[64,5120]{1,0:T(8,128)(2,1)S(1)} %constant_dynamic-update-slice_fusion.refs_0_), channel_id=1, source_target_pairs={{0,2},{2,4},{4,6},{6,0},{1,3},{3,5},{5,7},{7,1},{8,10},{10,12},{12... | collective-permute-start | bytes 1966088 | tf_op jit(solution)/shard_map/ppermute | solution.py:34
  26.0 16.7 %collective-permute-start.2 = (bf16[64,5120]{1,0:T(8,128)(2,1)S(1)}, bf16[64,5120]{1,0:T(8,128)(2,1)S(1)}, u32[]{:S(2)}, u32[]{:S(2)}) collective-permute-start(bf16[64,5120]{1,0:T(8,128)(2,1)S(1)} %constant_dynamic-update-slice_fusion.refs_0_), channel_id=1, source_target_pairs={{0,6},{2,0},{4,2},{6,4},{1,7},{3,1},{5,3},{7,5},{8,14},{10,8},{12,... | collective-permute-start | bytes 1966088 | tf_op jit(solution)/shard_map/ppermute | solution.py:34
  27.5 15.1 %collective-permute-start.5 = (bf16[64,5120]{1,0:T(8,128)(2,1)S(1)}, bf16[64,5120]{1,0:T(8,128)(2,1)S(1)}, u32[]{:S(2)}, u32[]{:S(2)}) collective-permute-start(bf16[64,5120]{1,0:T(8,128)(2,1)S(1)} %constant_dynamic-update-slice_fusion.refs_0_), channel_id=1, source_target_pairs={{0,1},{1,0},{2,3},{3,2},{4,5},{5,4},{6,7},{7,6},{8,9},{9,8},{10,11... | collective-permute-start | bytes 1966088 | tf_op jit(solution)/shard_map/ppermute | solution.py:434
  31.9 10.7 %collective-permute-start.4 = (bf16[128,1024]{1,0:T(8,128)(2,1)S(1)}, bf16[128,1024]{1,0:T(8,128)(2,1)S(1)}, u32[]{:S(2)}, u32[]{:S(2)}) collective-permute-start(bf16[128,1024]{1,0:T(8,128)(2,1)S(1)} %get-tuple-element.56), channel_id=1, source_target_pairs={{0,8},{8,0},{1,9},{9,1},{2,10},{10,2},{3,11},{11,3},{4,12},{12,4},... | collective-permute-start | bytes 786440 | tf_op jit(solution)/shard_map/ppermute | solution.py:433
  38.9 35.1 %copy-start = (bf16[16,32,256]{2,1,0:T(8,128)(2,1)}, bf16[16,32,256]{2,1,0:T(8,128)(2,1)S(1)}, u32[]{:S(2)}) copy-start(bf16[16,32,256]{2,1,0:T(8,128)(2,1)S(1)} %reorder.1.mixed) | copy-start | bytes 786436
  42.4 22.9 %copy-start.4 = (bf16[64,5120]{1,0:T(8,128)(2,1)}, bf16[64,5120]{1,0:T(8,128)(2,1)S(1)}, u32[]{:S(2)}) copy-start(bf16[64,5120]{1,0:T(8,128)(2,1)S(1)} %collective-permute-done.1.refs_1_) | copy-start | bytes 1966084
  42.7 22.6 %copy-start.5 = (bf16[64,5120]{1,0:T(8,128)(2,1)}, bf16[64,5120]{1,0:T(8,128)(2,1)S(1)}, u32[]{:S(2)}) copy-start(bf16[64,5120]{1,0:T(8,128)(2,1)S(1)} %collective-permute-done.2.refs_2_) | copy-start | bytes 1966084
  42.7 19.5 %copy-start.8 = (bf16[64,5120]{1,0:T(8,128)(2,1)}, bf16[64,5120]{1,0:T(8,128)(2,1)S(1)}, u32[]{:S(2)}) copy-start(bf16[64,5120]{1,0:T(8,128)(2,1)S(1)} %collective-permute-done.5.refs_5_) | copy-start | bytes 1966084
  42.7 31.3 %copy-start.19 = (bf16[128,1024]{1,0:T(8,128)(2,1)}, bf16[128,1024]{1,0:T(8,128)(2,1)S(1)}, u32[]{:S(2)}) copy-start(bf16[128,1024]{1,0:T(8,128)(2,1)S(1)} %collective-permute-done.4.left) | copy-start | bytes 786436
  42.7 18.8 %collective-permute-start.8 = (bf16[64,5120]{1,0:T(8,128)(2,1)S(1)}, bf16[64,5120]{1,0:T(8,128)(2,1)S(1)}, u32[]{:S(2)}, u32[]{:S(2)}) collective-permute-start(bf16[64,5120]{1,0:T(8,128)(2,1)S(1)} %collective-permute-done.1.refs_1_), channel_id=1, source_target_pairs={{0,1},{1,0},{2,3},{3,2},{4,5},{5,4},{6,7},{7,6},{8,9},{9,8},{10,11... | collective-permute-start | bytes 1966088 | tf_op jit(solution)/shard_map/ppermute | solution.py:441
  42.8 18.7 %collective-permute-start.9 = (bf16[64,5120]{1,0:T(8,128)(2,1)S(1)}, bf16[64,5120]{1,0:T(8,128)(2,1)S(1)}, u32[]{:S(2)}, u32[]{:S(2)}) collective-permute-start(bf16[64,5120]{1,0:T(8,128)(2,1)S(1)} %collective-permute-done.2.refs_2_), channel_id=1, source_target_pairs={{0,1},{1,0},{2,3},{3,2},{4,5},{5,4},{6,7},{7,6},{8,9},{9,8},{10,11... | collective-permute-start | bytes 1966088 | tf_op jit(solution)/shard_map/ppermute | solution.py:441
  43.3 18.1 %collective-permute-start.6 = (bf16[32,5120]{1,0:T(8,128)(2,1)S(1)}, bf16[32,5120]{1,0:T(8,128)(2,1)S(1)}, u32[]{:S(2)}, u32[]{:S(2)}) collective-permute-start(bf16[32,5120]{1,0:T(8,128)(2,1)S(1)} %slice.15), channel_id=1, source_target_pairs={{0,2},{2,4},{4,6},{6,0},{1,3},{3,5},{5,7},{7,1},{8,10},{10,12},{12... | collective-permute-start | bytes 983048 | tf_op jit(solution)/shard_map/ppermute | solution.py:34
  44.9 16.6 %collective-permute-start.7 = (bf16[32,5120]{1,0:T(8,128)(2,1)S(1)}, bf16[32,5120]{1,0:T(8,128)(2,1)S(1)}, u32[]{:S(2)}, u32[]{:S(2)}) collective-permute-start(bf16[32,5120]{1,0:T(8,128)(2,1)S(1)} %slice.16), channel_id=1, source_target_pairs={{0,6},{2,0},{4,2},{6,4},{1,7},{3,1},{5,3},{7,5},{8,14},{10,8},{12,... | collective-permute-start | bytes 983048 | tf_op jit(solution)/shard_map/ppermute | solution.py:34
  61.5 3.8 %copy-start.13 = (bf16[32,5120]{1,0:T(8,128)(2,1)}, bf16[32,5120]{1,0:T(8,128)(2,1)S(1)}, u32[]{:S(2)}) copy-start(bf16[32,5120]{1,0:T(8,128)(2,1)S(1)} %collective-permute-done.6.refs_3_) | copy-start | bytes 983044
  61.5 20.8 %collective-permute-start.10 = (bf16[128,3072]{1,0:T(8,128)(2,1)S(1)}, bf16[128,3072]{1,0:T(8,128)(2,1)}, u32[]{:S(2)}, u32[]{:S(2)}) collective-permute-start(bf16[128,3072]{1,0:T(8,128)(2,1)S(1)} %get-tuple-element.67), channel_id=1, source_target_pairs={{0,8},{8,0},{1,9},{9,1},{2,10},{10,2},{3,11},{11,3},{4,12},{12,4},... | collective-permute-start | bytes 2359304 | tf_op jit(solution)/shard_map/ppermute | solution.py:445
  62.2 1.6 %collective-permute-start.11 = (bf16[32,5120]{1,0:T(8,128)(2,1)S(1)}, bf16[32,5120]{1,0:T(8,128)(2,1)S(1)}, u32[]{:S(2)}, u32[]{:S(2)}) collective-permute-start(bf16[32,5120]{1,0:T(8,128)(2,1)S(1)} %collective-permute-done.6.refs_3_), channel_id=1, source_target_pairs={{0,1},{1,0},{2,3},{3,2},{4,5},{5,4},{6,7},{7,6},{8,9},{9,8},{10,11... | collective-permute-start | bytes 983048 | tf_op jit(solution)/shard_map/ppermute | solution.py:446
  62.5 1.7 %collective-permute-start.12 = (bf16[32,5120]{1,0:T(8,128)(2,1)S(1)}, bf16[32,5120]{1,0:T(8,128)(2,1)S(1)}, u32[]{:S(2)}, u32[]{:S(2)}) collective-permute-start(bf16[32,5120]{1,0:T(8,128)(2,1)S(1)} %collective-permute-done.7.refs_4_), channel_id=1, source_target_pairs={{0,1},{1,0},{2,3},{3,2},{4,5},{5,4},{6,7},{7,6},{8,9},{9,8},{10,11... | collective-permute-start | bytes 983048 | tf_op jit(solution)/shard_map/ppermute | solution.py:446
  74.0 12.4 %all-to-all-start.2 = ((bf16[8,160,128]{2,1,0:T(8,128)(2,1)}), bf16[8,160,128]{2,1,0:T(8,128)(2,1)S(1)}, u32[]{:S(2)}, u32[]{:S(2)}) async-start(bf16[8,160,128]{2,1,0:T(8,128)(2,1)} %bitcast.19), calls=%async_computation.2 | async-start | bytes 655360 | tf_op jit(solution)/shard_map/all_to_all | solution.py:448
  86.4 18.2 %collective-permute-start.13 = (bf16[32,4096]{1,0:T(8,128)(2,1)}, bf16[32,4096]{1,0:T(8,128)(2,1)S(1)}, u32[]{:S(2)}, u32[]{:S(2)}) collective-permute-start(bf16[32,4096]{1,0:T(8,128)(2,1)} %get-tuple-element.83), channel_id=1, source_target_pairs={{0,2},{2,4},{4,6},{6,0},{1,3},{3,5},{5,7},{7,1},{8,10},{10,12},{12... | collective-permute-start | bytes 786440 | tf_op jit(solution)/shard_map/ppermute | solution.py:34
  86.7 17.9 %collective-permute-start.14 = (bf16[32,4096]{1,0:T(8,128)(2,1)}, bf16[32,4096]{1,0:T(8,128)(2,1)S(1)}, u32[]{:S(2)}, u32[]{:S(2)}) collective-permute-start(bf16[32,4096]{1,0:T(8,128)(2,1)} %get-tuple-element.84), channel_id=1, source_target_pairs={{0,4},{2,6},{4,0},{6,2},{1,5},{3,7},{5,1},{7,3},{8,12},{10,14},{12... | collective-permute-start | bytes 786440 | tf_op jit(solution)/shard_map/ppermute | solution.py:34
  88.9 15.7 %collective-permute-start.15 = (bf16[32,4096]{1,0:T(8,128)(2,1)}, bf16[32,4096]{1,0:T(8,128)(2,1)S(1)}, u32[]{:S(2)}, u32[]{:S(2)}) collective-permute-start(bf16[32,4096]{1,0:T(8,128)(2,1)} %get-tuple-element.85), channel_id=1, source_target_pairs={{0,6},{2,0},{4,2},{6,4},{1,7},{3,1},{5,3},{7,5},{8,14},{10,8},{12,... | collective-permute-start | bytes 786440 | tf_op jit(solution)/shard_map/ppermute | solution.py:34
  91.0 14.5 %all-to-all-start.3 = ((bf16[8,160,128]{2,1,0:T(8,128)(2,1)}), bf16[8,160,128]{2,1,0:T(8,128)(2,1)S(1)}, u32[]{:S(2)}, u32[]{:S(2)}) async-start(bf16[8,160,128]{2,1,0:T(8,128)(2,1)} %broadcast_in_dim.28), calls=%async_computation.3 | async-start | bytes 655360 | tf_op jit(solution)/shard_map/all_to_all | solution.py:39
  95.5 9.1 %copy-start.12 = (f32[32,4096]{1,0:T(8,128)S(1)}, f32[32,4096]{1,0:T(8,128)}, u32[]{:S(2)}) copy-start(f32[32,4096]{1,0:T(8,128)} %delta_rows.1) | copy-start | bytes 1572868
  95.5 9.1 %copy-start.18 = (f32[32,4096]{1,0:T(8,128)S(1)}, f32[32,4096]{1,0:T(8,128)}, u32[]{:S(2)}) copy-start(f32[32,4096]{1,0:T(8,128)} %get-tuple-element.81) | copy-start | bytes 1572868
  (7 other events, 11.2 us)

commit v5 on v3

--- a/solution.py
+++ b/solution.py
@@ -18,7 +18,7 @@
 HELD = ((0, 0, 0), (0, 1, 0), (1, 0, 1), (1, 1, 1), (2, 0, 3), (2, 1, 3), (3, 0, 2), (4, 0, 2))
 SCALE = 100
 KEPT = BF16
-LEFT = 1
+LEFT = 2
 TILE = 2048
 
 
@@ -338,48 +338,44 @@
             pltpu.VMEM((channels, width), BF16),
             pltpu.SemaphoreType.DMA,
         ],
-        compiler_params=params(60),
+        compiler_params=params(26),
         name="factor_grads",
         cost_estimate=cost(4 * rows * channels * width, rows * width * 2),
     )(order, mixed, tokens_t, *chunks)
 
 
-def token_grads(weight, cot, factor, d_inner, out, weight_held, cot_held, weight_sems, cot_sems):
-    steps = weight_sems.shape[0]
-    tile = weight.shape[1] // steps
-    cols = [slice(k * tile, (k + 1) * tile) for k in range(steps)]
-    copies = []
-    for k, c in enumerate(cols):
-        copies.append(pltpu.make_async_copy(cot.at[:, c], cot_held.at[:, c], cot_sems.at[k]))
-        copies.append(pltpu.make_async_copy(weight.at[:, c], weight_held.at[:, c], weight_sems.at[k]))
-    for copy in copies:
-        copy.start()
-    hidden, block = factor.shape
-    unit = lax.broadcasted_iota(jnp.int32, (hidden, block), 0)
-    zero = jnp.zeros((hidden, block), BF16)
-    first = jnp.where(unit < hidden // 2, factor[...], zero)
-    second = jnp.where(unit < hidden // 2, zero, factor[...])
-    out[...] = dot_nt(jnp.concatenate([first, second], axis=1), d_inner[...])
-    for k, c in enumerate(cols):
-        copies[2 * k].wait()
-        copies[2 * k + 1].wait()
-        out[...] += dot_nt(weight_held[:, c], cot_held[:, c])
-
-
-def call_token_grads(weight, cot, factor, d_inner, tile=1024):
+def token_grads(weight, cot, factor, d_inner, out):
+    term = dot_nt(weight[...], cot[...])
+
+    @pl.when(pl.program_id(0) == 0)
+    def _():
+        hidden, block = factor.shape
+        unit = lax.broadcasted_iota(jnp.int32, (hidden, block), 0)
+        zero = jnp.zeros((hidden, block), BF16)
+        first = jnp.where(unit < hidden // 2, factor[...], zero)
+        second = jnp.where(unit < hidden // 2, zero, factor[...])
+        wide = jnp.concatenate([first, second], axis=1)
+        out[...] = term + dot_nt(wide, d_inner[...])
+
+    @pl.when(pl.program_id(0) > 0)
+    def _():
+        out[...] += term
+
+
+def call_token_grads(weight, cot, factor, d_inner, tile=TILE):
     hidden, width = weight.shape
     rows, channels = d_inner.shape
     return pl.pallas_call(
         token_grads,
-        in_specs=[ANY, ANY, VMEM, VMEM],
-        out_specs=VMEM,
+        grid=(width // tile,),
+        in_specs=[
+            pl.BlockSpec((hidden, tile), lambda k: (0, k)),
+            pl.BlockSpec((rows, tile), lambda k: (0, k)),
+            pl.BlockSpec(factor.shape, lambda k: (0, 0)),
+            pl.BlockSpec((rows, channels), lambda k: (0, 0)),
+        ],
+        out_specs=pl.BlockSpec((hidden, rows), lambda k: (0, 0)),
         out_shape=jax.ShapeDtypeStruct((hidden, rows), F32),
-        scratch_shapes=[
-            pltpu.VMEM((hidden, width), BF16),
-            pltpu.VMEM((rows, width), BF16),
-            pltpu.SemaphoreType.DMA((width // tile,)),
-            pltpu.SemaphoreType.DMA((width // tile,)),
-        ],
         compiler_params=params(60),
         name="token_grads",
         cost_estimate=cost(2 * rows * hidden * width, hidden * width * 2),
@@ -410,19 +406,19 @@
     next_y, last_y = turn(pair, 1), turn(pair, 3)
     mixed = call_reorder(order, inner)
     sent, kept = call_pair_sum(own, lax.ppermute(other, "c", SWAP))
-    left = lax.ppermute(sent[0], "zh", SWAP)
     theirs = [lax.ppermute(pair, "c", SWAP)]
-    pair, next_y, last_y, mixed, left, right, kept, theirs = hold(
-        (pair, next_y, last_y, mixed, left, sent[1], kept, theirs)
+    pair, next_y, last_y, mixed, sent, kept, theirs = hold(
+        (pair, next_y, last_y, mixed, sent, kept, theirs)
     )
 
     far = [turn(next_y[:share], 1), turn(last_y[share:], 3)]
     mine = [pair, next_y, last_y]
     theirs = theirs + [lax.ppermute(v, "c", SWAP) for v in mine[1:]]
+    mixed_mine = lax.all_to_all(mixed, TENSOR, 0, 0)
+    left = lax.ppermute(sent[0], "zh", SWAP)
+    far, theirs, left, right, mixed_mine = hold((far, theirs, left, sent[1], mixed_mine))
+
     right = lax.ppermute(right, "zh", SWAP)
-    mixed_mine = lax.all_to_all(mixed, TENSOR, 0, 0)
-    far, theirs, left, right, mixed_mine = hold((far, theirs, left, right, mixed_mine))
-
     chunks = mine + far + theirs + [lax.ppermute(v, "c", SWAP) for v in far]
     d_inner, sums, cot = call_factor_grads(order, mixed_mine, tokens.T, chunks, room)
     sums = lax.all_to_all(sums.reshape(8, -1, block_out), DP, 0, 0)

time: 113 us -> 108 us (0.956)
  blocking collectives: 17.1 us -> 12.3 us
  starting transfers between devices: 34.5 us -> 37.7 us
  Pallas kernels: 36.7 us -> 34.2 us
  waiting for transfers between devices: 10.8 us -> 9.36 us
    all_to_all x1, blocking collectives: 17.1 us -> 12.3 us  [per_device(): mixed_mine = lax.all_to_all(mixed, TENSOR, 0, 0)]
    ppermute x7, starting transfers between devices: 8.54 us -> 11.9 us  [turn(): return lax.ppermute(value, 'y', [(i, (i + by) % 4) for i in range(4)])]
    pallas_call x1, Pallas kernels: 7.11 us -> 4.59 us  [call_factor_grads(): pl.pallas_call(factor_grads, in_specs=[VMEM] * (3 + CHUNKS), out_specs=[V...]
    ppermute x7, waiting for transfers between devices: 6.35 us -> 8.6 us  [turn(): return lax.ppermute(value, 'y', [(i, (i + by) % 4) for i in range(4)])]
    ppermute x2, waiting for transfers between devices: 1.58 us -> 0.01 us  [per_device(): chunks = mine + far + theirs + [lax.ppermute(v, 'c', SWAP) for v in far]]
    unnamed x52 -> x50, local copies, waits for them, and re-layouts: 7.88 us -> 8.61 us
  transfers between devices with their start and end apart: 19 -> 19, of which waited for: 6 -> 3; matrix products, arithmetic and copies ran while one was open for 5% -> 5% of each run, Pallas kernels for 25% -> 30%
where the time goes in v5:
time: 108 us; the launch traced here: 107 us
  starting transfers between devices  37.7 us (35%)
  Pallas kernels  34.2 us (32%)
  blocking collectives  12.3 us (11%)
  local copies, waits for them, and re-layouts  10.4 us (10%)
  waiting for transfers between devices  9.36 us (9%)
  other arithmetic  1.99 us (2%)
    all_to_all x1, blocking collectives, per_device(): mixed_mine = lax.all_to_all(mixed, TENSOR, 0, 0)  12.3 us
    ppermute x7, starting transfers between devices, turn(): return lax.ppermute(value, 'y', [(i, (i + by) % 4) for i in range(4)])  11.9 us
    pallas_call x1, Pallas kernels, call_token_grads(): pl.pallas_call(token_grads, grid=(width // tile,), in_specs=[pl.BlockSpec...  9.08 us
    pallas_call x1, Pallas kernels, call_base_rows(): pl.pallas_call(base_rows, grid=(width // tile,), in_specs=[pl.BlockSpec((...  8.67 us
    unnamed x50, local copies, waits for them, and re-layouts  8.61 us
    ppermute x7, waiting for transfers between devices, turn(): return lax.ppermute(value, 'y', [(i, (i + by) % 4) for i in range(4)])  8.6 us
    all_to_all x1, starting transfers between devices, per_device(): sums = lax.all_to_all(sums.reshape(8, -1, block_out), DP, 0, 0)  5.28 us
    all_to_all x1, starting transfers between devices, spread(): return lax.all_to_all(whole, axes, 0, 0)  4.98 us
  transfers between devices with their start and end apart: 19, of which 3 were waited for; matrix products, arithmetic and copies ran while one was open for 5% of the time, Pallas kernels for 30%

profile of v5, /device:TPU:2, one launch (start us, length us, event | category | flops | bytes accessed | tf_op | source)
XLA Modules:
  0.0 107.4 jit_solution(11254251884979594225)
XLA Ops:
  0.6 1.8 %pack.1 = bf16[32,5120]{1,0:T(8,128)(2,1)} custom-call(bf16[32,4096]{1,0:T(8,128)(2,1)} %cotangent.1, bf16[256,128]{1,0:T(8,128)(2,1)} %bitcast.20), custom_call_target="tpu_custom_call" | custom-call | bytes 5242 | tf_op jit(solution)/shard_map/pack/pallas_call | solution.py:64
  2.4 3.9 %collective-permute-start = (bf16[32,5120]{1,0:T(8,128)(2,1)}, bf16[32,5120]{1,0:T(8,128)(2,1)S(1)}, u32[]{:S(2)}, u32[]{:S(2)}) collective-permute-start(bf16[32,5120]{1,0:T(8,128)(2,1)} %pack.1), channel_id=1, source_target_pairs={{0,8},{8,0},{1,9},{9,1},{2,10},{10,2},{3,11},{11,3},{4,12},{12,4},... | collective-permute-start | bytes 983048 | tf_op jit(solution)/shard_map/ppermute | solution.py:396
  6.3 1.0 copy.13
  8.2 0.8 copy.14
  9.0 4.6 %all-to-all-start = ((bf16[16,32,256]{2,1,0:T(8,128)(2,1)}), bf16[16,32,256]{2,1,0:T(8,128)(2,1)S(1)}, u32[]{:S(2)}, u32[]{:S(2)}) async-start(bf16[16,32,256]{2,1,0:T(8,128)(2,1)} %bitcast.2), calls=%async_computation | async-start | bytes 524288 | tf_op jit(solution)/shard_map/all_to_all | solution.py:401
  13.6 1.3 %copy.15.tokens = bf16[512,924]{1,0:T(8,128)(2,1)} copy(bf16[512,924]{0,1:T(8,128)(2,1)S(1)} %copy-done.4) | data formatting | bytes 1892352 | tf_op args[0]
  14.9 8.7 %base_rows.1 = (bf16[256,4096]{1,0:T(8,128)(2,1)}, bf16[256,4096]{1,0:T(8,128)(2,1)}) custom-call(bf16[512,924]{1,0:T(8,128)(2,1)} %copy.15.tokens, bf16[924,4096]{1,0:T(8,128)(2,1)} %weight.3), custom_call_target="tpu_custom_call" | custom-call | flops 38755368 | bytes 75694 | tf_op jit(solution)/shard_map/base_rows/pallas_call | solution.py:101
  24.1 1.8 %collective-permute-start.1 = (bf16[64,5120]{1,0:T(8,128)(2,1)S(1)}, bf16[64,5120]{1,0:T(8,128)(2,1)S(1)}, u32[]{:S(2)}, u32[]{:S(2)}) collective-permute-start(bf16[64,5120]{1,0:T(8,128)(2,1)S(1)} %constant_dynamic-update-slice_fusion.refs_0_), channel_id=1, source_target_pairs={{0,2},{2,4},{4,6},{6,0},{1,3},{3,5},{5,7},{7,1},{8,10},{10,12},{12... | collective-permute-start | bytes 1966088 | tf_op jit(solution)/shard_map/ppermute | solution.py:34
  25.9 1.6 %collective-permute-start.2 = (bf16[64,5120]{1,0:T(8,128)(2,1)S(1)}, bf16[64,5120]{1,0:T(8,128)(2,1)S(1)}, u32[]{:S(2)}, u32[]{:S(2)}) collective-permute-start(bf16[64,5120]{1,0:T(8,128)(2,1)S(1)} %constant_dynamic-update-slice_fusion.refs_0_), channel_id=1, source_target_pairs={{0,6},{2,0},{4,2},{6,4},{1,7},{3,1},{5,3},{7,5},{8,14},{10,8},{12,... | collective-permute-start | bytes 1966088 | tf_op jit(solution)/shard_map/ppermute | solution.py:34
  27.5 3.5 %reorder.1.mixed = bf16[16,32,256]{2,1,0:T(8,128)(2,1)S(1)} custom-call(s32[32,128]{1,0:T(8,128)S(1)} %bitcast.15, bf16[16,32,256]{2,1,0:T(8,128)(2,1)S(1)} %all-to-all-done.inner), custom_call_target="tpu_custom_call" | custom-call | flops 167772 | bytes 5242 | tf_op jit(solution)/shard_map/reorder/pallas_call | solution.py:213
  31.0 1.7 %copy-done.9 = bf16[256,4096]{1,0:T(8,128)(2,1)S(1)} copy-done((bf16[256,4096]{1,0:T(8,128)(2,1)S(1)}, bf16[256,4096]{1,0:T(8,128)(2,1)}, u32[]{:S(2)}) %copy-start.9) | copy-done | bytes 2097176
  32.7 1.3 %pair_sum.1 = (bf16[128,2048]{1,0:T(8,128)(2,1)S(1)}, bf16[128,2048]{1,0:T(8,128)(2,1)S(1)}, bf16[128,4096]{1,0:T(8,128)(2,1)S(1)}) custom-call(bf16[256,4096]{1,0:T(8,128)(2,1)S(1)} %copy-done.9, bf16[256,4096]{1,0:T(8,128)(2,1)S(1)} %collective-permute-done.3.got), custom_call_target="tpu_custom_call" | custom-call | flops 10485 | bytes 62914 | tf_op jit(solution)/shard_map/pair_sum/pallas_call | solution.py:139
  34.0 8.3 %collective-permute-done.1.refs_1_ = bf16[64,5120]{1,0:T(8,128)(2,1)S(1)} collective-permute-done((bf16[64,5120]{1,0:T(8,128)(2,1)S(1)}, bf16[64,5120]{1,0:T(8,128)(2,1)S(1)}, u32[]{:S(2)}, u32[]{:S(2)}) %collective-permute-start.1) | collective-permute-done | bytes 655392 | tf_op jit(solution)/shard_map/ppermute | solution.py:34
  43.2 3.0 %collective-permute-start.9 = (bf16[128,2048]{1,0:T(8,128)(2,1)S(1)}, bf16[128,2048]{1,0:T(8,128)(2,1)S(1)}, u32[]{:S(2)}, u32[]{:S(2)}) collective-permute-start(bf16[128,2048]{1,0:T(8,128)(2,1)S(1)} %get-tuple-element.63), channel_id=1, source_target_pairs={{0,8},{8,0},{1,9},{9,1},{2,10},{10,2},{3,11},{11,3},{4,12},{12,4},... | collective-permute-start | bytes 1572872 | tf_op jit(solution)/shard_map/ppermute | solution.py:418
  46.3 1.5 %collective-permute-start.5 = (bf16[32,5120]{1,0:T(8,128)(2,1)S(1)}, bf16[32,5120]{1,0:T(8,128)(2,1)S(1)}, u32[]{:S(2)}, u32[]{:S(2)}) collective-permute-start(bf16[32,5120]{1,0:T(8,128)(2,1)S(1)} %slice.15), channel_id=1, source_target_pairs={{0,2},{2,4},{4,6},{6,0},{1,3},{3,5},{5,7},{7,1},{8,10},{10,12},{12... | collective-permute-start | bytes 983048 | tf_op jit(solution)/shard_map/ppermute | solution.py:34
  47.8 1.8 %collective-permute-start.6 = (bf16[32,5120]{1,0:T(8,128)(2,1)S(1)}, bf16[32,5120]{1,0:T(8,128)(2,1)S(1)}, u32[]{:S(2)}, u32[]{:S(2)}) collective-permute-start(bf16[32,5120]{1,0:T(8,128)(2,1)S(1)} %slice.16), channel_id=1, source_target_pairs={{0,6},{2,0},{4,2},{6,4},{1,7},{3,1},{5,3},{7,5},{8,14},{10,8},{12,... | collective-permute-start | bytes 983048 | tf_op jit(solution)/shard_map/ppermute | solution.py:34
  49.6 12.3 %all_to_all.20.mixed = bf16[16,32,256]{2,1,0:T(8,128)(2,1)S(1)} all-to-all(bf16[16,32,256]{2,1,0:T(8,128)(2,1)S(1)} %reorder.1.mixed), channel_id=1, replica_groups=mesh['zl'=2,'x'=4,'zh'=2,'y'=4,'c'=2] {'zh','y','c'}, dimensions={0} | all-to-all | bytes 524288 | tf_op jit(solution)/shard_map/all_to_all | solution.py:417
  62.5 2.4 %collective-permute-start.10 = (bf16[128,2048]{1,0:T(8,128)(2,1)S(1)}, bf16[128,2048]{1,0:T(8,128)(2,1)S(1)}, u32[]{:S(2)}, u32[]{:S(2)}) collective-permute-start(bf16[128,2048]{1,0:T(8,128)(2,1)S(1)} %get-tuple-element.67), channel_id=1, source_target_pairs={{0,8},{8,0},{1,9},{9,1},{2,10},{10,2},{3,11},{11,3},{4,12},{12,4},... | collective-permute-start | bytes 1572872 | tf_op jit(solution)/shard_map/ppermute | solution.py:421
  65.0 4.6 %factor_grads.1 = (bf16[512,256]{1,0:T(8,128)(2,1)S(1)}, bf16[1280,128]{1,0:T(8,128)(2,1)}, bf16[512,4096]{1,0:T(8,128)(2,1)S(1)}) custom-call(s32[32,128]{1,0:T(8,128)S(1)} %bitcast.16, bf16[16,32,256]{2,1,0:T(8,128)(2,1)S(1)} %all_to_all.20.mixed, bf16[924,512]{1,0:T(8,128)(2,1)S(1)} %bitcast.14, ...), custom_call_target="tpu_custom_call" | custom-call | flops 21474836 | bytes 41943 | tf_op jit(solution)/shard_map/factor_grads/pallas_call | solution.py:327
  69.7 2.0 %copy-done = bf16[512,4096]{1,0:T(8,128)(2,1)} copy-done((bf16[512,4096]{1,0:T(8,128)(2,1)}, bf16[512,4096]{1,0:T(8,128)(2,1)S(1)}, u32[]{:S(2)}) %copy-start) | copy-done | bytes 4194328
  72.4 5.3 %all-to-all-start.2 = ((bf16[8,160,128]{2,1,0:T(8,128)(2,1)}), bf16[8,160,128]{2,1,0:T(8,128)(2,1)S(1)}, u32[]{:S(2)}, u32[]{:S(2)}) async-start(bf16[8,160,128]{2,1,0:T(8,128)(2,1)} %bitcast.5), calls=%async_computation.2 | async-start | bytes 655360 | tf_op jit(solution)/shard_map/all_to_all | solution.py:424
  77.7 2.6 %delta_rows.1 = f32[32,4096]{1,0:T(8,128)} custom-call(bf16[16,32,256]{2,1,0:T(8,128)(2,1)} %copy-done.8, bf16[64,5120]{1,0:T(8,128)(2,1)} %copy-done.3, bf16[64,5120]{1,0:T(8,128)(2,1)} %copy-done.1, bf16[64,5120]{1,0:T(8,128)(2,1)} %copy-done.2, bf16[32,5120]{1,0:T(8,128)(2,1)} %copy-done.10, bf16[32,5120]{1,0:T(8,128)(2,1)} %copy-done.11, ...), custom_call_target="tpu_custom_call" | custom-call | flops 335544 | bytes 7864 | tf_op jit(solution)/shard_map/delta_rows/pallas_call | solution.py:262
  80.3 0.8 copy-done.22
  81.1 2.6 %quad_sum.1 = (bf16[32,4096]{1,0:T(8,128)(2,1)}, bf16[32,4096]{1,0:T(8,128)(2,1)}, bf16[32,4096]{1,0:T(8,128)(2,1)}, f32[32,4096]{1,0:T(8,128)}) custom-call(bf16[128,4096]{1,0:T(8,128)(2,1)} %copy-done.14, bf16[128,2048]{1,0:T(8,128)(2,1)} %copy-done.20, bf16[128,2048]{1,0:T(8,128)(2,1)} %copy-done.22), custom_call_target="tpu_custom_call" | custom-call | flops 5242 | bytes 41943 | tf_op jit(solution)/shard_map/quad_sum/pallas_call | solution.py:172
  84.5 1.4 %collective-permute-start.13 = (bf16[32,4096]{1,0:T(8,128)(2,1)}, bf16[32,4096]{1,0:T(8,128)(2,1)S(1)}, u32[]{:S(2)}, u32[]{:S(2)}) collective-permute-start(bf16[32,4096]{1,0:T(8,128)(2,1)} %get-tuple-element.83), channel_id=1, source_target_pairs={{0,2},{2,4},{4,6},{6,0},{1,3},{3,5},{5,7},{7,1},{8,10},{10,12},{12... | collective-permute-start | bytes 786440 | tf_op jit(solution)/shard_map/ppermute | solution.py:34
  85.9 3.0 %collective-permute-start.14 = (bf16[32,4096]{1,0:T(8,128)(2,1)}, bf16[32,4096]{1,0:T(8,128)(2,1)S(1)}, u32[]{:S(2)}, u32[]{:S(2)}) collective-permute-start(bf16[32,4096]{1,0:T(8,128)(2,1)} %get-tuple-element.84), channel_id=1, source_target_pairs={{0,4},{2,6},{4,0},{6,2},{1,5},{3,7},{5,1},{7,3},{8,12},{10,14},{12... | collective-permute-start | bytes 786440 | tf_op jit(solution)/shard_map/ppermute | solution.py:34
  88.9 0.9 collective-permute-start.15
  89.8 0.8 broadcast_in_dim.28
  90.6 5.0 %all-to-all-start.3 = ((bf16[8,160,128]{2,1,0:T(8,128)(2,1)}), bf16[8,160,128]{2,1,0:T(8,128)(2,1)S(1)}, u32[]{:S(2)}, u32[]{:S(2)}) async-start(bf16[8,160,128]{2,1,0:T(8,128)(2,1)} %broadcast_in_dim.28), calls=%async_computation.3 | async-start | bytes 655360 | tf_op jit(solution)/shard_map/all_to_all | solution.py:39
  95.6 9.1 %token_grads.1 = f32[924,512]{1,0:T(8,128)} custom-call(bf16[924,4096]{1,0:T(8,128)(2,1)} %weight.3, bf16[512,4096]{1,0:T(8,128)(2,1)} %copy-done, bf16[924,128]{1,0:T(8,128)(2,1)} %copy-done.17, bf16[512,256]{1,0:T(8,128)(2,1)} %copy-done.15), custom_call_target="tpu_custom_call" | custom-call | flops 38755368 | bytes 75694 | tf_op jit(solution)/shard_map/token_grads/pallas_call | solution.py:368
  104.7 0.9 convert_add_fusion
  105.7 1.0 copy.16
  (81 shorter events, 5.2 us)
Async XLA Ops:
  2.4 21.2 %collective-permute-start = (bf16[32,5120]{1,0:T(8,128)(2,1)}, bf16[32,5120]{1,0:T(8,128)(2,1)S(1)}, u32[]{:S(2)}, u32[]{:S(2)}) collective-permute-start(bf16[32,5120]{1,0:T(8,128)(2,1)} %pack.1), channel_id=1, source_target_pairs={{0,8},{8,0},{1,9},{9,1},{2,10},{10,2},{3,11},{11,3},{4,12},{12,4},... | collective-permute-start | bytes 983048 | tf_op jit(solution)/shard_map/ppermute | solution.py:396
  9.0 14.6 %all-to-all-start = ((bf16[16,32,256]{2,1,0:T(8,128)(2,1)}), bf16[16,32,256]{2,1,0:T(8,128)(2,1)S(1)}, u32[]{:S(2)}, u32[]{:S(2)}) async-start(bf16[16,32,256]{2,1,0:T(8,128)(2,1)} %bitcast.2), calls=%async_computation | async-start | bytes 524288 | tf_op jit(solution)/shard_map/all_to_all | solution.py:401
  14.9 9.2 %copy-start.19 = (bf16[32,5120]{1,0:T(8,128)(2,1)S(1)}, bf16[32,5120]{1,0:T(8,128)(2,1)}, u32[]{:S(2)}) copy-start(bf16[32,5120]{1,0:T(8,128)(2,1)} %pack.1) | copy-start | bytes 983044
  14.9 12.5 %copy-start.16 = (s32[4096]{0:T(1024)S(1)}, s32[4096]{0:T(1024)}, u32[]{:S(2)}) copy-start(s32[4096]{0:T(1024)} %param.10) | copy-start | bytes 49156
  23.6 7.4 %collective-permute-start.3 = (bf16[256,4096]{1,0:T(8,128)(2,1)}, bf16[256,4096]{1,0:T(8,128)(2,1)S(1)}, u32[]{:S(2)}, u32[]{:S(2)}) collective-permute-start(bf16[256,4096]{1,0:T(8,128)(2,1)} %get-tuple-element.55), channel_id=1, source_target_pairs={{0,1},{1,0},{2,3},{3,2},{4,5},{5,4},{6,7},{7,6},{8,9},{9,8},{10,11... | collective-permute-start | bytes 6291464 | tf_op jit(solution)/shard_map/ppermute | solution.py:408
  24.1 40.8 %copy-start.3 = (bf16[64,5120]{1,0:T(8,128)(2,1)}, bf16[64,5120]{1,0:T(8,128)(2,1)S(1)}, u32[]{:S(2)}) copy-start(bf16[64,5120]{1,0:T(8,128)(2,1)S(1)} %constant_dynamic-update-slice_fusion.refs_0_) | copy-start | bytes 1966084
  24.1 18.2 %collective-permute-start.1 = (bf16[64,5120]{1,0:T(8,128)(2,1)S(1)}, bf16[64,5120]{1,0:T(8,128)(2,1)S(1)}, u32[]{:S(2)}, u32[]{:S(2)}) collective-permute-start(bf16[64,5120]{1,0:T(8,128)(2,1)S(1)} %constant_dynamic-update-slice_fusion.refs_0_), channel_id=1, source_target_pairs={{0,2},{2,4},{4,6},{6,0},{1,3},{3,5},{5,7},{7,1},{8,10},{10,12},{12... | collective-permute-start | bytes 1966088 | tf_op jit(solution)/shard_map/ppermute | solution.py:34
  25.9 16.7 %collective-permute-start.2 = (bf16[64,5120]{1,0:T(8,128)(2,1)S(1)}, bf16[64,5120]{1,0:T(8,128)(2,1)S(1)}, u32[]{:S(2)}, u32[]{:S(2)}) collective-permute-start(bf16[64,5120]{1,0:T(8,128)(2,1)S(1)} %constant_dynamic-update-slice_fusion.refs_0_), channel_id=1, source_target_pairs={{0,6},{2,0},{4,2},{6,4},{1,7},{3,1},{5,3},{7,5},{8,14},{10,8},{12,... | collective-permute-start | bytes 1966088 | tf_op jit(solution)/shard_map/ppermute | solution.py:34
  27.5 15.2 %collective-permute-start.4 = (bf16[64,5120]{1,0:T(8,128)(2,1)S(1)}, bf16[64,5120]{1,0:T(8,128)(2,1)S(1)}, u32[]{:S(2)}, u32[]{:S(2)}) collective-permute-start(bf16[64,5120]{1,0:T(8,128)(2,1)S(1)} %constant_dynamic-update-slice_fusion.refs_0_), channel_id=1, source_target_pairs={{0,1},{1,0},{2,3},{3,2},{4,5},{5,4},{6,7},{7,6},{8,9},{9,8},{10,11... | collective-permute-start | bytes 1966088 | tf_op jit(solution)/shard_map/ppermute | solution.py:409
  31.0 18.6 %copy-start.8 = (bf16[16,32,256]{2,1,0:T(8,128)(2,1)}, bf16[16,32,256]{2,1,0:T(8,128)(2,1)S(1)}, u32[]{:S(2)}) copy-start(bf16[16,32,256]{2,1,0:T(8,128)(2,1)S(1)} %reorder.1.mixed) | copy-start | bytes 786436
  34.0 31.0 %copy-start.14 = (bf16[128,4096]{1,0:T(8,128)(2,1)}, bf16[128,4096]{1,0:T(8,128)(2,1)S(1)}, u32[]{:S(2)}) copy-start(bf16[128,4096]{1,0:T(8,128)(2,1)S(1)} %get-tuple-element.59.kept) | copy-start | bytes 3145732
  42.4 27.2 %copy-start.1 = (bf16[64,5120]{1,0:T(8,128)(2,1)}, bf16[64,5120]{1,0:T(8,128)(2,1)S(1)}, u32[]{:S(2)}) copy-start(bf16[64,5120]{1,0:T(8,128)(2,1)S(1)} %collective-permute-done.1.refs_1_) | copy-start | bytes 1966084
  42.6 27.0 %copy-start.2 = (bf16[64,5120]{1,0:T(8,128)(2,1)}, bf16[64,5120]{1,0:T(8,128)(2,1)S(1)}, u32[]{:S(2)}) copy-start(bf16[64,5120]{1,0:T(8,128)(2,1)S(1)} %collective-permute-done.2.refs_2_) | copy-start | bytes 1966084
  42.6 27.0 %copy-start.5 = (bf16[64,5120]{1,0:T(8,128)(2,1)}, bf16[64,5120]{1,0:T(8,128)(2,1)S(1)}, u32[]{:S(2)}) copy-start(bf16[64,5120]{1,0:T(8,128)(2,1)S(1)} %collective-permute-done.4.refs_5_) | copy-start | bytes 1966084
  42.6 19.3 %collective-permute-start.7 = (bf16[64,5120]{1,0:T(8,128)(2,1)S(1)}, bf16[64,5120]{1,0:T(8,128)(2,1)S(1)}, u32[]{:S(2)}, u32[]{:S(2)}) collective-permute-start(bf16[64,5120]{1,0:T(8,128)(2,1)S(1)} %collective-permute-done.1.refs_1_), channel_id=1, source_target_pairs={{0,1},{1,0},{2,3},{3,2},{4,5},{5,4},{6,7},{7,6},{8,9},{9,8},{10,11... | collective-permute-start | bytes 1966088 | tf_op jit(solution)/shard_map/ppermute | solution.py:416
  42.7 19.2 %collective-permute-start.8 = (bf16[64,5120]{1,0:T(8,128)(2,1)S(1)}, bf16[64,5120]{1,0:T(8,128)(2,1)S(1)}, u32[]{:S(2)}, u32[]{:S(2)}) collective-permute-start(bf16[64,5120]{1,0:T(8,128)(2,1)S(1)} %collective-permute-done.2.refs_2_), channel_id=1, source_target_pairs={{0,1},{1,0},{2,3},{3,2},{4,5},{5,4},{6,7},{7,6},{8,9},{9,8},{10,11... | collective-permute-start | bytes 1966088 | tf_op jit(solution)/shard_map/ppermute | solution.py:416
  43.2 18.7 %collective-permute-start.9 = (bf16[128,2048]{1,0:T(8,128)(2,1)S(1)}, bf16[128,2048]{1,0:T(8,128)(2,1)S(1)}, u32[]{:S(2)}, u32[]{:S(2)}) collective-permute-start(bf16[128,2048]{1,0:T(8,128)(2,1)S(1)} %get-tuple-element.63), channel_id=1, source_target_pairs={{0,8},{8,0},{1,9},{9,1},{2,10},{10,2},{3,11},{11,3},{4,12},{12,4},... | collective-permute-start | bytes 1572872 | tf_op jit(solution)/shard_map/ppermute | solution.py:418
  46.3 15.6 %collective-permute-start.5 = (bf16[32,5120]{1,0:T(8,128)(2,1)S(1)}, bf16[32,5120]{1,0:T(8,128)(2,1)S(1)}, u32[]{:S(2)}, u32[]{:S(2)}) collective-permute-start(bf16[32,5120]{1,0:T(8,128)(2,1)S(1)} %slice.15), channel_id=1, source_target_pairs={{0,2},{2,4},{4,6},{6,0},{1,3},{3,5},{5,7},{7,1},{8,10},{10,12},{12... | collective-permute-start | bytes 983048 | tf_op jit(solution)/shard_map/ppermute | solution.py:34
  47.8 14.1 %collective-permute-start.6 = (bf16[32,5120]{1,0:T(8,128)(2,1)S(1)}, bf16[32,5120]{1,0:T(8,128)(2,1)S(1)}, u32[]{:S(2)}, u32[]{:S(2)}) collective-permute-start(bf16[32,5120]{1,0:T(8,128)(2,1)S(1)} %slice.16), channel_id=1, source_target_pairs={{0,6},{2,0},{4,2},{6,4},{1,7},{3,1},{5,3},{7,5},{8,14},{10,8},{12,... | collective-permute-start | bytes 983048 | tf_op jit(solution)/shard_map/ppermute | solution.py:34
  61.9 7.8 %copy-start.10 = (bf16[32,5120]{1,0:T(8,128)(2,1)}, bf16[32,5120]{1,0:T(8,128)(2,1)S(1)}, u32[]{:S(2)}) copy-start(bf16[32,5120]{1,0:T(8,128)(2,1)S(1)} %collective-permute-done.5.refs_3_) | copy-start | bytes 983044
  61.9 7.8 %copy-start.11 = (bf16[32,5120]{1,0:T(8,128)(2,1)}, bf16[32,5120]{1,0:T(8,128)(2,1)S(1)}, u32[]{:S(2)}) copy-start(bf16[32,5120]{1,0:T(8,128)(2,1)S(1)} %collective-permute-done.6.refs_4_) | copy-start | bytes 983044
  61.9 7.8 %copy-start.20 = (bf16[128,2048]{1,0:T(8,128)(2,1)}, bf16[128,2048]{1,0:T(8,128)(2,1)S(1)}, u32[]{:S(2)}) copy-start(bf16[128,2048]{1,0:T(8,128)(2,1)S(1)} %collective-permute-done.9.left) | copy-start | bytes 1572868
  61.9 3.0 %collective-permute-start.11 = (bf16[32,5120]{1,0:T(8,128)(2,1)S(1)}, bf16[32,5120]{1,0:T(8,128)(2,1)S(1)}, u32[]{:S(2)}, u32[]{:S(2)}) collective-permute-start(bf16[32,5120]{1,0:T(8,128)(2,1)S(1)} %collective-permute-done.5.refs_3_), channel_id=1, source_target_pairs={{0,1},{1,0},{2,3},{3,2},{4,5},{5,4},{6,7},{7,6},{8,9},{9,8},{10,11... | collective-permute-start | bytes 983048 | tf_op jit(solution)/shard_map/ppermute | solution.py:422
  62.0 2.9 %collective-permute-start.12 = (bf16[32,5120]{1,0:T(8,128)(2,1)S(1)}, bf16[32,5120]{1,0:T(8,128)(2,1)S(1)}, u32[]{:S(2)}, u32[]{:S(2)}) collective-permute-start(bf16[32,5120]{1,0:T(8,128)(2,1)S(1)} %collective-permute-done.6.refs_4_), channel_id=1, source_target_pairs={{0,1},{1,0},{2,3},{3,2},{4,5},{5,4},{6,7},{7,6},{8,9},{9,8},{10,11... | collective-permute-start | bytes 983048 | tf_op jit(solution)/shard_map/ppermute | solution.py:422
  62.5 17.8 %collective-permute-start.10 = (bf16[128,2048]{1,0:T(8,128)(2,1)S(1)}, bf16[128,2048]{1,0:T(8,128)(2,1)S(1)}, u32[]{:S(2)}, u32[]{:S(2)}) collective-permute-start(bf16[128,2048]{1,0:T(8,128)(2,1)S(1)} %get-tuple-element.67), channel_id=1, source_target_pairs={{0,8},{8,0},{1,9},{9,1},{2,10},{10,2},{3,11},{11,3},{4,12},{12,4},... | collective-permute-start | bytes 1572872 | tf_op jit(solution)/shard_map/ppermute | solution.py:421
  72.4 12.1 %all-to-all-start.2 = ((bf16[8,160,128]{2,1,0:T(8,128)(2,1)}), bf16[8,160,128]{2,1,0:T(8,128)(2,1)S(1)}, u32[]{:S(2)}, u32[]{:S(2)}) async-start(bf16[8,160,128]{2,1,0:T(8,128)(2,1)} %bitcast.5), calls=%async_computation.2 | async-start | bytes 655360 | tf_op jit(solution)/shard_map/all_to_all | solution.py:424
  84.5 20.2 %collective-permute-start.13 = (bf16[32,4096]{1,0:T(8,128)(2,1)}, bf16[32,4096]{1,0:T(8,128)(2,1)S(1)}, u32[]{:S(2)}, u32[]{:S(2)}) collective-permute-start(bf16[32,4096]{1,0:T(8,128)(2,1)} %get-tuple-element.83), channel_id=1, source_target_pairs={{0,2},{2,4},{4,6},{6,0},{1,3},{3,5},{5,7},{7,1},{8,10},{10,12},{12... | collective-permute-start | bytes 786440 | tf_op jit(solution)/shard_map/ppermute | solution.py:34
  85.9 18.7 %collective-permute-start.14 = (bf16[32,4096]{1,0:T(8,128)(2,1)}, bf16[32,4096]{1,0:T(8,128)(2,1)S(1)}, u32[]{:S(2)}, u32[]{:S(2)}) collective-permute-start(bf16[32,4096]{1,0:T(8,128)(2,1)} %get-tuple-element.84), channel_id=1, source_target_pairs={{0,4},{2,6},{4,0},{6,2},{1,5},{3,7},{5,1},{7,3},{8,12},{10,14},{12... | collective-permute-start | bytes 786440 | tf_op jit(solution)/shard_map/ppermute | solution.py:34
  88.9 15.8 %collective-permute-start.15 = (bf16[32,4096]{1,0:T(8,128)(2,1)}, bf16[32,4096]{1,0:T(8,128)(2,1)S(1)}, u32[]{:S(2)}, u32[]{:S(2)}) collective-permute-start(bf16[32,4096]{1,0:T(8,128)(2,1)} %get-tuple-element.85), channel_id=1, source_target_pairs={{0,6},{2,0},{4,2},{6,4},{1,7},{3,1},{5,3},{7,5},{8,14},{10,8},{12,... | collective-permute-start | bytes 786440 | tf_op jit(solution)/shard_map/ppermute | solution.py:34
  90.6 15.0 %all-to-all-start.3 = ((bf16[8,160,128]{2,1,0:T(8,128)(2,1)}), bf16[8,160,128]{2,1,0:T(8,128)(2,1)S(1)}, u32[]{:S(2)}, u32[]{:S(2)}) async-start(bf16[8,160,128]{2,1,0:T(8,128)(2,1)} %broadcast_in_dim.28), calls=%async_computation.3 | async-start | bytes 655360 | tf_op jit(solution)/shard_map/all_to_all | solution.py:39
  95.6 9.1 %copy-start.18 = (f32[32,4096]{1,0:T(8,128)S(1)}, f32[32,4096]{1,0:T(8,128)}, u32[]{:S(2)}) copy-start(f32[32,4096]{1,0:T(8,128)} %delta_rows.1) | copy-start | bytes 1572868
  95.6 9.1 %copy-start.21 = (f32[32,4096]{1,0:T(8,128)S(1)}, f32[32,4096]{1,0:T(8,128)}, u32[]{:S(2)}) copy-start(f32[32,4096]{1,0:T(8,128)} %get-tuple-element.81) | copy-start | bytes 1572868
  (10 other events, 44.7 us)

commit v6 on v5

--- a/solution.py
+++ b/solution.py
@@ -18,7 +18,7 @@
 HELD = ((0, 0, 0), (0, 1, 0), (1, 0, 1), (1, 1, 1), (2, 0, 3), (2, 1, 3), (3, 0, 2), (4, 0, 2))
 SCALE = 100
 KEPT = BF16
-LEFT = 2
+LEFT = 3
 TILE = 2048
 
 
@@ -132,7 +132,7 @@
         right[...] = total[:quarter].astype(BF16)
 
 
-def call_pair_sum(own, got, tile=1024):
+def call_pair_sum(own, got, tile=512):
     half, width = own.shape
     steps = width // tile
     out = (half // 2, tile)

time: 108 us -> 107 us (level)
  starting transfers between devices: 37.7 us -> 34.8 us
  waiting for transfers between devices: 9.36 us -> 11.5 us
    ppermute x1, starting transfers between devices: 2.42 us -> 0.69 us  [per_device(): right = lax.ppermute(right, 'zh', SWAP)]
    ppermute x2, waiting for transfers between devices: 0.01 us -> 1.68 us  [per_device(): chunks = mine + far + theirs + [lax.ppermute(v, 'c', SWAP) for v in far]]
  transfers between devices with their start and end apart: 19 -> 19, of which waited for: 3 -> 5; matrix products, arithmetic and copies ran while one was open for 5% -> 5% of each run, Pallas kernels for 30% -> 30%
where the time goes in v6:
time: 107 us
  starting transfers between devices  34.8 us (33%)
  Pallas kernels  34.3 us (32%)
  blocking collectives  12.3 us (11%)
  waiting for transfers between devices  11.5 us (11%)
  local copies, waits for them, and re-layouts  10.4 us (10%)
  other arithmetic  1.99 us (2%)
    all_to_all x1, blocking collectives, per_device(): mixed_mine = lax.all_to_all(mixed, TENSOR, 0, 0)  12.3 us
    ppermute x7, starting transfers between devices, turn(): return lax.ppermute(value, 'y', [(i, (i + by) % 4) for i in range(4)])  11.2 us
    pallas_call x1, Pallas kernels, call_token_grads(): pl.pallas_call(token_grads, grid=(width // tile,), in_specs=[pl.BlockSpec...  9.09 us
    pallas_call x1, Pallas kernels, call_base_rows(): pl.pallas_call(base_rows, grid=(width // tile,), in_specs=[pl.BlockSpec((...  8.67 us
    unnamed x50, local copies, waits for them, and re-layouts  8.65 us
    ppermute x7, waiting for transfers between devices, turn(): return lax.ppermute(value, 'y', [(i, (i + by) % 4) for i in range(4)])  8.54 us
    all_to_all x1, starting transfers between devices, per_device(): sums = lax.all_to_all(sums.reshape(8, -1, block_out), DP, 0, 0)  5.3 us
    all_to_all x1, starting transfers between devices, spread(): return lax.all_to_all(whole, axes, 0, 0)  4.6 us
  transfers between devices with their start and end apart: 19, of which 5 were waited for; matrix products, arithmetic and copies ran while one was open for 5% of the time, Pallas kernels for 30%

profile of v6, /device:TPU:2, one launch (start us, length us, event | category | flops | bytes accessed | tf_op | source)
XLA Modules:
  0.0 106.7 jit_solution(666187934107680491)
XLA Ops:
  0.6 1.8 %pack.1 = bf16[32,5120]{1,0:T(8,128)(2,1)} custom-call(bf16[32,4096]{1,0:T(8,128)(2,1)} %cotangent.1, bf16[256,128]{1,0:T(8,128)(2,1)} %bitcast.20), custom_call_target="tpu_custom_call" | custom-call | bytes 5242 | tf_op jit(solution)/shard_map/pack/pallas_call | solution.py:64
  2.4 3.9 %collective-permute-start = (bf16[32,5120]{1,0:T(8,128)(2,1)}, bf16[32,5120]{1,0:T(8,128)(2,1)S(1)}, u32[]{:S(2)}, u32[]{:S(2)}) collective-permute-start(bf16[32,5120]{1,0:T(8,128)(2,1)} %pack.1), channel_id=1, source_target_pairs={{0,8},{8,0},{1,9},{9,1},{2,10},{10,2},{3,11},{11,3},{4,12},{12,4},... | collective-permute-start | bytes 983048 | tf_op jit(solution)/shard_map/ppermute | solution.py:396
  6.3 1.0 copy.13
  8.2 0.8 copy.14
  9.0 4.6 %all-to-all-start = ((bf16[16,32,256]{2,1,0:T(8,128)(2,1)}), bf16[16,32,256]{2,1,0:T(8,128)(2,1)S(1)}, u32[]{:S(2)}, u32[]{:S(2)}) async-start(bf16[16,32,256]{2,1,0:T(8,128)(2,1)} %bitcast.2), calls=%async_computation | async-start | bytes 524288 | tf_op jit(solution)/shard_map/all_to_all | solution.py:401
  13.6 1.3 %copy.15.tokens = bf16[512,924]{1,0:T(8,128)(2,1)} copy(bf16[512,924]{0,1:T(8,128)(2,1)S(1)} %copy-done.4) | data formatting | bytes 1892352 | tf_op args[0]
  14.9 8.7 %base_rows.1 = (bf16[256,4096]{1,0:T(8,128)(2,1)}, bf16[256,4096]{1,0:T(8,128)(2,1)}) custom-call(bf16[512,924]{1,0:T(8,128)(2,1)} %copy.15.tokens, bf16[924,4096]{1,0:T(8,128)(2,1)} %weight.3), custom_call_target="tpu_custom_call" | custom-call | flops 38755368 | bytes 75694 | tf_op jit(solution)/shard_map/base_rows/pallas_call | solution.py:101
  24.1 1.8 %collective-permute-start.1 = (bf16[64,5120]{1,0:T(8,128)(2,1)S(1)}, bf16[64,5120]{1,0:T(8,128)(2,1)S(1)}, u32[]{:S(2)}, u32[]{:S(2)}) collective-permute-start(bf16[64,5120]{1,0:T(8,128)(2,1)S(1)} %constant_dynamic-update-slice_fusion.refs_0_), channel_id=1, source_target_pairs={{0,2},{2,4},{4,6},{6,0},{1,3},{3,5},{5,7},{7,1},{8,10},{10,12},{12... | collective-permute-start | bytes 1966088 | tf_op jit(solution)/shard_map/ppermute | solution.py:34
  25.9 1.6 %collective-permute-start.2 = (bf16[64,5120]{1,0:T(8,128)(2,1)S(1)}, bf16[64,5120]{1,0:T(8,128)(2,1)S(1)}, u32[]{:S(2)}, u32[]{:S(2)}) collective-permute-start(bf16[64,5120]{1,0:T(8,128)(2,1)S(1)} %constant_dynamic-update-slice_fusion.refs_0_), channel_id=1, source_target_pairs={{0,6},{2,0},{4,2},{6,4},{1,7},{3,1},{5,3},{7,5},{8,14},{10,8},{12,... | collective-permute-start | bytes 1966088 | tf_op jit(solution)/shard_map/ppermute | solution.py:34
  27.5 3.5 %reorder.1.mixed = bf16[16,32,256]{2,1,0:T(8,128)(2,1)S(1)} custom-call(s32[32,128]{1,0:T(8,128)S(1)} %bitcast.15, bf16[16,32,256]{2,1,0:T(8,128)(2,1)S(1)} %all-to-all-done.inner), custom_call_target="tpu_custom_call" | custom-call | flops 167772 | bytes 5242 | tf_op jit(solution)/shard_map/reorder/pallas_call | solution.py:213
  31.0 1.7 %copy-done.9 = bf16[256,4096]{1,0:T(8,128)(2,1)S(1)} copy-done((bf16[256,4096]{1,0:T(8,128)(2,1)S(1)}, bf16[256,4096]{1,0:T(8,128)(2,1)}, u32[]{:S(2)}) %copy-start.9) | copy-done | bytes 2097176
  32.7 1.4 %pair_sum.1 = (bf16[128,1536]{1,0:T(8,128)(2,1)S(1)}, bf16[128,2560]{1,0:T(8,128)(2,1)S(1)}, bf16[128,4096]{1,0:T(8,128)(2,1)S(1)}) custom-call(bf16[256,4096]{1,0:T(8,128)(2,1)S(1)} %copy-done.9, bf16[256,4096]{1,0:T(8,128)(2,1)S(1)} %collective-permute-done.3.got), custom_call_target="tpu_custom_call" | custom-call | flops 10485 | bytes 62914 | tf_op jit(solution)/shard_map/pair_sum/pallas_call | solution.py:139
  34.1 8.3 %collective-permute-done.1.refs_1_ = bf16[64,5120]{1,0:T(8,128)(2,1)S(1)} collective-permute-done((bf16[64,5120]{1,0:T(8,128)(2,1)S(1)}, bf16[64,5120]{1,0:T(8,128)(2,1)S(1)}, u32[]{:S(2)}, u32[]{:S(2)}) %collective-permute-start.1) | collective-permute-done | bytes 655392 | tf_op jit(solution)/shard_map/ppermute | solution.py:34
  43.2 3.0 %collective-permute-start.9 = (bf16[128,1536]{1,0:T(8,128)(2,1)S(1)}, bf16[128,1536]{1,0:T(8,128)(2,1)S(1)}, u32[]{:S(2)}, u32[]{:S(2)}) collective-permute-start(bf16[128,1536]{1,0:T(8,128)(2,1)S(1)} %get-tuple-element.63), channel_id=1, source_target_pairs={{0,8},{8,0},{1,9},{9,1},{2,10},{10,2},{3,11},{11,3},{4,12},{12,4},... | collective-permute-start | bytes 1179656 | tf_op jit(solution)/shard_map/ppermute | solution.py:418
  46.3 1.5 %collective-permute-start.5 = (bf16[32,5120]{1,0:T(8,128)(2,1)S(1)}, bf16[32,5120]{1,0:T(8,128)(2,1)S(1)}, u32[]{:S(2)}, u32[]{:S(2)}) collective-permute-start(bf16[32,5120]{1,0:T(8,128)(2,1)S(1)} %slice.15), channel_id=1, source_target_pairs={{0,2},{2,4},{4,6},{6,0},{1,3},{3,5},{5,7},{7,1},{8,10},{10,12},{12... | collective-permute-start | bytes 983048 | tf_op jit(solution)/shard_map/ppermute | solution.py:34
  47.8 1.8 %collective-permute-start.6 = (bf16[32,5120]{1,0:T(8,128)(2,1)S(1)}, bf16[32,5120]{1,0:T(8,128)(2,1)S(1)}, u32[]{:S(2)}, u32[]{:S(2)}) collective-permute-start(bf16[32,5120]{1,0:T(8,128)(2,1)S(1)} %slice.16), channel_id=1, source_target_pairs={{0,6},{2,0},{4,2},{6,4},{1,7},{3,1},{5,3},{7,5},{8,14},{10,8},{12,... | collective-permute-start | bytes 983048 | tf_op jit(solution)/shard_map/ppermute | solution.py:34
  49.6 12.3 %all_to_all.20.mixed = bf16[16,32,256]{2,1,0:T(8,128)(2,1)S(1)} all-to-all(bf16[16,32,256]{2,1,0:T(8,128)(2,1)S(1)} %reorder.1.mixed), channel_id=1, replica_groups=mesh['zl'=2,'x'=4,'zh'=2,'y'=4,'c'=2] {'zh','y','c'}, dimensions={0} | all-to-all | bytes 524288 | tf_op jit(solution)/shard_map/all_to_all | solution.py:417
  63.1 1.2 %collective-permute-done.11.refs_8_ = bf16[32,5120]{1,0:T(8,128)(2,1)S(1)} collective-permute-done((bf16[32,5120]{1,0:T(8,128)(2,1)S(1)}, bf16[32,5120]{1,0:T(8,128)(2,1)S(1)}, u32[]{:S(2)}, u32[]{:S(2)}) %collective-permute-start.11) | collective-permute-done | bytes 327712 | tf_op jit(solution)/shard_map/ppermute | solution.py:422
  64.8 4.6 %factor_grads.1 = (bf16[512,256]{1,0:T(8,128)(2,1)S(1)}, bf16[1280,128]{1,0:T(8,128)(2,1)}, bf16[512,4096]{1,0:T(8,128)(2,1)S(1)}) custom-call(s32[32,128]{1,0:T(8,128)S(1)} %bitcast.16, bf16[16,32,256]{2,1,0:T(8,128)(2,1)S(1)} %all_to_all.20.mixed, bf16[924,512]{1,0:T(8,128)(2,1)S(1)} %bitcast.14, ...), custom_call_target="tpu_custom_call" | custom-call | flops 21474836 | bytes 41943 | tf_op jit(solution)/shard_map/factor_grads/pallas_call | solution.py:327
  69.5 2.0 %copy-done = bf16[512,4096]{1,0:T(8,128)(2,1)} copy-done((bf16[512,4096]{1,0:T(8,128)(2,1)}, bf16[512,4096]{1,0:T(8,128)(2,1)S(1)}, u32[]{:S(2)}) %copy-start) | copy-done | bytes 4194328
  72.2 5.3 %all-to-all-start.2 = ((bf16[8,160,128]{2,1,0:T(8,128)(2,1)}), bf16[8,160,128]{2,1,0:T(8,128)(2,1)S(1)}, u32[]{:S(2)}, u32[]{:S(2)}) async-start(bf16[8,160,128]{2,1,0:T(8,128)(2,1)} %bitcast.5), calls=%async_computation.2 | async-start | bytes 655360 | tf_op jit(solution)/shard_map/all_to_all | solution.py:424
  77.5 2.6 %delta_rows.1 = f32[32,4096]{1,0:T(8,128)} custom-call(bf16[16,32,256]{2,1,0:T(8,128)(2,1)} %copy-done.8, bf16[64,5120]{1,0:T(8,128)(2,1)} %copy-done.3, bf16[64,5120]{1,0:T(8,128)(2,1)} %copy-done.1, bf16[64,5120]{1,0:T(8,128)(2,1)} %copy-done.2, bf16[32,5120]{1,0:T(8,128)(2,1)} %copy-done.10, bf16[32,5120]{1,0:T(8,128)(2,1)} %copy-done.11, ...), custom_call_target="tpu_custom_call" | custom-call | flops 335544 | bytes 7864 | tf_op jit(solution)/shard_map/delta_rows/pallas_call | solution.py:262
  80.1 0.9 copy-done.20
  81.0 2.6 %quad_sum.1 = (bf16[32,4096]{1,0:T(8,128)(2,1)}, bf16[32,4096]{1,0:T(8,128)(2,1)}, bf16[32,4096]{1,0:T(8,128)(2,1)}, f32[32,4096]{1,0:T(8,128)}) custom-call(bf16[128,4096]{1,0:T(8,128)(2,1)} %copy-done.14, bf16[128,1536]{1,0:T(8,128)(2,1)} %copy-done.22, bf16[128,2560]{1,0:T(8,128)(2,1)} %copy-done.20), custom_call_target="tpu_custom_call" | custom-call | flops 5242 | bytes 41943 | tf_op jit(solution)/shard_map/quad_sum/pallas_call | solution.py:172
  83.6 1.2 %all-to-all-done.2 = bf16[8,160,128]{2,1,0:T(8,128)(2,1)S(1)} async-done(((bf16[8,160,128]{2,1,0:T(8,128)(2,1)}), bf16[8,160,128]{2,1,0:T(8,128)(2,1)S(1)}, u32[]{:S(2)}, u32[]{:S(2)}) %all-to-all-start.2) | async-done | bytes 327712 | tf_op jit(solution)/shard_map/all_to_all | solution.py:424
  84.9 1.1 %collective-permute-start.13 = (bf16[32,4096]{1,0:T(8,128)(2,1)}, bf16[32,4096]{1,0:T(8,128)(2,1)S(1)}, u32[]{:S(2)}, u32[]{:S(2)}) collective-permute-start(bf16[32,4096]{1,0:T(8,128)(2,1)} %get-tuple-element.83), channel_id=1, source_target_pairs={{0,2},{2,4},{4,6},{6,0},{1,3},{3,5},{5,7},{7,1},{8,10},{10,12},{12... | collective-permute-start | bytes 786440 | tf_op jit(solution)/shard_map/ppermute | solution.py:34
  86.0 2.9 %collective-permute-start.14 = (bf16[32,4096]{1,0:T(8,128)(2,1)}, bf16[32,4096]{1,0:T(8,128)(2,1)S(1)}, u32[]{:S(2)}, u32[]{:S(2)}) collective-permute-start(bf16[32,4096]{1,0:T(8,128)(2,1)} %get-tuple-element.84), channel_id=1, source_target_pairs={{0,4},{2,6},{4,0},{6,2},{1,5},{3,7},{5,1},{7,3},{8,12},{10,14},{12... | collective-permute-start | bytes 786440 | tf_op jit(solution)/shard_map/ppermute | solution.py:34
  89.5 0.8 broadcast_in_dim.28
  90.2 4.6 %all-to-all-start.3 = ((bf16[8,160,128]{2,1,0:T(8,128)(2,1)}), bf16[8,160,128]{2,1,0:T(8,128)(2,1)S(1)}, u32[]{:S(2)}, u32[]{:S(2)}) async-start(bf16[8,160,128]{2,1,0:T(8,128)(2,1)} %broadcast_in_dim.28), calls=%async_computation.3 | async-start | bytes 655360 | tf_op jit(solution)/shard_map/all_to_all | solution.py:39
  94.8 9.1 %token_grads.1 = f32[924,512]{1,0:T(8,128)} custom-call(bf16[924,4096]{1,0:T(8,128)(2,1)} %weight.3, bf16[512,4096]{1,0:T(8,128)(2,1)} %copy-done, bf16[924,128]{1,0:T(8,128)(2,1)} %copy-done.17, bf16[512,256]{1,0:T(8,128)(2,1)} %copy-done.15), custom_call_target="tpu_custom_call" | custom-call | flops 38755368 | bytes 75694 | tf_op jit(solution)/shard_map/token_grads/pallas_call | solution.py:368
  104.0 0.9 convert_add_fusion
  105.0 1.0 copy.16
  (81 shorter events, 6.0 us)
Async XLA Ops:
  2.4 21.2 %collective-permute-start = (bf16[32,5120]{1,0:T(8,128)(2,1)}, bf16[32,5120]{1,0:T(8,128)(2,1)S(1)}, u32[]{:S(2)}, u32[]{:S(2)}) collective-permute-start(bf16[32,5120]{1,0:T(8,128)(2,1)} %pack.1), channel_id=1, source_target_pairs={{0,8},{8,0},{1,9},{9,1},{2,10},{10,2},{3,11},{11,3},{4,12},{12,4},... | collective-permute-start | bytes 983048 | tf_op jit(solution)/shard_map/ppermute | solution.py:396
  9.0 14.6 %all-to-all-start = ((bf16[16,32,256]{2,1,0:T(8,128)(2,1)}), bf16[16,32,256]{2,1,0:T(8,128)(2,1)S(1)}, u32[]{:S(2)}, u32[]{:S(2)}) async-start(bf16[16,32,256]{2,1,0:T(8,128)(2,1)} %bitcast.2), calls=%async_computation | async-start | bytes 524288 | tf_op jit(solution)/shard_map/all_to_all | solution.py:401
  14.9 9.2 %copy-start.19 = (bf16[32,5120]{1,0:T(8,128)(2,1)S(1)}, bf16[32,5120]{1,0:T(8,128)(2,1)}, u32[]{:S(2)}) copy-start(bf16[32,5120]{1,0:T(8,128)(2,1)} %pack.1) | copy-start | bytes 983044
  14.9 12.5 %copy-start.16 = (s32[4096]{0:T(1024)S(1)}, s32[4096]{0:T(1024)}, u32[]{:S(2)}) copy-start(s32[4096]{0:T(1024)} %param.10) | copy-start | bytes 49156
  23.6 7.4 %collective-permute-start.3 = (bf16[256,4096]{1,0:T(8,128)(2,1)}, bf16[256,4096]{1,0:T(8,128)(2,1)S(1)}, u32[]{:S(2)}, u32[]{:S(2)}) collective-permute-start(bf16[256,4096]{1,0:T(8,128)(2,1)} %get-tuple-element.55), channel_id=1, source_target_pairs={{0,1},{1,0},{2,3},{3,2},{4,5},{5,4},{6,7},{7,6},{8,9},{9,8},{10,11... | collective-permute-start | bytes 6291464 | tf_op jit(solution)/shard_map/ppermute | solution.py:408
  24.1 40.7 %copy-start.3 = (bf16[64,5120]{1,0:T(8,128)(2,1)}, bf16[64,5120]{1,0:T(8,128)(2,1)S(1)}, u32[]{:S(2)}) copy-start(bf16[64,5120]{1,0:T(8,128)(2,1)S(1)} %constant_dynamic-update-slice_fusion.refs_0_) | copy-start | bytes 1966084
  24.1 18.2 %collective-permute-start.1 = (bf16[64,5120]{1,0:T(8,128)(2,1)S(1)}, bf16[64,5120]{1,0:T(8,128)(2,1)S(1)}, u32[]{:S(2)}, u32[]{:S(2)}) collective-permute-start(bf16[64,5120]{1,0:T(8,128)(2,1)S(1)} %constant_dynamic-update-slice_fusion.refs_0_), channel_id=1, source_target_pairs={{0,2},{2,4},{4,6},{6,0},{1,3},{3,5},{5,7},{7,1},{8,10},{10,12},{12... | collective-permute-start | bytes 1966088 | tf_op jit(solution)/shard_map/ppermute | solution.py:34
  25.9 16.7 %collective-permute-start.2 = (bf16[64,5120]{1,0:T(8,128)(2,1)S(1)}, bf16[64,5120]{1,0:T(8,128)(2,1)S(1)}, u32[]{:S(2)}, u32[]{:S(2)}) collective-permute-start(bf16[64,5120]{1,0:T(8,128)(2,1)S(1)} %constant_dynamic-update-slice_fusion.refs_0_), channel_id=1, source_target_pairs={{0,6},{2,0},{4,2},{6,4},{1,7},{3,1},{5,3},{7,5},{8,14},{10,8},{12,... | collective-permute-start | bytes 1966088 | tf_op jit(solution)/shard_map/ppermute | solution.py:34
  27.5 15.2 %collective-permute-start.4 = (bf16[64,5120]{1,0:T(8,128)(2,1)S(1)}, bf16[64,5120]{1,0:T(8,128)(2,1)S(1)}, u32[]{:S(2)}, u32[]{:S(2)}) collective-permute-start(bf16[64,5120]{1,0:T(8,128)(2,1)S(1)} %constant_dynamic-update-slice_fusion.refs_0_), channel_id=1, source_target_pairs={{0,1},{1,0},{2,3},{3,2},{4,5},{5,4},{6,7},{7,6},{8,9},{9,8},{10,11... | collective-permute-start | bytes 1966088 | tf_op jit(solution)/shard_map/ppermute | solution.py:409
  31.0 18.6 %copy-start.8 = (bf16[16,32,256]{2,1,0:T(8,128)(2,1)}, bf16[16,32,256]{2,1,0:T(8,128)(2,1)S(1)}, u32[]{:S(2)}) copy-start(bf16[16,32,256]{2,1,0:T(8,128)(2,1)S(1)} %reorder.1.mixed) | copy-start | bytes 786436
  34.1 30.8 %copy-start.14 = (bf16[128,4096]{1,0:T(8,128)(2,1)}, bf16[128,4096]{1,0:T(8,128)(2,1)S(1)}, u32[]{:S(2)}) copy-start(bf16[128,4096]{1,0:T(8,128)(2,1)S(1)} %get-tuple-element.59.kept) | copy-start | bytes 3145732
  42.4 27.1 %copy-start.1 = (bf16[64,5120]{1,0:T(8,128)(2,1)}, bf16[64,5120]{1,0:T(8,128)(2,1)S(1)}, u32[]{:S(2)}) copy-start(bf16[64,5120]{1,0:T(8,128)(2,1)S(1)} %collective-permute-done.1.refs_1_) | copy-start | bytes 1966084
  42.6 26.8 %copy-start.2 = (bf16[64,5120]{1,0:T(8,128)(2,1)}, bf16[64,5120]{1,0:T(8,128)(2,1)S(1)}, u32[]{:S(2)}) copy-start(bf16[64,5120]{1,0:T(8,128)(2,1)S(1)} %collective-permute-done.2.refs_2_) | copy-start | bytes 1966084
  42.6 26.8 %copy-start.5 = (bf16[64,5120]{1,0:T(8,128)(2,1)}, bf16[64,5120]{1,0:T(8,128)(2,1)S(1)}, u32[]{:S(2)}) copy-start(bf16[64,5120]{1,0:T(8,128)(2,1)S(1)} %collective-permute-done.4.refs_5_) | copy-start | bytes 1966084
  42.6 19.3 %collective-permute-start.7 = (bf16[64,5120]{1,0:T(8,128)(2,1)S(1)}, bf16[64,5120]{1,0:T(8,128)(2,1)S(1)}, u32[]{:S(2)}, u32[]{:S(2)}) collective-permute-start(bf16[64,5120]{1,0:T(8,128)(2,1)S(1)} %collective-permute-done.1.refs_1_), channel_id=1, source_target_pairs={{0,1},{1,0},{2,3},{3,2},{4,5},{5,4},{6,7},{7,6},{8,9},{9,8},{10,11... | collective-permute-start | bytes 1966088 | tf_op jit(solution)/shard_map/ppermute | solution.py:416
  42.7 19.2 %collective-permute-start.8 = (bf16[64,5120]{1,0:T(8,128)(2,1)S(1)}, bf16[64,5120]{1,0:T(8,128)(2,1)S(1)}, u32[]{:S(2)}, u32[]{:S(2)}) collective-permute-start(bf16[64,5120]{1,0:T(8,128)(2,1)S(1)} %collective-permute-done.2.refs_2_), channel_id=1, source_target_pairs={{0,1},{1,0},{2,3},{3,2},{4,5},{5,4},{6,7},{7,6},{8,9},{9,8},{10,11... | collective-permute-start | bytes 1966088 | tf_op jit(solution)/shard_map/ppermute | solution.py:416
  43.2 18.7 %collective-permute-start.9 = (bf16[128,1536]{1,0:T(8,128)(2,1)S(1)}, bf16[128,1536]{1,0:T(8,128)(2,1)S(1)}, u32[]{:S(2)}, u32[]{:S(2)}) collective-permute-start(bf16[128,1536]{1,0:T(8,128)(2,1)S(1)} %get-tuple-element.63), channel_id=1, source_target_pairs={{0,8},{8,0},{1,9},{9,1},{2,10},{10,2},{3,11},{11,3},{4,12},{12,4},... | collective-permute-start | bytes 1179656 | tf_op jit(solution)/shard_map/ppermute | solution.py:418
  46.3 15.6 %collective-permute-start.5 = (bf16[32,5120]{1,0:T(8,128)(2,1)S(1)}, bf16[32,5120]{1,0:T(8,128)(2,1)S(1)}, u32[]{:S(2)}, u32[]{:S(2)}) collective-permute-start(bf16[32,5120]{1,0:T(8,128)(2,1)S(1)} %slice.15), channel_id=1, source_target_pairs={{0,2},{2,4},{4,6},{6,0},{1,3},{3,5},{5,7},{7,1},{8,10},{10,12},{12... | collective-permute-start | bytes 983048 | tf_op jit(solution)/shard_map/ppermute | solution.py:34
  47.8 14.1 %collective-permute-start.6 = (bf16[32,5120]{1,0:T(8,128)(2,1)S(1)}, bf16[32,5120]{1,0:T(8,128)(2,1)S(1)}, u32[]{:S(2)}, u32[]{:S(2)}) collective-permute-start(bf16[32,5120]{1,0:T(8,128)(2,1)S(1)} %slice.16), channel_id=1, source_target_pairs={{0,6},{2,0},{4,2},{6,4},{1,7},{3,1},{5,3},{7,5},{8,14},{10,8},{12,... | collective-permute-start | bytes 983048 | tf_op jit(solution)/shard_map/ppermute | solution.py:34
  61.9 7.6 %copy-start.10 = (bf16[32,5120]{1,0:T(8,128)(2,1)}, bf16[32,5120]{1,0:T(8,128)(2,1)S(1)}, u32[]{:S(2)}) copy-start(bf16[32,5120]{1,0:T(8,128)(2,1)S(1)} %collective-permute-done.5.refs_3_) | copy-start | bytes 983044
  61.9 7.6 %copy-start.11 = (bf16[32,5120]{1,0:T(8,128)(2,1)}, bf16[32,5120]{1,0:T(8,128)(2,1)S(1)}, u32[]{:S(2)}) copy-start(bf16[32,5120]{1,0:T(8,128)(2,1)S(1)} %collective-permute-done.6.refs_4_) | copy-start | bytes 983044
  61.9 7.6 %copy-start.22 = (bf16[128,1536]{1,0:T(8,128)(2,1)}, bf16[128,1536]{1,0:T(8,128)(2,1)S(1)}, u32[]{:S(2)}) copy-start(bf16[128,1536]{1,0:T(8,128)(2,1)S(1)} %collective-permute-done.9.left) | copy-start | bytes 1179652
  61.9 18.2 %collective-permute-start.10 = (bf16[128,2560]{1,0:T(8,128)(2,1)S(1)}, bf16[128,2560]{1,0:T(8,128)(2,1)S(1)}, u32[]{:S(2)}, u32[]{:S(2)}) collective-permute-start(bf16[128,2560]{1,0:T(8,128)(2,1)S(1)} %get-tuple-element.67), channel_id=1, source_target_pairs={{0,8},{8,0},{1,9},{9,1},{2,10},{10,2},{3,11},{11,3},{4,12},{12,4},... | collective-permute-start | bytes 1966088 | tf_op jit(solution)/shard_map/ppermute | solution.py:421
  62.6 1.7 %collective-permute-start.11 = (bf16[32,5120]{1,0:T(8,128)(2,1)S(1)}, bf16[32,5120]{1,0:T(8,128)(2,1)S(1)}, u32[]{:S(2)}, u32[]{:S(2)}) collective-permute-start(bf16[32,5120]{1,0:T(8,128)(2,1)S(1)} %collective-permute-done.5.refs_3_), channel_id=1, source_target_pairs={{0,1},{1,0},{2,3},{3,2},{4,5},{5,4},{6,7},{7,6},{8,9},{9,8},{10,11... | collective-permute-start | bytes 983048 | tf_op jit(solution)/shard_map/ppermute | solution.py:422
  63.1 1.7 %collective-permute-start.12 = (bf16[32,5120]{1,0:T(8,128)(2,1)S(1)}, bf16[32,5120]{1,0:T(8,128)(2,1)S(1)}, u32[]{:S(2)}, u32[]{:S(2)}) collective-permute-start(bf16[32,5120]{1,0:T(8,128)(2,1)S(1)} %collective-permute-done.6.refs_4_), channel_id=1, source_target_pairs={{0,1},{1,0},{2,3},{3,2},{4,5},{5,4},{6,7},{7,6},{8,9},{9,8},{10,11... | collective-permute-start | bytes 983048 | tf_op jit(solution)/shard_map/ppermute | solution.py:422
  72.2 12.6 %all-to-all-start.2 = ((bf16[8,160,128]{2,1,0:T(8,128)(2,1)}), bf16[8,160,128]{2,1,0:T(8,128)(2,1)S(1)}, u32[]{:S(2)}, u32[]{:S(2)}) async-start(bf16[8,160,128]{2,1,0:T(8,128)(2,1)} %bitcast.5), calls=%async_computation.2 | async-start | bytes 655360 | tf_op jit(solution)/shard_map/all_to_all | solution.py:424
  84.9 19.1 %collective-permute-start.13 = (bf16[32,4096]{1,0:T(8,128)(2,1)}, bf16[32,4096]{1,0:T(8,128)(2,1)S(1)}, u32[]{:S(2)}, u32[]{:S(2)}) collective-permute-start(bf16[32,4096]{1,0:T(8,128)(2,1)} %get-tuple-element.83), channel_id=1, source_target_pairs={{0,2},{2,4},{4,6},{6,0},{1,3},{3,5},{5,7},{7,1},{8,10},{10,12},{12... | collective-permute-start | bytes 786440 | tf_op jit(solution)/shard_map/ppermute | solution.py:34
  86.0 17.9 %collective-permute-start.14 = (bf16[32,4096]{1,0:T(8,128)(2,1)}, bf16[32,4096]{1,0:T(8,128)(2,1)S(1)}, u32[]{:S(2)}, u32[]{:S(2)}) collective-permute-start(bf16[32,4096]{1,0:T(8,128)(2,1)} %get-tuple-element.84), channel_id=1, source_target_pairs={{0,4},{2,6},{4,0},{6,2},{1,5},{3,7},{5,1},{7,3},{8,12},{10,14},{12... | collective-permute-start | bytes 786440 | tf_op jit(solution)/shard_map/ppermute | solution.py:34
  89.0 15.0 %collective-permute-start.15 = (bf16[32,4096]{1,0:T(8,128)(2,1)}, bf16[32,4096]{1,0:T(8,128)(2,1)S(1)}, u32[]{:S(2)}, u32[]{:S(2)}) collective-permute-start(bf16[32,4096]{1,0:T(8,128)(2,1)} %get-tuple-element.85), channel_id=1, source_target_pairs={{0,6},{2,0},{4,2},{6,4},{1,7},{3,1},{5,3},{7,5},{8,14},{10,8},{12,... | collective-permute-start | bytes 786440 | tf_op jit(solution)/shard_map/ppermute | solution.py:34
  90.2 14.7 %all-to-all-start.3 = ((bf16[8,160,128]{2,1,0:T(8,128)(2,1)}), bf16[8,160,128]{2,1,0:T(8,128)(2,1)S(1)}, u32[]{:S(2)}, u32[]{:S(2)}) async-start(bf16[8,160,128]{2,1,0:T(8,128)(2,1)} %broadcast_in_dim.28), calls=%async_computation.3 | async-start | bytes 655360 | tf_op jit(solution)/shard_map/all_to_all | solution.py:39
  94.8 9.1 %copy-start.18 = (f32[32,4096]{1,0:T(8,128)S(1)}, f32[32,4096]{1,0:T(8,128)}, u32[]{:S(2)}) copy-start(f32[32,4096]{1,0:T(8,128)} %delta_rows.1) | copy-start | bytes 1572868
  94.8 9.1 %copy-start.21 = (f32[32,4096]{1,0:T(8,128)S(1)}, f32[32,4096]{1,0:T(8,128)}, u32[]{:S(2)}) copy-start(f32[32,4096]{1,0:T(8,128)} %get-tuple-element.81) | copy-start | bytes 1572868
  (10 other events, 44.9 us)

commit v7 on v6

--- a/solution.py
+++ b/solution.py
@@ -94,7 +94,7 @@
     own[...] = total[half:].astype(own.dtype)
 
 
-def call_base_rows(tokens, weight, tile=1024):
+def call_base_rows(tokens, weight, tile=2048):
     rows, hidden = tokens.shape
     width = weight.shape[1]
     half = rows // 2

time: 107 us -> 107 us (level)
  no operation moved by 1% of the time
where the time goes in v7:
time: 107 us
  starting transfers between devices  34.8 us (33%)
  Pallas kernels  34.1 us (32%)
  blocking collectives  12.3 us (11%)
  waiting for transfers between devices  11.5 us (11%)
  local copies, waits for them, and re-layouts  10.4 us (10%)
  other arithmetic  1.99 us (2%)
    all_to_all x1, blocking collectives, per_device(): mixed_mine = lax.all_to_all(mixed, TENSOR, 0, 0)  12.3 us
    ppermute x7, starting transfers between devices, turn(): return lax.ppermute(value, 'y', [(i, (i + by) % 4) for i in range(4)])  11.2 us
    pallas_call x1, Pallas kernels, call_token_grads(): pl.pallas_call(token_grads, grid=(width // tile,), in_specs=[pl.BlockSpec...  9.09 us
    unnamed x50, local copies, waits for them, and re-layouts  8.65 us
    ppermute x7, waiting for transfers between devices, turn(): return lax.ppermute(value, 'y', [(i, (i + by) % 4) for i in range(4)])  8.54 us
    pallas_call x1, Pallas kernels, call_base_rows(): pl.pallas_call(base_rows, grid=(width // tile,), in_specs=[pl.BlockSpec((...  8.53 us
    all_to_all x1, starting transfers between devices, per_device(): sums = lax.all_to_all(sums.reshape(8, -1, block_out), DP, 0, 0)  5.3 us
    all_to_all x1, starting transfers between devices, spread(): return lax.all_to_all(whole, axes, 0, 0)  4.6 us
  transfers between devices with their start and end apart: 19, of which 5 were waited for; matrix products, arithmetic and copies ran while one was open for 5% of the time, Pallas kernels for 30%

profile of v7, /device:TPU:2, one launch (start us, length us, event | category | flops | bytes accessed | tf_op | source)
XLA Modules:
  0.0 106.6 jit_solution(2452188237519051033)
XLA Ops:
  0.6 1.8 %pack.1 = bf16[32,5120]{1,0:T(8,128)(2,1)} custom-call(bf16[32,4096]{1,0:T(8,128)(2,1)} %cotangent.1, bf16[256,128]{1,0:T(8,128)(2,1)} %bitcast.20), custom_call_target="tpu_custom_call" | custom-call | bytes 5242 | tf_op jit(solution)/shard_map/pack/pallas_call | solution.py:64
  2.4 3.9 %collective-permute-start = (bf16[32,5120]{1,0:T(8,128)(2,1)}, bf16[32,5120]{1,0:T(8,128)(2,1)S(1)}, u32[]{:S(2)}, u32[]{:S(2)}) collective-permute-start(bf16[32,5120]{1,0:T(8,128)(2,1)} %pack.1), channel_id=1, source_target_pairs={{0,8},{8,0},{1,9},{9,1},{2,10},{10,2},{3,11},{11,3},{4,12},{12,4},... | collective-permute-start | bytes 983048 | tf_op jit(solution)/shard_map/ppermute | solution.py:396
  6.3 1.0 copy.13
  8.2 0.8 copy.14
  9.0 4.6 %all-to-all-start = ((bf16[16,32,256]{2,1,0:T(8,128)(2,1)}), bf16[16,32,256]{2,1,0:T(8,128)(2,1)S(1)}, u32[]{:S(2)}, u32[]{:S(2)}) async-start(bf16[16,32,256]{2,1,0:T(8,128)(2,1)} %bitcast.2), calls=%async_computation | async-start | bytes 524288 | tf_op jit(solution)/shard_map/all_to_all | solution.py:401
  13.6 1.3 %copy.15.tokens = bf16[512,924]{1,0:T(8,128)(2,1)} copy(bf16[512,924]{0,1:T(8,128)(2,1)S(1)} %copy-done.4) | data formatting | bytes 1892352 | tf_op args[0]
  14.9 8.5 %base_rows.1 = (bf16[256,4096]{1,0:T(8,128)(2,1)}, bf16[256,4096]{1,0:T(8,128)(2,1)}) custom-call(bf16[512,924]{1,0:T(8,128)(2,1)} %copy.15.tokens, bf16[924,4096]{1,0:T(8,128)(2,1)} %weight.3), custom_call_target="tpu_custom_call" | custom-call | flops 38755368 | bytes 75694 | tf_op jit(solution)/shard_map/base_rows/pallas_call | solution.py:101
  24.0 1.7 %collective-permute-start.1 = (bf16[64,5120]{1,0:T(8,128)(2,1)S(1)}, bf16[64,5120]{1,0:T(8,128)(2,1)S(1)}, u32[]{:S(2)}, u32[]{:S(2)}) collective-permute-start(bf16[64,5120]{1,0:T(8,128)(2,1)S(1)} %constant_dynamic-update-slice_fusion.refs_0_), channel_id=1, source_target_pairs={{0,2},{2,4},{4,6},{6,0},{1,3},{3,5},{5,7},{7,1},{8,10},{10,12},{12... | collective-permute-start | bytes 1966088 | tf_op jit(solution)/shard_map/ppermute | solution.py:34
  25.8 1.6 %collective-permute-start.2 = (bf16[64,5120]{1,0:T(8,128)(2,1)S(1)}, bf16[64,5120]{1,0:T(8,128)(2,1)S(1)}, u32[]{:S(2)}, u32[]{:S(2)}) collective-permute-start(bf16[64,5120]{1,0:T(8,128)(2,1)S(1)} %constant_dynamic-update-slice_fusion.refs_0_), channel_id=1, source_target_pairs={{0,6},{2,0},{4,2},{6,4},{1,7},{3,1},{5,3},{7,5},{8,14},{10,8},{12,... | collective-permute-start | bytes 1966088 | tf_op jit(solution)/shard_map/ppermute | solution.py:34
  27.3 3.5 %reorder.1.mixed = bf16[16,32,256]{2,1,0:T(8,128)(2,1)S(1)} custom-call(s32[32,128]{1,0:T(8,128)S(1)} %bitcast.15, bf16[16,32,256]{2,1,0:T(8,128)(2,1)S(1)} %all-to-all-done.inner), custom_call_target="tpu_custom_call" | custom-call | flops 167772 | bytes 5242 | tf_op jit(solution)/shard_map/reorder/pallas_call | solution.py:213
  30.9 1.7 %copy-done.9 = bf16[256,4096]{1,0:T(8,128)(2,1)S(1)} copy-done((bf16[256,4096]{1,0:T(8,128)(2,1)S(1)}, bf16[256,4096]{1,0:T(8,128)(2,1)}, u32[]{:S(2)}) %copy-start.9) | copy-done | bytes 2097176
  32.6 1.4 %pair_sum.1 = (bf16[128,1536]{1,0:T(8,128)(2,1)S(1)}, bf16[128,2560]{1,0:T(8,128)(2,1)S(1)}, bf16[128,4096]{1,0:T(8,128)(2,1)S(1)}) custom-call(bf16[256,4096]{1,0:T(8,128)(2,1)S(1)} %copy-done.9, bf16[256,4096]{1,0:T(8,128)(2,1)S(1)} %collective-permute-done.3.got), custom_call_target="tpu_custom_call" | custom-call | flops 10485 | bytes 62914 | tf_op jit(solution)/shard_map/pair_sum/pallas_call | solution.py:139
  33.9 8.3 %collective-permute-done.1.refs_1_ = bf16[64,5120]{1,0:T(8,128)(2,1)S(1)} collective-permute-done((bf16[64,5120]{1,0:T(8,128)(2,1)S(1)}, bf16[64,5120]{1,0:T(8,128)(2,1)S(1)}, u32[]{:S(2)}, u32[]{:S(2)}) %collective-permute-start.1) | collective-permute-done | bytes 655392 | tf_op jit(solution)/shard_map/ppermute | solution.py:34
  43.1 3.0 %collective-permute-start.9 = (bf16[128,1536]{1,0:T(8,128)(2,1)S(1)}, bf16[128,1536]{1,0:T(8,128)(2,1)S(1)}, u32[]{:S(2)}, u32[]{:S(2)}) collective-permute-start(bf16[128,1536]{1,0:T(8,128)(2,1)S(1)} %get-tuple-element.63), channel_id=1, source_target_pairs={{0,8},{8,0},{1,9},{9,1},{2,10},{10,2},{3,11},{11,3},{4,12},{12,4},... | collective-permute-start | bytes 1179656 | tf_op jit(solution)/shard_map/ppermute | solution.py:418
  46.1 1.5 %collective-permute-start.5 = (bf16[32,5120]{1,0:T(8,128)(2,1)S(1)}, bf16[32,5120]{1,0:T(8,128)(2,1)S(1)}, u32[]{:S(2)}, u32[]{:S(2)}) collective-permute-start(bf16[32,5120]{1,0:T(8,128)(2,1)S(1)} %slice.15), channel_id=1, source_target_pairs={{0,2},{2,4},{4,6},{6,0},{1,3},{3,5},{5,7},{7,1},{8,10},{10,12},{12... | collective-permute-start | bytes 983048 | tf_op jit(solution)/shard_map/ppermute | solution.py:34
  47.6 1.8 %collective-permute-start.6 = (bf16[32,5120]{1,0:T(8,128)(2,1)S(1)}, bf16[32,5120]{1,0:T(8,128)(2,1)S(1)}, u32[]{:S(2)}, u32[]{:S(2)}) collective-permute-start(bf16[32,5120]{1,0:T(8,128)(2,1)S(1)} %slice.16), channel_id=1, source_target_pairs={{0,6},{2,0},{4,2},{6,4},{1,7},{3,1},{5,3},{7,5},{8,14},{10,8},{12,... | collective-permute-start | bytes 983048 | tf_op jit(solution)/shard_map/ppermute | solution.py:34
  49.4 12.3 %all_to_all.20.mixed = bf16[16,32,256]{2,1,0:T(8,128)(2,1)S(1)} all-to-all(bf16[16,32,256]{2,1,0:T(8,128)(2,1)S(1)} %reorder.1.mixed), channel_id=1, replica_groups=mesh['zl'=2,'x'=4,'zh'=2,'y'=4,'c'=2] {'zh','y','c'}, dimensions={0} | all-to-all | bytes 524288 | tf_op jit(solution)/shard_map/all_to_all | solution.py:417
  63.0 1.2 %collective-permute-done.11.refs_8_ = bf16[32,5120]{1,0:T(8,128)(2,1)S(1)} collective-permute-done((bf16[32,5120]{1,0:T(8,128)(2,1)S(1)}, bf16[32,5120]{1,0:T(8,128)(2,1)S(1)}, u32[]{:S(2)}, u32[]{:S(2)}) %collective-permute-start.11) | collective-permute-done | bytes 327712 | tf_op jit(solution)/shard_map/ppermute | solution.py:422
  64.7 4.6 %factor_grads.1 = (bf16[512,256]{1,0:T(8,128)(2,1)S(1)}, bf16[1280,128]{1,0:T(8,128)(2,1)}, bf16[512,4096]{1,0:T(8,128)(2,1)S(1)}) custom-call(s32[32,128]{1,0:T(8,128)S(1)} %bitcast.16, bf16[16,32,256]{2,1,0:T(8,128)(2,1)S(1)} %all_to_all.20.mixed, bf16[924,512]{1,0:T(8,128)(2,1)S(1)} %bitcast.14, ...), custom_call_target="tpu_custom_call" | custom-call | flops 21474836 | bytes 41943 | tf_op jit(solution)/shard_map/factor_grads/pallas_call | solution.py:327
  69.4 2.0 %copy-done = bf16[512,4096]{1,0:T(8,128)(2,1)} copy-done((bf16[512,4096]{1,0:T(8,128)(2,1)}, bf16[512,4096]{1,0:T(8,128)(2,1)S(1)}, u32[]{:S(2)}) %copy-start) | copy-done | bytes 4194328
  72.1 5.3 %all-to-all-start.2 = ((bf16[8,160,128]{2,1,0:T(8,128)(2,1)}), bf16[8,160,128]{2,1,0:T(8,128)(2,1)S(1)}, u32[]{:S(2)}, u32[]{:S(2)}) async-start(bf16[8,160,128]{2,1,0:T(8,128)(2,1)} %bitcast.5), calls=%async_computation.2 | async-start | bytes 655360 | tf_op jit(solution)/shard_map/all_to_all | solution.py:424
  77.4 2.6 %delta_rows.1 = f32[32,4096]{1,0:T(8,128)} custom-call(bf16[16,32,256]{2,1,0:T(8,128)(2,1)} %copy-done.8, bf16[64,5120]{1,0:T(8,128)(2,1)} %copy-done.3, bf16[64,5120]{1,0:T(8,128)(2,1)} %copy-done.1, bf16[64,5120]{1,0:T(8,128)(2,1)} %copy-done.2, bf16[32,5120]{1,0:T(8,128)(2,1)} %copy-done.10, bf16[32,5120]{1,0:T(8,128)(2,1)} %copy-done.11, ...), custom_call_target="tpu_custom_call" | custom-call | flops 335544 | bytes 7864 | tf_op jit(solution)/shard_map/delta_rows/pallas_call | solution.py:262
  80.0 0.9 copy-done.20
  80.9 2.6 %quad_sum.1 = (bf16[32,4096]{1,0:T(8,128)(2,1)}, bf16[32,4096]{1,0:T(8,128)(2,1)}, bf16[32,4096]{1,0:T(8,128)(2,1)}, f32[32,4096]{1,0:T(8,128)}) custom-call(bf16[128,4096]{1,0:T(8,128)(2,1)} %copy-done.14, bf16[128,1536]{1,0:T(8,128)(2,1)} %copy-done.22, bf16[128,2560]{1,0:T(8,128)(2,1)} %copy-done.20), custom_call_target="tpu_custom_call" | custom-call | flops 5242 | bytes 41943 | tf_op jit(solution)/shard_map/quad_sum/pallas_call | solution.py:172
  83.5 1.2 %all-to-all-done.2 = bf16[8,160,128]{2,1,0:T(8,128)(2,1)S(1)} async-done(((bf16[8,160,128]{2,1,0:T(8,128)(2,1)}), bf16[8,160,128]{2,1,0:T(8,128)(2,1)S(1)}, u32[]{:S(2)}, u32[]{:S(2)}) %all-to-all-start.2) | async-done | bytes 327712 | tf_op jit(solution)/shard_map/all_to_all | solution.py:424
  84.7 1.1 %collective-permute-start.13 = (bf16[32,4096]{1,0:T(8,128)(2,1)}, bf16[32,4096]{1,0:T(8,128)(2,1)S(1)}, u32[]{:S(2)}, u32[]{:S(2)}) collective-permute-start(bf16[32,4096]{1,0:T(8,128)(2,1)} %get-tuple-element.83), channel_id=1, source_target_pairs={{0,2},{2,4},{4,6},{6,0},{1,3},{3,5},{5,7},{7,1},{8,10},{10,12},{12... | collective-permute-start | bytes 786440 | tf_op jit(solution)/shard_map/ppermute | solution.py:34
  85.9 3.0 %collective-permute-start.14 = (bf16[32,4096]{1,0:T(8,128)(2,1)}, bf16[32,4096]{1,0:T(8,128)(2,1)S(1)}, u32[]{:S(2)}, u32[]{:S(2)}) collective-permute-start(bf16[32,4096]{1,0:T(8,128)(2,1)} %get-tuple-element.84), channel_id=1, source_target_pairs={{0,4},{2,6},{4,0},{6,2},{1,5},{3,7},{5,1},{7,3},{8,12},{10,14},{12... | collective-permute-start | bytes 786440 | tf_op jit(solution)/shard_map/ppermute | solution.py:34
  89.3 0.8 broadcast_in_dim.28
  90.1 4.6 %all-to-all-start.3 = ((bf16[8,160,128]{2,1,0:T(8,128)(2,1)}), bf16[8,160,128]{2,1,0:T(8,128)(2,1)S(1)}, u32[]{:S(2)}, u32[]{:S(2)}) async-start(bf16[8,160,128]{2,1,0:T(8,128)(2,1)} %broadcast_in_dim.28), calls=%async_computation.3 | async-start | bytes 655360 | tf_op jit(solution)/shard_map/all_to_all | solution.py:39
  94.7 9.1 %token_grads.1 = f32[924,512]{1,0:T(8,128)} custom-call(bf16[924,4096]{1,0:T(8,128)(2,1)} %weight.3, bf16[512,4096]{1,0:T(8,128)(2,1)} %copy-done, bf16[924,128]{1,0:T(8,128)(2,1)} %copy-done.17, bf16[512,256]{1,0:T(8,128)(2,1)} %copy-done.15), custom_call_target="tpu_custom_call" | custom-call | flops 38755368 | bytes 75694 | tf_op jit(solution)/shard_map/token_grads/pallas_call | solution.py:368
  103.8 0.9 convert_add_fusion
  104.9 1.0 copy.16
  (81 shorter events, 6.0 us)
Async XLA Ops:
  2.4 21.0 %collective-permute-start = (bf16[32,5120]{1,0:T(8,128)(2,1)}, bf16[32,5120]{1,0:T(8,128)(2,1)S(1)}, u32[]{:S(2)}, u32[]{:S(2)}) collective-permute-start(bf16[32,5120]{1,0:T(8,128)(2,1)} %pack.1), channel_id=1, source_target_pairs={{0,8},{8,0},{1,9},{9,1},{2,10},{10,2},{3,11},{11,3},{4,12},{12,4},... | collective-permute-start | bytes 983048 | tf_op jit(solution)/shard_map/ppermute | solution.py:396
  9.0 14.4 %all-to-all-start = ((bf16[16,32,256]{2,1,0:T(8,128)(2,1)}), bf16[16,32,256]{2,1,0:T(8,128)(2,1)S(1)}, u32[]{:S(2)}, u32[]{:S(2)}) async-start(bf16[16,32,256]{2,1,0:T(8,128)(2,1)} %bitcast.2), calls=%async_computation | async-start | bytes 524288 | tf_op jit(solution)/shard_map/all_to_all | solution.py:401
  14.9 9.0 %copy-start.19 = (bf16[32,5120]{1,0:T(8,128)(2,1)S(1)}, bf16[32,5120]{1,0:T(8,128)(2,1)}, u32[]{:S(2)}) copy-start(bf16[32,5120]{1,0:T(8,128)(2,1)} %pack.1) | copy-start | bytes 983044
  14.9 12.4 %copy-start.16 = (s32[4096]{0:T(1024)S(1)}, s32[4096]{0:T(1024)}, u32[]{:S(2)}) copy-start(s32[4096]{0:T(1024)} %param.10) | copy-start | bytes 49156
  23.5 7.4 %collective-permute-start.3 = (bf16[256,4096]{1,0:T(8,128)(2,1)}, bf16[256,4096]{1,0:T(8,128)(2,1)S(1)}, u32[]{:S(2)}, u32[]{:S(2)}) collective-permute-start(bf16[256,4096]{1,0:T(8,128)(2,1)} %get-tuple-element.55), channel_id=1, source_target_pairs={{0,1},{1,0},{2,3},{3,2},{4,5},{5,4},{6,7},{7,6},{8,9},{9,8},{10,11... | collective-permute-start | bytes 6291464 | tf_op jit(solution)/shard_map/ppermute | solution.py:408
  24.0 40.7 %copy-start.3 = (bf16[64,5120]{1,0:T(8,128)(2,1)}, bf16[64,5120]{1,0:T(8,128)(2,1)S(1)}, u32[]{:S(2)}) copy-start(bf16[64,5120]{1,0:T(8,128)(2,1)S(1)} %constant_dynamic-update-slice_fusion.refs_0_) | copy-start | bytes 1966084
  24.0 18.2 %collective-permute-start.1 = (bf16[64,5120]{1,0:T(8,128)(2,1)S(1)}, bf16[64,5120]{1,0:T(8,128)(2,1)S(1)}, u32[]{:S(2)}, u32[]{:S(2)}) collective-permute-start(bf16[64,5120]{1,0:T(8,128)(2,1)S(1)} %constant_dynamic-update-slice_fusion.refs_0_), channel_id=1, source_target_pairs={{0,2},{2,4},{4,6},{6,0},{1,3},{3,5},{5,7},{7,1},{8,10},{10,12},{12... | collective-permute-start | bytes 1966088 | tf_op jit(solution)/shard_map/ppermute | solution.py:34
  25.8 16.7 %collective-permute-start.2 = (bf16[64,5120]{1,0:T(8,128)(2,1)S(1)}, bf16[64,5120]{1,0:T(8,128)(2,1)S(1)}, u32[]{:S(2)}, u32[]{:S(2)}) collective-permute-start(bf16[64,5120]{1,0:T(8,128)(2,1)S(1)} %constant_dynamic-update-slice_fusion.refs_0_), channel_id=1, source_target_pairs={{0,6},{2,0},{4,2},{6,4},{1,7},{3,1},{5,3},{7,5},{8,14},{10,8},{12,... | collective-permute-start | bytes 1966088 | tf_op jit(solution)/shard_map/ppermute | solution.py:34
  27.3 15.2 %collective-permute-start.4 = (bf16[64,5120]{1,0:T(8,128)(2,1)S(1)}, bf16[64,5120]{1,0:T(8,128)(2,1)S(1)}, u32[]{:S(2)}, u32[]{:S(2)}) collective-permute-start(bf16[64,5120]{1,0:T(8,128)(2,1)S(1)} %constant_dynamic-update-slice_fusion.refs_0_), channel_id=1, source_target_pairs={{0,1},{1,0},{2,3},{3,2},{4,5},{5,4},{6,7},{7,6},{8,9},{9,8},{10,11... | collective-permute-start | bytes 1966088 | tf_op jit(solution)/shard_map/ppermute | solution.py:409
  30.9 18.6 %copy-start.8 = (bf16[16,32,256]{2,1,0:T(8,128)(2,1)}, bf16[16,32,256]{2,1,0:T(8,128)(2,1)S(1)}, u32[]{:S(2)}) copy-start(bf16[16,32,256]{2,1,0:T(8,128)(2,1)S(1)} %reorder.1.mixed) | copy-start | bytes 786436
  33.9 30.8 %copy-start.14 = (bf16[128,4096]{1,0:T(8,128)(2,1)}, bf16[128,4096]{1,0:T(8,128)(2,1)S(1)}, u32[]{:S(2)}) copy-start(bf16[128,4096]{1,0:T(8,128)(2,1)S(1)} %get-tuple-element.59.kept) | copy-start | bytes 3145732
  42.2 27.1 %copy-start.1 = (bf16[64,5120]{1,0:T(8,128)(2,1)}, bf16[64,5120]{1,0:T(8,128)(2,1)S(1)}, u32[]{:S(2)}) copy-start(bf16[64,5120]{1,0:T(8,128)(2,1)S(1)} %collective-permute-done.1.refs_1_) | copy-start | bytes 1966084
  42.5 26.8 %copy-start.2 = (bf16[64,5120]{1,0:T(8,128)(2,1)}, bf16[64,5120]{1,0:T(8,128)(2,1)S(1)}, u32[]{:S(2)}) copy-start(bf16[64,5120]{1,0:T(8,128)(2,1)S(1)} %collective-permute-done.2.refs_2_) | copy-start | bytes 1966084
  42.5 26.8 %copy-start.5 = (bf16[64,5120]{1,0:T(8,128)(2,1)}, bf16[64,5120]{1,0:T(8,128)(2,1)S(1)}, u32[]{:S(2)}) copy-start(bf16[64,5120]{1,0:T(8,128)(2,1)S(1)} %collective-permute-done.4.refs_5_) | copy-start | bytes 1966084
  42.5 19.3 %collective-permute-start.7 = (bf16[64,5120]{1,0:T(8,128)(2,1)S(1)}, bf16[64,5120]{1,0:T(8,128)(2,1)S(1)}, u32[]{:S(2)}, u32[]{:S(2)}) collective-permute-start(bf16[64,5120]{1,0:T(8,128)(2,1)S(1)} %collective-permute-done.1.refs_1_), channel_id=1, source_target_pairs={{0,1},{1,0},{2,3},{3,2},{4,5},{5,4},{6,7},{7,6},{8,9},{9,8},{10,11... | collective-permute-start | bytes 1966088 | tf_op jit(solution)/shard_map/ppermute | solution.py:416
  42.6 19.2 %collective-permute-start.8 = (bf16[64,5120]{1,0:T(8,128)(2,1)S(1)}, bf16[64,5120]{1,0:T(8,128)(2,1)S(1)}, u32[]{:S(2)}, u32[]{:S(2)}) collective-permute-start(bf16[64,5120]{1,0:T(8,128)(2,1)S(1)} %collective-permute-done.2.refs_2_), channel_id=1, source_target_pairs={{0,1},{1,0},{2,3},{3,2},{4,5},{5,4},{6,7},{7,6},{8,9},{9,8},{10,11... | collective-permute-start | bytes 1966088 | tf_op jit(solution)/shard_map/ppermute | solution.py:416
  43.1 18.7 %collective-permute-start.9 = (bf16[128,1536]{1,0:T(8,128)(2,1)S(1)}, bf16[128,1536]{1,0:T(8,128)(2,1)S(1)}, u32[]{:S(2)}, u32[]{:S(2)}) collective-permute-start(bf16[128,1536]{1,0:T(8,128)(2,1)S(1)} %get-tuple-element.63), channel_id=1, source_target_pairs={{0,8},{8,0},{1,9},{9,1},{2,10},{10,2},{3,11},{11,3},{4,12},{12,4},... | collective-permute-start | bytes 1179656 | tf_op jit(solution)/shard_map/ppermute | solution.py:418
  46.1 15.6 %collective-permute-start.5 = (bf16[32,5120]{1,0:T(8,128)(2,1)S(1)}, bf16[32,5120]{1,0:T(8,128)(2,1)S(1)}, u32[]{:S(2)}, u32[]{:S(2)}) collective-permute-start(bf16[32,5120]{1,0:T(8,128)(2,1)S(1)} %slice.15), channel_id=1, source_target_pairs={{0,2},{2,4},{4,6},{6,0},{1,3},{3,5},{5,7},{7,1},{8,10},{10,12},{12... | collective-permute-start | bytes 983048 | tf_op jit(solution)/shard_map/ppermute | solution.py:34
  47.6 14.1 %collective-permute-start.6 = (bf16[32,5120]{1,0:T(8,128)(2,1)S(1)}, bf16[32,5120]{1,0:T(8,128)(2,1)S(1)}, u32[]{:S(2)}, u32[]{:S(2)}) collective-permute-start(bf16[32,5120]{1,0:T(8,128)(2,1)S(1)} %slice.16), channel_id=1, source_target_pairs={{0,6},{2,0},{4,2},{6,4},{1,7},{3,1},{5,3},{7,5},{8,14},{10,8},{12,... | collective-permute-start | bytes 983048 | tf_op jit(solution)/shard_map/ppermute | solution.py:34
  61.7 7.6 %copy-start.10 = (bf16[32,5120]{1,0:T(8,128)(2,1)}, bf16[32,5120]{1,0:T(8,128)(2,1)S(1)}, u32[]{:S(2)}) copy-start(bf16[32,5120]{1,0:T(8,128)(2,1)S(1)} %collective-permute-done.5.refs_3_) | copy-start | bytes 983044
  61.7 7.6 %copy-start.11 = (bf16[32,5120]{1,0:T(8,128)(2,1)}, bf16[32,5120]{1,0:T(8,128)(2,1)S(1)}, u32[]{:S(2)}) copy-start(bf16[32,5120]{1,0:T(8,128)(2,1)S(1)} %collective-permute-done.6.refs_4_) | copy-start | bytes 983044
  61.8 7.6 %copy-start.22 = (bf16[128,1536]{1,0:T(8,128)(2,1)}, bf16[128,1536]{1,0:T(8,128)(2,1)S(1)}, u32[]{:S(2)}) copy-start(bf16[128,1536]{1,0:T(8,128)(2,1)S(1)} %collective-permute-done.9.left) | copy-start | bytes 1179652
  61.8 18.2 %collective-permute-start.10 = (bf16[128,2560]{1,0:T(8,128)(2,1)S(1)}, bf16[128,2560]{1,0:T(8,128)(2,1)S(1)}, u32[]{:S(2)}, u32[]{:S(2)}) collective-permute-start(bf16[128,2560]{1,0:T(8,128)(2,1)S(1)} %get-tuple-element.67), channel_id=1, source_target_pairs={{0,8},{8,0},{1,9},{9,1},{2,10},{10,2},{3,11},{11,3},{4,12},{12,4},... | collective-permute-start | bytes 1966088 | tf_op jit(solution)/shard_map/ppermute | solution.py:421
  62.5 1.7 %collective-permute-start.11 = (bf16[32,5120]{1,0:T(8,128)(2,1)S(1)}, bf16[32,5120]{1,0:T(8,128)(2,1)S(1)}, u32[]{:S(2)}, u32[]{:S(2)}) collective-permute-start(bf16[32,5120]{1,0:T(8,128)(2,1)S(1)} %collective-permute-done.5.refs_3_), channel_id=1, source_target_pairs={{0,1},{1,0},{2,3},{3,2},{4,5},{5,4},{6,7},{7,6},{8,9},{9,8},{10,11... | collective-permute-start | bytes 983048 | tf_op jit(solution)/shard_map/ppermute | solution.py:422
  63.0 1.7 %collective-permute-start.12 = (bf16[32,5120]{1,0:T(8,128)(2,1)S(1)}, bf16[32,5120]{1,0:T(8,128)(2,1)S(1)}, u32[]{:S(2)}, u32[]{:S(2)}) collective-permute-start(bf16[32,5120]{1,0:T(8,128)(2,1)S(1)} %collective-permute-done.6.refs_4_), channel_id=1, source_target_pairs={{0,1},{1,0},{2,3},{3,2},{4,5},{5,4},{6,7},{7,6},{8,9},{9,8},{10,11... | collective-permute-start | bytes 983048 | tf_op jit(solution)/shard_map/ppermute | solution.py:422
  72.1 12.6 %all-to-all-start.2 = ((bf16[8,160,128]{2,1,0:T(8,128)(2,1)}), bf16[8,160,128]{2,1,0:T(8,128)(2,1)S(1)}, u32[]{:S(2)}, u32[]{:S(2)}) async-start(bf16[8,160,128]{2,1,0:T(8,128)(2,1)} %bitcast.5), calls=%async_computation.2 | async-start | bytes 655360 | tf_op jit(solution)/shard_map/all_to_all | solution.py:424
  84.7 19.1 %collective-permute-start.13 = (bf16[32,4096]{1,0:T(8,128)(2,1)}, bf16[32,4096]{1,0:T(8,128)(2,1)S(1)}, u32[]{:S(2)}, u32[]{:S(2)}) collective-permute-start(bf16[32,4096]{1,0:T(8,128)(2,1)} %get-tuple-element.83), channel_id=1, source_target_pairs={{0,2},{2,4},{4,6},{6,0},{1,3},{3,5},{5,7},{7,1},{8,10},{10,12},{12... | collective-permute-start | bytes 786440 | tf_op jit(solution)/shard_map/ppermute | solution.py:34
  85.9 17.9 %collective-permute-start.14 = (bf16[32,4096]{1,0:T(8,128)(2,1)}, bf16[32,4096]{1,0:T(8,128)(2,1)S(1)}, u32[]{:S(2)}, u32[]{:S(2)}) collective-permute-start(bf16[32,4096]{1,0:T(8,128)(2,1)} %get-tuple-element.84), channel_id=1, source_target_pairs={{0,4},{2,6},{4,0},{6,2},{1,5},{3,7},{5,1},{7,3},{8,12},{10,14},{12... | collective-permute-start | bytes 786440 | tf_op jit(solution)/shard_map/ppermute | solution.py:34
  88.8 15.0 %collective-permute-start.15 = (bf16[32,4096]{1,0:T(8,128)(2,1)}, bf16[32,4096]{1,0:T(8,128)(2,1)S(1)}, u32[]{:S(2)}, u32[]{:S(2)}) collective-permute-start(bf16[32,4096]{1,0:T(8,128)(2,1)} %get-tuple-element.85), channel_id=1, source_target_pairs={{0,6},{2,0},{4,2},{6,4},{1,7},{3,1},{5,3},{7,5},{8,14},{10,8},{12,... | collective-permute-start | bytes 786440 | tf_op jit(solution)/shard_map/ppermute | solution.py:34
  90.1 14.7 %all-to-all-start.3 = ((bf16[8,160,128]{2,1,0:T(8,128)(2,1)}), bf16[8,160,128]{2,1,0:T(8,128)(2,1)S(1)}, u32[]{:S(2)}, u32[]{:S(2)}) async-start(bf16[8,160,128]{2,1,0:T(8,128)(2,1)} %broadcast_in_dim.28), calls=%async_computation.3 | async-start | bytes 655360 | tf_op jit(solution)/shard_map/all_to_all | solution.py:39
  94.7 9.1 %copy-start.18 = (f32[32,4096]{1,0:T(8,128)S(1)}, f32[32,4096]{1,0:T(8,128)}, u32[]{:S(2)}) copy-start(f32[32,4096]{1,0:T(8,128)} %delta_rows.1) | copy-start | bytes 1572868
  94.7 9.1 %copy-start.21 = (f32[32,4096]{1,0:T(8,128)S(1)}, f32[32,4096]{1,0:T(8,128)}, u32[]{:S(2)}) copy-start(f32[32,4096]{1,0:T(8,128)} %get-tuple-element.81) | copy-start | bytes 1572868
  (10 other events, 44.9 us)
